TPU v7x, 512 devices: a whole 4x4x16 slice. The times are simulated.
512 devices in a mesh: dp: 8 (over z_hi, y), seq: 64 (over x, z_lo, core).
Axes of the slice: x: 4, y: 4, z: 16 (z_hi: 2, z_lo: 8; z = z_hi * 8 + z_lo), core: 2. Of those that a mesh axis runs over, the one named last changes fastest.
Arguments:
- features: bfloat16 [65536, 320], P(('dp', 'seq')), parts along dimension 0, may hold values from -40 to 40
- hint: bfloat16 [65536, 320], P(('dp', 'seq')), parts along dimension 0, may hold values from -6 to 6
- conv_weight: bfloat16 [3, 3, 320, 320], replicated, may hold values from -0.109375 to 0.109375
- conv_bias: float32 [320], replicated, may hold values from -3 to 3
- zero_weight: bfloat16 [320, 320], replicated, may hold values from -0.3125 to 0.3125
- zero_bias: float32 [320], replicated, may hold values from -2 to 2
- group_gain: float32 [320], replicated, may hold values from 0.5 to 1.5
- proj_in: bfloat16 [320, 320], replicated, may hold values from -0.3125 to 0.3125
- norm_gain: float32 [320], replicated, may hold values from 0.5 to 1.5
- query_weight: bfloat16 [320, 320], replicated, may hold values from -2 to 2
- key_weight: bfloat16 [320, 320], replicated, may hold values from -2 to 2
- value_weight: bfloat16 [320, 320], replicated, may hold values from -0.3125 to 0.3125
- attn_out: bfloat16 [320, 320], replicated, may hold values from -0.3125 to 0.3125
- proj_out: bfloat16 [320, 320], replicated, may hold values from -0.3125 to 0.3125
Outputs:
- block_out: bfloat16 [65536, 320], P(('dp', 'seq')), parts along dimension 0
There are 8 independent parts, one for each index of `dp`. A program takes and returns all parts, laid end to end along the dimension named above; an argument that names none is the same for every part. Nothing has to cross between parts.
All inputs are finite; a program needn't handle non-finite values.
Results may differ from a plain program's by a relative error of at most 0.023.
Values may be sent and summed in bfloat16 or wider, within the bound.
No kernel may reach another device: no remote copies, remote signals or barrier semaphores. Data moves between devices by JAX's collectives and lax.ppermute only.
A program may use at most 64 MiB of HBM per device.

v0:
```python
import math

import jax
import jax.numpy as jnp
from jax import lax
from jax.sharding import Mesh
from jax.sharding import PartitionSpec as P

HEADS = 8
GROUPS = 32
WIDTH = 128
SEQ = ("seq_0", "seq_1", "seq_2")
DP_SEQ = ("dp", "seq_0", "seq_1", "seq_2")


norm_eps = 1e-06
layer_eps = 1e-05


def with_halo(block, sides, width):
    for axis, dim in sides:
        count = lax.axis_size(axis)
        forward = [(i, i + 1) for i in range(count - 1)]
        backward = [(target, source) for source, target in forward]
        low = lax.ppermute(
            lax.slice_in_dim(block, block.shape[dim] - width, None, axis=dim), axis, forward
        )
        high = lax.ppermute(lax.slice_in_dim(block, 0, width, axis=dim), axis, backward)
        block = jnp.concatenate([low, block, high], axis=dim)
    return block


def from_everyone(array, axis):
    length = lax.axis_size(axis)
    return lax.all_to_all(
        jnp.broadcast_to(array[None], (length, *array.shape)), axis, 0, 0, tiled=True
    )


def taken_together(array, axis):
    everything = from_everyone(array, axis)
    return jnp.sum(everything, axis=0)


def packed_total(arrays, axis):
    ends = [0]
    for a in arrays:
        ends.append(ends[-1] + a.size)
    so_far = taken_together(jnp.concatenate([a.ravel() for a in arrays]), axis)
    return tuple((so_far[b:e].reshape(a.shape) for a, b, e in zip(arrays, ends, ends[1:])))


def sent_together(arrays, axis, split_dim, concat_dim, along):
    ends, at = ([], 0)
    for a in arrays[:-1]:
        at += a.shape[along]
        ends.append(at)
    both = jnp.concatenate(arrays, axis=along)
    return tuple(
        jnp.split(
            lax.all_to_all(both, axis, split_axis=split_dim, concat_axis=concat_dim, tiled=True),
            ends,
            axis=along,
        )
    )


def cut_along(array, dim, length):
    before, after = (array.shape[:dim], array.shape[dim + 1 :])
    return jnp.moveaxis(array.reshape(*before, length, -1, *after), dim, 0)


def laid_out(parts, dim):
    lengths = list(parts.shape[1:])
    lengths[dim] *= parts.shape[0]
    return jnp.moveaxis(parts, 0, dim).reshape(lengths)


def exchange_in_order(parts, axes, order):
    lengths = [lax.axis_size(a) for a in axes]
    parts = parts.reshape(*lengths, *parts.shape[1:])
    for k in order:
        parts = lax.all_to_all(parts, axes[k], split_axis=k, concat_axis=k, tiled=True)
    return parts.reshape(-1, *parts.shape[len(axes) :])


def exchange_by_chip(array, groups, order, split_dim, concat_dim):
    length = lax.axis_size(groups[0]) * lax.axis_size(groups[1])
    parts = cut_along(array, split_dim, length)
    return laid_out(exchange_in_order(parts, groups, order), concat_dim)


def conv_extended(extended, conv_weight, conv_bias, width):
    line_count = extended.shape[0] // width - 2
    channels = extended.shape[1]
    lattice = extended.reshape(line_count + 2, width, channels)
    padded = jnp.pad(lattice, ((0, 0), (1, 1), (0, 0)))
    summed = jnp.zeros((line_count * width, conv_weight.shape[3]), jnp.float32)
    for row_shift in range(3):
        for col_shift in range(3):
            window = padded[row_shift : row_shift + line_count, col_shift : col_shift + width]
            window = window.reshape(line_count * width, channels)
            summed = summed + jnp.dot(
                window, conv_weight[row_shift, col_shift], preferred_element_type=jnp.float32
            )
    return summed + conv_bias


def fold_blocks(carry_in, queries, pieces, make_pairs):
    row_total = pieces[0].shape[0]
    block_len = math.gcd(row_total, 1024)
    stacked = tuple(
        (member.reshape(row_total // block_len, block_len, member.shape[1]) for member in pieces)
    )
    score_scale = 1.0 / math.sqrt(queries.shape[2])

    def advance(carry_now, slab_rows):
        running_max, running_sum, weighted = carry_now
        keys_block, values_block = make_pairs(slab_rows)
        scores = (
            jnp.einsum("qhd,khd->hqk", queries, keys_block, preferred_element_type=jnp.float32)
            * score_scale
        )
        new_max = jnp.maximum(running_max, jnp.max(scores, axis=2))
        decay_by = jnp.exp(running_max - new_max)
        weights = jnp.exp(scores - new_max[:, :, None])
        running_sum = running_sum * decay_by + jnp.sum(weights, axis=2)
        weighted = weighted * jnp.transpose(decay_by)[:, :, None] + jnp.einsum(
            "hqk,khd->qhd",
            weights.astype(jnp.bfloat16),
            values_block,
            preferred_element_type=jnp.float32,
        )
        return ((new_max, running_sum, weighted), None)

    carry_out, unused = lax.scan(advance, carry_in, stacked)
    return carry_out


def local(
    features,
    hint,
    conv_weight,
    conv_bias,
    zero_weight,
    zero_bias,
    group_gain,
    proj_in,
    norm_gain,
    query_weight,
    key_weight,
    value_weight,
    attn_out,
    proj_out,
):
    tok_count, channels = features.shape
    head_dim = channels // HEADS
    extended = with_halo(hint, ((SEQ, 0),), WIDTH)
    control = jax.nn.silu(conv_extended(extended, conv_weight, conv_bias, WIDTH)).astype(
        jnp.bfloat16
    )
    branch = jnp.dot(control, zero_weight, preferred_element_type=jnp.float32) + zero_bias
    merged = (features.astype(jnp.float32) + branch).astype(jnp.bfloat16)
    widened = merged.astype(jnp.float32)
    per_group = channels // GROUPS
    entry_count = tok_count * lax.axis_size(SEQ) * per_group
    local_sum = jnp.sum(widened.reshape(tok_count, GROUPS, per_group), axis=(0, 2))
    local_square = jnp.sum(jnp.square(widened).reshape(tok_count, GROUPS, per_group), axis=(0, 2))
    group_total, square_total = packed_total((local_sum, local_square), SEQ)
    mean_group = group_total / entry_count
    var_group = square_total / entry_count - jnp.square(mean_group)
    mean_chan = jnp.repeat(mean_group, per_group)
    inv_chan = jnp.repeat(lax.rsqrt(var_group + norm_eps), per_group)
    grouped = ((widened - mean_chan) * inv_chan * group_gain).astype(jnp.bfloat16)
    inner_rows = jnp.dot(grouped, proj_in, preferred_element_type=jnp.float32).astype(jnp.bfloat16)
    inner_wide = inner_rows.astype(jnp.float32)
    centre = jnp.mean(inner_wide, axis=1, keepdims=True)
    spread = jnp.mean(jnp.square(inner_wide - centre), axis=1, keepdims=True)
    normed = ((inner_wide - centre) * lax.rsqrt(spread + layer_eps) * norm_gain).astype(
        jnp.bfloat16
    )
    queries = jnp.dot(normed, query_weight, preferred_element_type=jnp.float32).astype(jnp.bfloat16)
    queries = queries.reshape(tok_count, HEADS, head_dim)
    group_span = lax.axis_size(SEQ) // HEADS
    sub_rows = tok_count // group_span
    local_keys = jnp.dot(normed, key_weight, preferred_element_type=jnp.float32).astype(
        jnp.bfloat16
    )
    local_values = jnp.dot(normed, value_weight, preferred_element_type=jnp.float32).astype(
        jnp.bfloat16
    )
    query_send = (
        queries.reshape(group_span, sub_rows, HEADS, head_dim)
        .transpose(2, 0, 1, 3)
        .reshape(HEADS * group_span, sub_rows, head_dim)
    )

    def copies_for(matrix):
        by_head = matrix.reshape(tok_count, HEADS, head_dim).transpose(1, 0, 2)
        return jnp.broadcast_to(by_head[:, None], (HEADS, group_span, tok_count, head_dim)).reshape(
            HEADS * group_span, tok_count, head_dim
        )

    own_queries = lax.all_to_all(query_send, SEQ, split_axis=0, concat_axis=0, tiled=True)
    head_keys, head_values = sent_together(
        (copies_for(local_keys), copies_for(local_values)), SEQ, 0, 0, 1
    )
    query_rows = own_queries.shape[0] * sub_rows
    own_queries = own_queries.reshape(query_rows, 1, head_dim)
    key_rows = head_keys.reshape(-1, head_dim)
    value_rows = head_values.reshape(-1, head_dim)

    def single_pairs(slab_rows):
        return (slab_rows[0].reshape(-1, 1, head_dim), slab_rows[1].reshape(-1, 1, head_dim))

    head_carry = (
        jnp.full((1, query_rows), -1e30, jnp.float32),
        jnp.zeros((1, query_rows), jnp.float32),
        jnp.zeros((query_rows, 1, head_dim), jnp.float32),
    )
    running_max, running_sum, weighted = fold_blocks(
        head_carry, own_queries, (key_rows, value_rows), single_pairs
    )
    head_result = (weighted / jnp.transpose(running_sum)[:, :, None]).astype(jnp.bfloat16)
    head_result = head_result.reshape(lax.axis_size(SEQ), sub_rows, head_dim)
    returned = exchange_by_chip(head_result, (("seq_0", "seq_1"), "seq_2"), (1, 0), 0, 0)
    attended = (
        returned.reshape(HEADS, group_span, sub_rows, head_dim)
        .transpose(1, 2, 0, 3)
        .reshape(tok_count, channels)
    )
    after_attn = (
        inner_wide + jnp.dot(attended, attn_out, preferred_element_type=jnp.float32)
    ).astype(jnp.bfloat16)
    return (widened + jnp.dot(after_attn, proj_out, preferred_element_type=jnp.float32)).astype(
        jnp.bfloat16
    )


def solution(mesh):
    torus = Mesh(mesh.devices.reshape(mesh.shape["dp"], 4, 8, 2), ("dp", "seq_0", "seq_1", "seq_2"))
    in_specs = (
        P(DP_SEQ, None),
        P(DP_SEQ, None),
        P(),
        P(),
        P(),
        P(),
        P(),
        P(),
        P(),
        P(),
        P(),
        P(),
        P(),
        P(),
    )
    out_specs = P(DP_SEQ, None)
    return jax.shard_map(local, mesh=torus, in_specs=in_specs, out_specs=out_specs, check_vma=False)
```

profile of v0, /device:TPU:24, one launch (start us, length us, event | category | flops | bytes accessed | tf_op | source)
XLA Modules:
  0.0 237.4 jit_solution(5624541281948350875)
XLA Ops:
  0.0 2.0 collective-permute-start
  2.0 1.3 collective-permute-start.1
  3.3 3.8 %collective-permute-done.1 = bf16[128,320]{0,1:T(8,128)(2,1)S(1)} collective-permute-done((bf16[128,320]{0,1:T(8,128)(2,1)}, bf16[128,320]{0,1:T(8,128)(2,1)S(1)}, u32[]{:S(2)}, u32[]{:S(2)}) %collective-permute-start.1) | collective-permute-done | bytes 81952 | tf_op jit(solution)/shard_map/ppermute | solution.py:28
  7.1 0.9 pad_maximum_fusion.1
  8.2 1.2 fusion.39
  9.5 1.2 fusion.30
  12.3 0.9 convolution_add_fusion.4
  13.2 1.6 fusion.78
  15.4 36.2 %all_to_all.26 = f32[64,1,64]{2,1,0:T(1,128)S(1)} all-to-all(f32[64,1,64]{2,1,0:T(1,128)S(1)} %broadcast_in_dim.16), channel_id=1, replica_groups=mesh['dp'=8,'seq_0'=4,'seq_1'=8,'seq_2'=2] {'seq_0','seq_1','seq_2'}, dimensions={0} | all-to-all | bytes 32768 | tf_op jit(solution)/shard_map/all_to_all | solution.py:35
  52.2 0.5 fusion.82
  53.2 1.2 convolution_convert_fusion
  54.8 1.0 reshape.132
  55.9 4.6 %all-to-all-start.2 = ((bf16[64,2,320]{2,1,0:T(2,128)(2,1)}), bf16[64,2,320]{2,1,0:T(2,128)(2,1)S(1)}, u32[]{:S(2)}, u32[]{:S(2)}) async-start(bf16[64,2,320]{2,1,0:T(2,128)(2,1)} %reshape.132), calls=%async_computation.2 | async-start | bytes 196608 | tf_op jit(solution)/shard_map/all_to_all | solution.py:204
  61.0 1.2 pad_maximum_fusion
  62.2 11.8 %all-to-all-done.2 = bf16[64,2,320]{2,1,0:T(2,128)(2,1)S(1)} async-done(((bf16[64,2,320]{2,1,0:T(2,128)(2,1)}), bf16[64,2,320]{2,1,0:T(2,128)(2,1)S(1)}, u32[]{:S(2)}, u32[]{:S(2)}) %all-to-all-start.2) | async-done | bytes 81952 | tf_op jit(solution)/shard_map/all_to_all | solution.py:204
  74.0 5.9 %all-to-all-start.1 = ((bf16[64,256,40]{1,2,0:T(8,128)(2,1)}), bf16[64,256,40]{1,2,0:T(8,128)(2,1)S(1)}, u32[]{:S(2)}, u32[]{:S(2)}) async-start(bf16[64,256,40]{1,2,0:T(8,128)(2,1)} %pad_maximum_fusion), calls=%async_computation.1 | async-start | bytes 2621440 | tf_op jit(solution)/shard_map/all_to_all | solution.py:61
  80.3 61.2 %all-to-all-done.1 = bf16[64,256,40]{1,2,0:T(8,128)(2,1)S(1)} async-done(((bf16[64,256,40]{1,2,0:T(8,128)(2,1)}), bf16[64,256,40]{1,2,0:T(8,128)(2,1)S(1)}, u32[]{:S(2)}, u32[]{:S(2)}) %all-to-all-start.1) | async-done | bytes 1310752 | tf_op jit(solution)/shard_map/all_to_all | solution.py:61
  141.6 1.1 fusion.79
  142.6 2.0 copy.119
  144.6 1.8 copy.120
  146.4 63.1 %while.15 = (s32[]{:T(128)}, f32[1,1024]{1,0:T(1,128)S(1)}, f32[1,1024]{1,0:T(1,128)S(1)}, f32[1024,1,40]{0,2,1:T(8,128)S(1)}, bf16[8,1024,40]{2,1,0:T(8,128)(2,...) while((s32[]{:T(128)}, f32[1,1024]{1,0:T(1,128)S(1)}, ...), condition=%wide.region_10.11_spmd.clone, body=%wide.region_7.0_spmd.clone.sunk | while | flops 176288768 | bytes 30360200 | solution.py:136
  146.4 2.6 %multiply_reduce_fusion.4 = (f32[1024]{0:T(1024)S(1)}, f32[1024,1024]{1,0:T(8,128)}) fusion(bf16[1024,1,40]{0,2,1:T(8,128)(2,1)S(1)} %get-tuple-element.212, bf16[8,1024,40]{2,1,0:T(8,128)(2,1)S(1)} %get-tuple-element.211, s32[]{:T(128)} %get-tuple-element.198), kind=kOutput, calls=%fused_computation.1.clone.1 | convolution fusion | flops 85982208 | bytes 4542468 | tf_op jit(solution)/shard_map/while/body/eval_jaxpr/qhd,khd->hqk/dot_general | solution.py:121
  149.0 3.1 %fusion.107 = f32[1024]{0:T(1024)S(1)} fusion(f32[1024,1024]{1,0:T(8,128)} %get-tuple-element.186, f32[1024]{0:T(1024)S(1)} %bitcast.152), kind=kLoop, calls=%fused_computation.3.clone.1 | loop fusion | flops 3144704 | bytes 4202496 | tf_op jit(solution)/shard_map/while/body/eval_jaxpr/reduce_sum | solution.py:127
  152.5 1.8 fusion.109
  154.3 2.6 %multiply_reduce_fusion.4 = (f32[1024]{0:T(1024)S(1)}, f32[1024,1024]{1,0:T(8,128)}) fusion(bf16[1024,1,40]{0,2,1:T(8,128)(2,1)S(1)} %get-tuple-element.212, bf16[8,1024,40]{2,1,0:T(8,128)(2,1)S(1)} %get-tuple-element.211, s32[]{:T(128)} %get-tuple-element.198), kind=kOutput, calls=%fused_computation.1.clone.1 | convolution fusion | flops 85982208 | bytes 4542468 | tf_op jit(solution)/shard_map/while/body/eval_jaxpr/qhd,khd->hqk/dot_general | solution.py:121
  156.9 3.1 %fusion.107 = f32[1024]{0:T(1024)S(1)} fusion(f32[1024,1024]{1,0:T(8,128)} %get-tuple-element.186, f32[1024]{0:T(1024)S(1)} %bitcast.152), kind=kLoop, calls=%fused_computation.3.clone.1 | loop fusion | flops 3144704 | bytes 4202496 | tf_op jit(solution)/shard_map/while/body/eval_jaxpr/reduce_sum | solution.py:127
  160.3 1.8 fusion.109
  162.2 2.6 %multiply_reduce_fusion.4 = (f32[1024]{0:T(1024)S(1)}, f32[1024,1024]{1,0:T(8,128)}) fusion(bf16[1024,1,40]{0,2,1:T(8,128)(2,1)S(1)} %get-tuple-element.212, bf16[8,1024,40]{2,1,0:T(8,128)(2,1)S(1)} %get-tuple-element.211, s32[]{:T(128)} %get-tuple-element.198), kind=kOutput, calls=%fused_computation.1.clone.1 | convolution fusion | flops 85982208 | bytes 4542468 | tf_op jit(solution)/shard_map/while/body/eval_jaxpr/qhd,khd->hqk/dot_general | solution.py:121
  164.8 3.1 %fusion.107 = f32[1024]{0:T(1024)S(1)} fusion(f32[1024,1024]{1,0:T(8,128)} %get-tuple-element.186, f32[1024]{0:T(1024)S(1)} %bitcast.152), kind=kLoop, calls=%fused_computation.3.clone.1 | loop fusion | flops 3144704 | bytes 4202496 | tf_op jit(solution)/shard_map/while/body/eval_jaxpr/reduce_sum | solution.py:127
  168.2 1.8 fusion.109
  170.1 2.6 %multiply_reduce_fusion.4 = (f32[1024]{0:T(1024)S(1)}, f32[1024,1024]{1,0:T(8,128)}) fusion(bf16[1024,1,40]{0,2,1:T(8,128)(2,1)S(1)} %get-tuple-element.212, bf16[8,1024,40]{2,1,0:T(8,128)(2,1)S(1)} %get-tuple-element.211, s32[]{:T(128)} %get-tuple-element.198), kind=kOutput, calls=%fused_computation.1.clone.1 | convolution fusion | flops 85982208 | bytes 4542468 | tf_op jit(solution)/shard_map/while/body/eval_jaxpr/qhd,khd->hqk/dot_general | solution.py:121
  172.7 3.1 %fusion.107 = f32[1024]{0:T(1024)S(1)} fusion(f32[1024,1024]{1,0:T(8,128)} %get-tuple-element.186, f32[1024]{0:T(1024)S(1)} %bitcast.152), kind=kLoop, calls=%fused_computation.3.clone.1 | loop fusion | flops 3144704 | bytes 4202496 | tf_op jit(solution)/shard_map/while/body/eval_jaxpr/reduce_sum | solution.py:127
  176.1 1.8 fusion.109
  177.9 2.6 %multiply_reduce_fusion.4 = (f32[1024]{0:T(1024)S(1)}, f32[1024,1024]{1,0:T(8,128)}) fusion(bf16[1024,1,40]{0,2,1:T(8,128)(2,1)S(1)} %get-tuple-element.212, bf16[8,1024,40]{2,1,0:T(8,128)(2,1)S(1)} %get-tuple-element.211, s32[]{:T(128)} %get-tuple-element.198), kind=kOutput, calls=%fused_computation.1.clone.1 | convolution fusion | flops 85982208 | bytes 4542468 | tf_op jit(solution)/shard_map/while/body/eval_jaxpr/qhd,khd->hqk/dot_general | solution.py:121
  180.6 3.1 %fusion.107 = f32[1024]{0:T(1024)S(1)} fusion(f32[1024,1024]{1,0:T(8,128)} %get-tuple-element.186, f32[1024]{0:T(1024)S(1)} %bitcast.152), kind=kLoop, calls=%fused_computation.3.clone.1 | loop fusion | flops 3144704 | bytes 4202496 | tf_op jit(solution)/shard_map/while/body/eval_jaxpr/reduce_sum | solution.py:127
  184.0 1.8 fusion.109
  185.8 2.6 %multiply_reduce_fusion.4 = (f32[1024]{0:T(1024)S(1)}, f32[1024,1024]{1,0:T(8,128)}) fusion(bf16[1024,1,40]{0,2,1:T(8,128)(2,1)S(1)} %get-tuple-element.212, bf16[8,1024,40]{2,1,0:T(8,128)(2,1)S(1)} %get-tuple-element.211, s32[]{:T(128)} %get-tuple-element.198), kind=kOutput, calls=%fused_computation.1.clone.1 | convolution fusion | flops 85982208 | bytes 4542468 | tf_op jit(solution)/shard_map/while/body/eval_jaxpr/qhd,khd->hqk/dot_general | solution.py:121
  188.5 3.1 %fusion.107 = f32[1024]{0:T(1024)S(1)} fusion(f32[1024,1024]{1,0:T(8,128)} %get-tuple-element.186, f32[1024]{0:T(1024)S(1)} %bitcast.152), kind=kLoop, calls=%fused_computation.3.clone.1 | loop fusion | flops 3144704 | bytes 4202496 | tf_op jit(solution)/shard_map/while/body/eval_jaxpr/reduce_sum | solution.py:127
  191.9 1.8 fusion.109
  193.7 2.6 %multiply_reduce_fusion.4 = (f32[1024]{0:T(1024)S(1)}, f32[1024,1024]{1,0:T(8,128)}) fusion(bf16[1024,1,40]{0,2,1:T(8,128)(2,1)S(1)} %get-tuple-element.212, bf16[8,1024,40]{2,1,0:T(8,128)(2,1)S(1)} %get-tuple-element.211, s32[]{:T(128)} %get-tuple-element.198), kind=kOutput, calls=%fused_computation.1.clone.1 | convolution fusion | flops 85982208 | bytes 4542468 | tf_op jit(solution)/shard_map/while/body/eval_jaxpr/qhd,khd->hqk/dot_general | solution.py:121
  196.4 3.1 %fusion.107 = f32[1024]{0:T(1024)S(1)} fusion(f32[1024,1024]{1,0:T(8,128)} %get-tuple-element.186, f32[1024]{0:T(1024)S(1)} %bitcast.152), kind=kLoop, calls=%fused_computation.3.clone.1 | loop fusion | flops 3144704 | bytes 4202496 | tf_op jit(solution)/shard_map/while/body/eval_jaxpr/reduce_sum | solution.py:127
  199.8 1.8 fusion.109
  201.6 2.6 %multiply_reduce_fusion.4 = (f32[1024]{0:T(1024)S(1)}, f32[1024,1024]{1,0:T(8,128)}) fusion(bf16[1024,1,40]{0,2,1:T(8,128)(2,1)S(1)} %get-tuple-element.212, bf16[8,1024,40]{2,1,0:T(8,128)(2,1)S(1)} %get-tuple-element.211, s32[]{:T(128)} %get-tuple-element.198), kind=kOutput, calls=%fused_computation.1.clone.1 | convolution fusion | flops 85982208 | bytes 4542468 | tf_op jit(solution)/shard_map/while/body/eval_jaxpr/qhd,khd->hqk/dot_general | solution.py:121
  204.3 3.1 %fusion.107 = f32[1024]{0:T(1024)S(1)} fusion(f32[1024,1024]{1,0:T(8,128)} %get-tuple-element.186, f32[1024]{0:T(1024)S(1)} %bitcast.152), kind=kLoop, calls=%fused_computation.3.clone.1 | loop fusion | flops 3144704 | bytes 4202496 | tf_op jit(solution)/shard_map/while/body/eval_jaxpr/reduce_sum | solution.py:127
  207.7 1.8 fusion.109
  210.1 3.8 %all_to_all.27 = bf16[2,2,10240]{2,1,0:T(2,128)(2,1)S(1)} all-to-all(bf16[2,2,10240]{2,1,0:T(2,128)(2,1)S(1)} %reshape.134), channel_id=1, replica_groups=mesh['dp'=8,'seq_0'=4,'seq_1'=8,'seq_2'=2] {'seq_2'}, dimensions={0} | all-to-all | bytes 163840 | tf_op jit(solution)/shard_map/all_to_all | solution.py:83
  214.7 20.8 %all_to_all.28 = bf16[32,2,640]{2,1,0:T(2,128)(2,1)S(1)} all-to-all(bf16[32,2,640]{2,1,0:T(2,128)(2,1)S(1)} %reshape.136), channel_id=1, replica_groups=mesh['dp'=8,'seq_0'=4,'seq_1'=8,'seq_2'=2] {'seq_0','seq_1'}, dimensions={0} | all-to-all | bytes 163840 | tf_op jit(solution)/shard_map/all_to_all | solution.py:83
  236.3 1.1 fusion.28
  (113 shorter events, 9.6 us)
Async XLA Ops:
  0.0 13.2 %copy-start = (bf16[320,320]{1,0:T(8,128)(2,1)S(1)}, bf16[320,320]{1,0:T(8,128)(2,1)}, u32[]{:S(2)}) copy-start(bf16[320,320]{1,0:T(8,128)(2,1)} %param.20) | copy-start | bytes 614404
  0.0 10.7 %copy-start.2 = (bf16[3,3,320,320]{3,2,1,0:T(8,128)(2,1)S(1)}, bf16[3,3,320,320]{3,2,1,0:T(8,128)(2,1)}, u32[]{:S(2)}) copy-start(bf16[3,3,320,320]{3,2,1,0:T(8,128)(2,1)} %param.18) | copy-start | bytes 5529604
  0.0 3.3 %collective-permute-start = (bf16[128,320]{0,1:T(8,128)(2,1)}, bf16[128,320]{0,1:T(8,128)(2,1)S(1)}, u32[]{:S(2)}, u32[]{:S(2)}) collective-permute-start(bf16[128,320]{0,1:T(8,128)(2,1)} %param.17), channel_id=1, source_target_pairs={{0,1},{1,2},{2,3},{3,4},{4,5},{5,6},{6,7},{7,8},{8,9},{9,10},{10,1... | collective-permute-start | bytes 245768 | tf_op jit(solution)/shard_map/ppermute | solution.py:25
  2.0 5.1 %collective-permute-start.1 = (bf16[128,320]{0,1:T(8,128)(2,1)}, bf16[128,320]{0,1:T(8,128)(2,1)S(1)}, u32[]{:S(2)}, u32[]{:S(2)}) collective-permute-start(bf16[128,320]{0,1:T(8,128)(2,1)} %param.17), channel_id=1, source_target_pairs={{1,0},{2,1},{3,2},{4,3},{5,4},{6,5},{7,6},{8,7},{9,8},{10,9},{11,1... | collective-permute-start | bytes 245768 | tf_op jit(solution)/shard_map/ppermute | solution.py:28
  8.0 3.6 %copy-start.5 = (bf16[128,320]{0,1:T(8,128)(2,1)S(1)}, bf16[128,320]{0,1:T(8,128)(2,1)}, u32[]{:S(2)}) copy-start(bf16[128,320]{0,1:T(8,128)(2,1)} %param.17) | copy-start | bytes 245764
  11.0 2.2 copy-start.13
  11.0 2.2 copy-start.14
  11.6 40.5 %copy-start.6 = (bf16[320,320]{1,0:T(8,128)(2,1)S(1)}, bf16[320,320]{1,0:T(8,128)(2,1)}, u32[]{:S(2)}) copy-start(bf16[320,320]{1,0:T(8,128)(2,1)} %param.23) | copy-start | bytes 614404
  11.7 40.5 %copy-start.11 = (f32[320]{0:T(512)S(1)}, f32[320]{0:T(512)}, u32[]{:S(2)}) copy-start(f32[320]{0:T(512)} %param.22) | copy-start | bytes 3844
  12.0 40.8 %copy-start.12 = (f32[320]{0:T(512)S(1)}, f32[320]{0:T(512)}, u32[]{:S(2)}) copy-start(f32[320]{0:T(512)} %param.24) | copy-start | bytes 3844
  12.0 40.9 %copy-start.7 = (bf16[320,320]{1,0:T(8,128)(2,1)S(1)}, bf16[320,320]{1,0:T(8,128)(2,1)}, u32[]{:S(2)}) copy-start(bf16[320,320]{1,0:T(8,128)(2,1)} %param.26) | copy-start | bytes 614404
  14.9 37.9 %copy-start.3 = (f32[128,320]{0,1:T(8,128)}, f32[128,320]{0,1:T(8,128)S(1)}, u32[]{:S(2)}) copy-start(f32[128,320]{0,1:T(8,128)S(1)} %get-tuple-element.135) | copy-start | bytes 491524
  14.9 45.6 %copy-start.8 = (bf16[320,320]{1,0:T(8,128)(2,1)S(1)}, bf16[320,320]{1,0:T(8,128)(2,1)}, u32[]{:S(2)}) copy-start(bf16[320,320]{1,0:T(8,128)(2,1)} %param.27) | copy-start | bytes 614404
  55.9 18.1 %all-to-all-start.2 = ((bf16[64,2,320]{2,1,0:T(2,128)(2,1)}), bf16[64,2,320]{2,1,0:T(2,128)(2,1)S(1)}, u32[]{:S(2)}, u32[]{:S(2)}) async-start(bf16[64,2,320]{2,1,0:T(2,128)(2,1)} %reshape.132), calls=%async_computation.2 | async-start | bytes 196608 | tf_op jit(solution)/shard_map/all_to_all | solution.py:204
  74.0 67.6 %all-to-all-start.1 = ((bf16[64,256,40]{1,2,0:T(8,128)(2,1)}), bf16[64,256,40]{1,2,0:T(8,128)(2,1)S(1)}, u32[]{:S(2)}, u32[]{:S(2)}) async-start(bf16[64,256,40]{1,2,0:T(8,128)(2,1)} %pad_maximum_fusion), calls=%async_computation.1 | async-start | bytes 2621440 | tf_op jit(solution)/shard_map/all_to_all | solution.py:61
  149.0 3.4 %copy-start.1 = (f32[1024,1024]{1,0:T(8,128)S(1)}, f32[1024,1024]{1,0:T(8,128)}, u32[]{:S(2)}) copy-start(f32[1024,1024]{1,0:T(8,128)} %get-tuple-element.186) | copy-start | bytes 12582916 | tf_op jit(solution)/shard_map/while
  156.9 3.4 %copy-start.1 = (f32[1024,1024]{1,0:T(8,128)S(1)}, f32[1024,1024]{1,0:T(8,128)}, u32[]{:S(2)}) copy-start(f32[1024,1024]{1,0:T(8,128)} %get-tuple-element.186) | copy-start | bytes 12582916 | tf_op jit(solution)/shard_map/while
  164.8 3.4 %copy-start.1 = (f32[1024,1024]{1,0:T(8,128)S(1)}, f32[1024,1024]{1,0:T(8,128)}, u32[]{:S(2)}) copy-start(f32[1024,1024]{1,0:T(8,128)} %get-tuple-element.186) | copy-start | bytes 12582916 | tf_op jit(solution)/shard_map/while
  172.7 3.4 %copy-start.1 = (f32[1024,1024]{1,0:T(8,128)S(1)}, f32[1024,1024]{1,0:T(8,128)}, u32[]{:S(2)}) copy-start(f32[1024,1024]{1,0:T(8,128)} %get-tuple-element.186) | copy-start | bytes 12582916 | tf_op jit(solution)/shard_map/while
  180.6 3.4 %copy-start.1 = (f32[1024,1024]{1,0:T(8,128)S(1)}, f32[1024,1024]{1,0:T(8,128)}, u32[]{:S(2)}) copy-start(f32[1024,1024]{1,0:T(8,128)} %get-tuple-element.186) | copy-start | bytes 12582916 | tf_op jit(solution)/shard_map/while
  188.5 3.4 %copy-start.1 = (f32[1024,1024]{1,0:T(8,128)S(1)}, f32[1024,1024]{1,0:T(8,128)}, u32[]{:S(2)}) copy-start(f32[1024,1024]{1,0:T(8,128)} %get-tuple-element.186) | copy-start | bytes 12582916 | tf_op jit(solution)/shard_map/while
  196.4 3.4 %copy-start.1 = (f32[1024,1024]{1,0:T(8,128)S(1)}, f32[1024,1024]{1,0:T(8,128)}, u32[]{:S(2)}) copy-start(f32[1024,1024]{1,0:T(8,128)} %get-tuple-element.186) | copy-start | bytes 12582916 | tf_op jit(solution)/shard_map/while
  204.2 3.4 %copy-start.1 = (f32[1024,1024]{1,0:T(8,128)S(1)}, f32[1024,1024]{1,0:T(8,128)}, u32[]{:S(2)}) copy-start(f32[1024,1024]{1,0:T(8,128)} %get-tuple-element.186) | copy-start | bytes 12582916 | tf_op jit(solution)/shard_map/while
  209.5 26.8 %copy-start.4 = (f32[128,320]{0,1:T(8,128)S(1)}, f32[128,320]{0,1:T(8,128)}, u32[]{:S(2)}) copy-start(f32[128,320]{0,1:T(8,128)} %copy-done.3) | copy-start | bytes 491524
  209.5 26.8 %copy-start.9 = (bf16[320,320]{1,0:T(8,128)(2,1)S(1)}, bf16[320,320]{1,0:T(8,128)(2,1)}, u32[]{:S(2)}) copy-start(bf16[320,320]{1,0:T(8,128)(2,1)} %param.29) | copy-start | bytes 614404
  209.5 26.8 %copy-start.10 = (bf16[320,320]{1,0:T(8,128)(2,1)S(1)}, bf16[320,320]{1,0:T(8,128)(2,1)}, u32[]{:S(2)}) copy-start(bf16[320,320]{1,0:T(8,128)(2,1)} %param.28) | copy-start | bytes 614404
where the time goes:
time: 238 us; the launch traced here: 237 us
  waiting for transfers between devices  76.8 us (32%)
  blocking collectives  60.8 us (26%)
  matrix products  45.1 us (19%)
  other arithmetic  27.6 us (12%)
  starting transfers between devices  13.8 us (6%)
  local copies, waits for them, and re-layouts  12.5 us (5%)
    all_to_all x1, waiting for transfers between devices, sent_together(): lax.all_to_all(both, axis, split_axis=split_dim, concat_axis=concat_dim,...  61.2 us
    all_to_all x1, blocking collectives, from_everyone(): lax.all_to_all(jnp.broadcast_to(array[None], (length, *array.shape)), axi...  36.2 us
    reduce_sum x8, other arithmetic, advance(): running_sum = running_sum * decay_by + jnp.sum(weights, axis=2)  24.6 us
    all_to_all x2, blocking collectives, exchange_in_order(): lax.all_to_all(parts, axes[k], split_axis=k, concat_axis=k, tiled=True)  24.6 us
    dot_general x8, matrix products, advance(): jnp.einsum('qhd,khd->hqk', queries, keys_block, preferred_element_type=jn...  21 us
    dot_general x8, matrix products, advance(): jnp.einsum('hqk,khd->qhd', weights.astype(jnp.bfloat16), values_block, pr...  14.3 us
    all_to_all x1, waiting for transfers between devices, local(): lax.all_to_all(query_send, SEQ, split_axis=0, concat_axis=0, tiled=True)  11.8 us
    unnamed x38, local copies, waits for them, and re-layouts  6.76 us
  transfers between devices with their start and end apart: 4, of which 3 were waited for; matrix products, arithmetic and copies ran while one was open for 1% of the time, Pallas kernels for 0%

commit v1 on v0

v1 whole, which is shorter than its diff:
```python
import functools
import math

import jax
import jax.numpy as jnp
from jax import lax
from jax.experimental import pallas as pl
from jax.experimental.pallas import tpu as pltpu
from jax.sharding import Mesh
from jax.sharding import PartitionSpec as P

HEADS = 8
GROUPS = 32
WIDTH = 128
SEQ = ("x", "z", "c")
DP_SEQ = ("dp", "x", "z", "c")
NORM_EPS = 1e-06
LAYER_EPS = 1e-05
HIGHEST = lax.Precision.HIGHEST
F32 = jnp.float32
BF16 = jnp.bfloat16
VMEM = pl.BlockSpec(memory_space=pltpu.VMEM)
MIB = 1024 * 1024


def dot(a, b):
    return jnp.dot(a, b, preferred_element_type=F32)


def exact_dot(a, b):
    return jnp.dot(a, b, precision=HIGHEST, preferred_element_type=F32)


def call(body, out_shape, args, scratch=(), limit=24, flops=0, read=0, trans=0):
    many = isinstance(out_shape, (list, tuple))
    return pl.pallas_call(
        body,
        out_shape=out_shape,
        in_specs=[VMEM] * len(args),
        out_specs=[VMEM] * len(out_shape) if many else VMEM,
        scratch_shapes=scratch,
        compiler_params=pltpu.CompilerParams(vmem_limit_bytes=limit * MIB),
        cost_estimate=pl.CostEstimate(flops=flops, bytes_accessed=read, transcendentals=trans),
    )(*args)


def group_spread(channels, lanes, first):
    per_group = channels // GROUPS
    lane = lax.broadcasted_iota(jnp.int32, (lanes, channels), 0)
    chan = lax.broadcasted_iota(jnp.int32, (lanes, channels), 1)
    low = (lane - first) * per_group
    inside = (chan >= low) & (chan < low + per_group) & (lane >= first) & (lane < first + GROUPS)
    return inside.astype(F32)


def group_gather(channels, lanes, first):
    per_group = channels // GROUPS
    lane = lax.broadcasted_iota(jnp.int32, (channels, lanes), 1)
    chan = lax.broadcasted_iota(jnp.int32, (channels, lanes), 0)
    low = (lane - first) * per_group
    inside = (chan >= low) & (chan < low + per_group) & (lane >= first) & (lane < first + GROUPS)
    return inside.astype(F32)


def taps(row, weight, index):
    tokens, channels = row.shape
    wide = row.astype(F32)
    at = lax.broadcasted_iota(jnp.int32, (tokens, channels), 0)
    left = jnp.where(at == 0, 0.0, pltpu.roll(wide, 1, 0)).astype(BF16)
    right = jnp.where(at == tokens - 1, 0.0, pltpu.roll(wide, tokens - 1, 0)).astype(BF16)
    total = dot(left, weight[index, 0])
    total += dot(row, weight[index, 1])
    return total + dot(right, weight[index, 2])


def own_row_body(hint, weight, bias, out):
    out[...] = taps(hint[...], weight, 0) + bias[...]


def merge_body(partial, above, below, weight_up, weight_down, zero_weight, zero_bias, features, merged_out, stats_out):
    conv = partial[...] + taps(above[...], weight_up, 0) + taps(below[...], weight_down, 0)
    control = (conv / (1.0 + jnp.exp(-conv))).astype(BF16)
    branch = dot(control, zero_weight[...]) + zero_bias[...]
    merged = (features[...].astype(F32) + branch).astype(BF16)
    merged_out[...] = merged
    wide = merged.astype(F32)
    tokens, channels = wide.shape
    lanes = stats_out.shape[1]
    entries = tokens * (channels // GROUPS)
    mean = exact_dot(jnp.sum(wide, axis=0, keepdims=True), group_gather(channels, lanes, 0)) / entries
    centred = wide - exact_dot(mean, group_spread(channels, lanes, 0))
    square = exact_dot(
        jnp.sum(centred * centred, axis=0, keepdims=True), group_gather(channels, lanes, GROUPS)
    )
    stats_out[...] = jnp.broadcast_to(mean + square / entries, stats_out.shape)


def project_body(stats, merged, group_gain, proj_in, norm_gain, wq, wk, wv, inner_out, send):
    channels = merged.shape[1]
    lanes = stats.shape[1]
    head_dim = channels // HEADS
    everyone = stats[...]
    average = jnp.mean(everyone, axis=0, keepdims=True)
    between = jnp.mean(jnp.square(everyone - average), axis=0, keepdims=True)
    spread = group_spread(channels, lanes, 0)
    mean = exact_dot(average, spread)
    variance = exact_dot(average, group_spread(channels, lanes, GROUPS)) + exact_dot(between, spread)
    factor = lax.rsqrt(variance + NORM_EPS)
    grouped = ((merged[...].astype(F32) - mean) * factor * group_gain[...]).astype(BF16)
    inner = dot(grouped, proj_in[...]).astype(BF16)
    inner_out[...] = inner
    wide = inner.astype(F32)
    centred = wide - jnp.mean(wide, axis=1, keepdims=True)
    variance = jnp.mean(centred * centred, axis=1, keepdims=True)
    normed = (centred * lax.rsqrt(variance + LAYER_EPS) * norm_gain[...]).astype(BF16)
    scale = math.log2(math.e) / math.sqrt(head_dim)
    queries = (dot(normed, wq[...]) * scale).T
    keys = dot(normed, wk[...]).T
    values = dot(normed, wv[...]).T
    gap = jnp.zeros((send.shape[1] - 3 * head_dim, queries.shape[1]), F32)
    for h in range(HEADS):
        rows = slice(h * head_dim, (h + 1) * head_dim)
        block = jnp.concatenate([queries[rows], gap, keys[rows], values[rows]], axis=0)
        send[h] = block.astype(BF16)


def attend_body(head_dim, q_rows, first, last, *refs):
    received, refs = refs[0], refs[1:]
    if not first:
        acc_in, max_in, refs = refs[0], refs[1], refs[2:]
    outs = 1 if last else 2
    pieces, outs = refs[: len(refs) - outs], refs[len(refs) - outs :]
    blocks, _, tokens = received.shape
    depth = received.shape[1] - pieces[0].shape[1]
    per_step = q_rows // tokens

    def step(i, carry):
        rows = pl.ds(pl.multiple_of(i * q_rows, q_rows), q_rows)
        queries = jnp.concatenate(
            [received[i * per_step + j, :depth, :].astype(F32).T for j in range(per_step)], axis=0
        ).astype(BF16)
        if first:
            acc = top = None
        else:
            acc, top = acc_in[rows, :], max_in[rows, :1]
        for piece in pieces:
            pair = jnp.concatenate([piece[b] for b in range(piece.shape[0])], axis=1)
            scores = dot(queries, pair[:depth])
            high = jnp.max(scores, axis=1, keepdims=True)
            new_top = high if top is None else jnp.maximum(top, high)
            probs = jnp.exp2(scores - new_top).astype(BF16)
            ones = jnp.ones((128 - pair.shape[0], pair.shape[1]), BF16)
            product = lax.dot_general(
                probs,
                jnp.concatenate([pair, ones], axis=0),
                (((1,), (1,)), ((), ())),
                preferred_element_type=F32,
            )
            acc = product if acc is None else acc * jnp.exp2(top - new_top) + product
            top = new_top
        if last:
            total = acc.T
            result = total[head_dim : 2 * head_dim] / total[2 * head_dim : 2 * head_dim + 1]
            for j in range(per_step):
                outs[0][i * per_step + j] = result[:, j * tokens : (j + 1) * tokens].astype(BF16)
        else:
            outs[0][rows, :] = acc
            outs[1][rows, :] = jnp.broadcast_to(top, (q_rows, 128))
        return carry

    lax.fori_loop(0, blocks // per_step, step, 0)


def attend(received, pieces, state, last, head_dim, q_rows=512):
    blocks, _, tokens = received.shape
    args = [received, *(state or ()), *pieces]
    rows = blocks * tokens
    if last:
        out_shape = jax.ShapeDtypeStruct((blocks, head_dim, tokens), BF16)
    else:
        out_shape = [jax.ShapeDtypeStruct((rows, 128), F32)] * 2
    keys = sum(p.shape[0] * p.shape[2] for p in pieces)
    return call(
        functools.partial(attend_body, head_dim, q_rows, state is None, last),
        out_shape,
        args,
        limit=48,
        flops=2 * rows * keys * 512,
        read=keys * 160,
        trans=rows * keys,
    )


def finish_body(attended, inner, merged, attn_out, proj_out, out):
    rows = attended[...].astype(F32).T.astype(BF16)
    after = (inner[...].astype(F32) + dot(rows, attn_out[...])).astype(BF16)
    out[...] = (merged[...].astype(F32) + dot(after, proj_out[...])).astype(BF16)


def local(
    features,
    hint,
    conv_weight,
    conv_bias,
    zero_weight,
    zero_bias,
    group_gain,
    proj_in,
    norm_gain,
    query_weight,
    key_weight,
    value_weight,
    attn_out,
    proj_out,
):
    tokens, channels = features.shape
    head_dim = channels // HEADS
    everyone = lax.axis_size(SEQ)
    shape = jax.ShapeDtypeStruct
    onward = [(i, i + 1) for i in range(everyone - 1)]
    above = lax.ppermute(hint, SEQ, onward)
    below = lax.ppermute(hint, SEQ, [(b, a) for a, b in onward])
    row = lambda v: v.reshape(1, channels)
    partial = call(
        own_row_body,
        shape((tokens, channels), F32),
        (hint, conv_weight[1:2], row(conv_bias)),
        flops=2 * tokens * channels * channels * 3,
        read=3 * channels * channels * 2,
    )
    merged, stats = call(
        merge_body,
        [shape((tokens, channels), BF16), shape((everyone, 128), F32)],
        (partial, above, below, conv_weight[:1], conv_weight[2:], zero_weight, row(zero_bias), features),
        flops=2 * tokens * channels * channels * 7,
        read=7 * channels * channels * 2,
    )
    stats = lax.all_to_all(stats, SEQ, 0, 0, tiled=True)
    inner, send = call(
        project_body,
        [shape((tokens, channels), BF16), shape((HEADS, 128, tokens), BF16)],
        (stats, merged, row(group_gain), proj_in, row(norm_gain), query_weight, key_weight, value_weight),
        flops=2 * tokens * channels * channels * 4,
        read=4 * channels * channels * 2,
    )
    received = lax.all_to_all(send, "z", 0, 0, tiled=True)
    pair = received[:, 128 - 2 * head_dim :, :]
    by_core = lax.all_gather(pair, "c")
    by_chip = lax.all_gather(by_core, "x")
    pieces = [by_chip[i, j] for i in range(by_chip.shape[0]) for j in range(by_chip.shape[1])]
    result = attend(received, pieces, None, True, head_dim)
    attended = lax.all_to_all(result, "z", 0, 0, tiled=True).reshape(channels, tokens)
    return call(
        finish_body,
        shape((tokens, channels), BF16),
        (attended, inner, merged, attn_out, proj_out),
        flops=2 * tokens * channels * channels * 2,
        read=2 * channels * channels * 2,
    )


def solution(mesh):
    torus = Mesh(mesh.devices.reshape(mesh.shape["dp"], 4, 8, 2), DP_SEQ)
    return jax.shard_map(
        local,
        mesh=torus,
        in_specs=(P(DP_SEQ, None), P(DP_SEQ, None)) + (P(),) * 12,
        out_specs=P(DP_SEQ, None),
        check_vma=False,
    )
```

time: 238 us -> 148 us (0.62)
  matrix products: 45.1 us -> 0 us
  waiting for transfers between devices: 76.8 us -> 39.9 us
  other arithmetic: 27.6 us -> 0 us
  blocking collectives: 60.8 us -> 42.3 us
  Pallas kernels: 0 us -> 15.4 us
  starting transfers between devices: 13.8 us -> 28.7 us
  between operations: 0.51 us -> 13.6 us
  local copies, waits for them, and re-layouts: 12.5 us -> 7.15 us
    all_to_all x2 -> x1, waiting for transfers between devices: 73 us -> 12.3 us  [local(): stats = lax.all_to_all(stats, SEQ, 0, 0, tiled=True)]
    dot_general x30 -> x0, matrix products: 45.1 us -> none  [the longest x8 21 us: advance(): jnp.einsum('qhd,khd->hqk', queries, keys_block, preferred_element_type=jn...]
    all_gather x0 -> x1, waiting for transfers between devices: none -> 27.6 us  [local(): by_chip = lax.all_gather(by_core, 'x')]
    reduce_sum x12 -> x0, other arithmetic: 24.9 us -> none  [the longest x8 24.6 us: advance(): running_sum = running_sum * decay_by + jnp.sum(weights, axis=2)]
    all_to_all x3 -> x2, blocking collectives: 60.8 us -> 40.2 us  [the longest x1 20.8 us: local(): lax.all_to_all(result, 'z', 0, 0, tiled=True).reshape(channels, tokens)]
    pallas_call x0 -> x5, Pallas kernels: none -> 15.4 us  [call(): pl.pallas_call(body, out_shape=out_shape, in_specs=[VMEM] * len(args), ou...]
    all_to_all x2 -> x1, starting transfers between devices: 10.5 us -> 23.5 us  [local(): stats = lax.all_to_all(stats, SEQ, 0, 0, tiled=True)]
    ppermute x2, waiting for transfers between devices: 3.78 us -> 0.01 us  [the longest x1 0.01 us: local(): above = lax.ppermute(hint, SEQ, onward)]
  transfers between devices with their start and end apart: 4 -> 4, of which waited for: 3 -> 2; matrix products, arithmetic and copies ran while one was open for 1% -> 2% of each run, Pallas kernels for 0% -> 0%
where the time goes in v1:
time: 148 us; the launch traced here: 147 us
  blocking collectives  42.3 us (29%)
  waiting for transfers between devices  39.9 us (27%)
  starting transfers between devices  28.7 us (19%)
  Pallas kernels  15.4 us (10%)
  between operations  13.6 us (9%)
  local copies, waits for them, and re-layouts  7.15 us (5%)
    all_gather x1, waiting for transfers between devices, local(): by_chip = lax.all_gather(by_core, 'x')  27.6 us
    all_to_all x1, starting transfers between devices, local(): stats = lax.all_to_all(stats, SEQ, 0, 0, tiled=True)  23.5 us
    all_to_all x1, blocking collectives, local(): lax.all_to_all(result, 'z', 0, 0, tiled=True).reshape(channels, tokens)  20.8 us
    all_to_all x1, blocking collectives, local(): received = lax.all_to_all(send, 'z', 0, 0, tiled=True)  19.3 us
    pallas_call x5, Pallas kernels, call(): pl.pallas_call(body, out_shape=out_shape, in_specs=[VMEM] * len(args), ou...  15.4 us
    all_to_all x1, waiting for transfers between devices, local(): stats = lax.all_to_all(stats, SEQ, 0, 0, tiled=True)  12.3 us
    ppermute x1, starting transfers between devices, local(): above = lax.ppermute(hint, SEQ, onward)  3.68 us
    unnamed x24, local copies, waits for them, and re-layouts  3.12 us
  transfers between devices with their start and end apart: 4, of which 2 were waited for; matrix products, arithmetic and copies ran while one was open for 2% of the time, Pallas kernels for 0%

profile of v1, /device:TPU:24, one launch (start us, length us, event | category | flops | bytes accessed | tf_op | source)
XLA Modules:
  0.0 147.1 jit_solution(9733044771666020065)
XLA Ops:
  6.5 1.0 copy.20.hint
  7.5 0.0 copy-start.7
  7.6 0.0 copy-start.8
  7.6 1.4 collective-permute-start.1
  9.0 3.7 %collective-permute-start = (bf16[128,320]{1,0:T(8,128)(2,1)S(1)}, bf16[128,320]{1,0:T(8,128)(2,1)}, u32[]{:S(2)}, u32[]{:S(2)}) collective-permute-start(bf16[128,320]{1,0:T(8,128)(2,1)S(1)} %copy.20.hint), channel_id=1, source_target_pairs={{0,1},{1,2},{2,3},{3,4},{4,5},{5,6},{6,7},{7,8},{8,9},{9,10},{10,1... | collective-permute-start | bytes 245768 | tf_op jit(solution)/shard_map/ppermute | solution.py:221
  12.7 1.8 %fusion = (bf16[1,3,320,320]{3,2,1,0:T(8,128)(2,1)S(1)}, bf16[1,3,320,320]{3,2,1,0:T(8,128)(2,1)S(1)}, bf16[1,3,320,320]{3,2,1,0:T(8,128)(2,1)S(1)}) fusion(bf16[3,3,320,320]{3,2,1,0:T(8,128)(2,1)} %param.16), kind=kLoop, calls=%fused_computation.8 | loop fusion | bytes 3686400 | tf_op jit(solution)/shard_map/slice | solution.py:234
  14.5 0.0 copy-done.7
  14.5 0.0 copy-start.9
  14.5 0.0 copy-start.10
  14.5 0.0 copy-start
  14.5 0.0 copy-start.1
  14.5 0.0 copy-start.2
  14.5 0.0 copy-start.3
  14.6 0.0 copy-done.8
  14.6 1.1 copy.23.features
  15.7 0.3 shard_map.136.partial
  16.0 0.0 collective-permute-done.1.below
  16.1 0.0 collective-permute-done.above
  16.1 0.0 copy-start.4
  16.1 0.9 copy-done.4
  17.0 2.9 %shard_map.137 = (bf16[128,320]{1,0:T(8,128)(2,1)S(1)}, f32[64,128]{1,0:T(8,128)}) custom-call(f32[128,320]{1,0:T(8,128)S(1)} %shard_map.136.partial, bf16[128,320]{1,0:T(8,128)(2,1)} %collective-permute-done.above, bf16[128,320]{1,0:T(8,128)(2,1)S(1)} %collective-permute-done.1.below, bf16[1,3,320,320]{3,2,1,0:T(8,128)(2,1)S(1)} %get-tuple-element.15.weight_up, ...), custom_call_target="tpu_custom_call" | custom-call | flops 183500800 | bytes 1433600 | tf_op jit(solution)/shard_map/pallas_call | solution.py:36
  19.9 23.5 %all-to-all-start = ((f32[64,1,128]{2,1,0:T(1,128)}), f32[64,1,128]{2,1,0:T(1,128)S(1)}, u32[]{:S(2)}, u32[]{:S(2)}) async-start(f32[64,1,128]{2,1,0:T(1,128)} %bitcast.1), calls=%async_computation | async-start | bytes 65536 | tf_op jit(solution)/shard_map/all_to_all | solution.py:238
  43.4 0.0 all-gather.4.cloned.1.call-start
  43.5 0.0 copy-done.9
  43.5 0.0 copy-done.10
  43.5 12.3 %all-to-all-done = f32[64,1,128]{2,1,0:T(1,128)S(1)} async-done(((f32[64,1,128]{2,1,0:T(1,128)}), f32[64,1,128]{2,1,0:T(1,128)S(1)}, u32[]{:S(2)}, u32[]{:S(2)}) %all-to-all-start) | async-done | bytes 32800 | tf_op jit(solution)/shard_map/all_to_all | solution.py:238
  55.8 0.0 copy-done
  55.8 0.0 copy-done.1
  55.8 0.0 copy-done.2
  55.8 0.0 copy-done.3
  55.8 1.0 shard_map.138
  56.8 19.3 %all_to_all.21.refs_0_ = bf16[8,128,128]{2,1,0:T(8,128)(2,1)S(1)} all-to-all(bf16[8,128,128]{2,1,0:T(8,128)(2,1)S(1)} %get-tuple-element.11), channel_id=1, replica_groups=mesh['dp'=8,'x'=4,'z'=8,'c'=2] {'z'}, dimensions={0} | all-to-all | bytes 524288 | tf_op jit(solution)/shard_map/all_to_all | solution.py:246
  76.2 2.2 %all-gather = bf16[16,80,128]{2,1,0:T(8,128)(2,1)} all-gather(bf16[8,80,128]{2,1,0:T(8,128)(2,1)S(1)} %slice.48), channel_id=2, replica_groups=mesh['dp'=8,'x'=4,'z'=8,'c'=2] {'c'}, dimensions={0}, use_global_device_ids=true | all-gather | bytes 491520 | tf_op jit(solution)/shard_map/all_gather | solution.py:248
  78.3 0.0 all-gather.4.cloned.1.call-update
  78.4 27.6 %all-gather.4.cloned.1.call-done = bf16[8,8,80,128]{3,2,1,0:T(8,128)(2,1)} async-done(((bf16[2,8,80,128]{3,2,1,0:T(8,128)(2,1)}), bf16[8,8,80,128]{3,2,1,0:T(8,128)(2,1)}) %all-gather.4.cloned.1.call-update) | async-done | bytes 1310736 | tf_op jit(solution)/shard_map/all_gather | solution.py:249
  106.0 1.5 %slice_bitcast_fusion = (bf16[8,80,128]{2,1,0:T(8,128)(2,1)S(1)}, bf16[8,80,128]{2,1,0:T(8,128)(2,1)S(1)}, bf16[8,80,128]{2,1,0:T(8,128)(2,1)S(1)}, bf16[8,80,12...) fusion(bf16[4,2,8,80,128]{4,3,2,1,0:T(8,128)(2,1)} %bitcast.25), kind=kLoop, calls=%fused_computation | loop fusion | bytes 2621440 | tf_op jit(solution)/shard_map/squeeze | solution.py:250
  107.5 0.0 copy-start.5
  107.5 0.0 copy-start.6
  107.5 10.8 %shard_map.139 = bf16[8,40,128]{2,1,0:T(8,128)(2,1)S(1)} custom-call(bf16[8,128,128]{2,1,0:T(8,128)(2,1)S(1)} %all_to_all.21.refs_0_, bf16[8,80,128]{2,1,0:T(8,128)(2,1)S(1)} %get-tuple-element.23.refs_1_, bf16[8,80,128]{2,1,0:T(8,128)(2,1)S(1)} %get-tuple-element.22.refs_2_, bf16[8,80,128]{2,1,0:T(8,128)(2,1)S(1)} %get-tuple-element.21.refs_3_, ...), custom_call_target="tpu_custom_call" | custom-call | flops 8589934592 | bytes 1310720 | tf_op jit(solution)/shard_map/pallas_call | solution.py:36
  118.3 20.8 %all_to_all.22 = bf16[8,40,128]{2,1,0:T(8,128)(2,1)S(1)} all-to-all(bf16[8,40,128]{2,1,0:T(8,128)(2,1)S(1)} %shard_map.139), channel_id=1, replica_groups=mesh['dp'=8,'x'=4,'z'=8,'c'=2] {'z'}, dimensions={0} | all-to-all | bytes 163840 | tf_op jit(solution)/shard_map/all_to_all | solution.py:252
  139.1 0.0 copy-done.5
  139.1 0.0 copy-done.6
  139.1 0.4 shard_map.140
  139.5 0.7 copy.25
  (5 shorter events, 0.0 us)
Async XLA Ops:
  7.5 6.9 %copy-start.7 = (f32[320]{0:T(512)S(1)}, f32[320]{0:T(512)}, u32[]{:S(2)}) copy-start(f32[320]{0:T(512)} %param.17) | copy-start | bytes 3844
  7.6 7.0 %copy-start.8 = (f32[320]{0:T(512)S(1)}, f32[320]{0:T(512)}, u32[]{:S(2)}) copy-start(f32[320]{0:T(512)} %param.19) | copy-start | bytes 3844
  7.6 8.5 %collective-permute-start.1 = (bf16[128,320]{1,0:T(8,128)(2,1)S(1)}, bf16[128,320]{1,0:T(8,128)(2,1)S(1)}, u32[]{:S(2)}, u32[]{:S(2)}) collective-permute-start(bf16[128,320]{1,0:T(8,128)(2,1)S(1)} %copy.20.hint), channel_id=1, source_target_pairs={{1,0},{2,1},{3,2},{4,3},{5,4},{6,5},{7,6},{8,7},{9,8},{10,9},{11,1... | collective-permute-start | bytes 245768 | tf_op jit(solution)/shard_map/ppermute | solution.py:222
  9.0 7.1 %collective-permute-start = (bf16[128,320]{1,0:T(8,128)(2,1)S(1)}, bf16[128,320]{1,0:T(8,128)(2,1)}, u32[]{:S(2)}, u32[]{:S(2)}) collective-permute-start(bf16[128,320]{1,0:T(8,128)(2,1)S(1)} %copy.20.hint), channel_id=1, source_target_pairs={{0,1},{1,2},{2,3},{3,4},{4,5},{5,6},{6,7},{7,8},{8,9},{9,10},{10,1... | collective-permute-start | bytes 245768 | tf_op jit(solution)/shard_map/ppermute | solution.py:221
  14.5 29.0 %copy-start.9 = (f32[320]{0:T(512)S(1)}, f32[320]{0:T(512)}, u32[]{:S(2)}) copy-start(f32[320]{0:T(512)} %param.20) | copy-start | bytes 3844
  14.5 29.0 %copy-start.10 = (f32[320]{0:T(512)S(1)}, f32[320]{0:T(512)}, u32[]{:S(2)}) copy-start(f32[320]{0:T(512)} %param.22) | copy-start | bytes 3844
  14.5 41.3 %copy-start = (bf16[320,320]{1,0:T(8,128)(2,1)S(1)}, bf16[320,320]{1,0:T(8,128)(2,1)}, u32[]{:S(2)}) copy-start(bf16[320,320]{1,0:T(8,128)(2,1)} %proj_in.1) | copy-start | bytes 614404
  14.5 41.3 %copy-start.1 = (bf16[320,320]{1,0:T(8,128)(2,1)S(1)}, bf16[320,320]{1,0:T(8,128)(2,1)}, u32[]{:S(2)}) copy-start(bf16[320,320]{1,0:T(8,128)(2,1)} %wq.1) | copy-start | bytes 614404
  14.5 41.3 %copy-start.2 = (bf16[320,320]{1,0:T(8,128)(2,1)S(1)}, bf16[320,320]{1,0:T(8,128)(2,1)}, u32[]{:S(2)}) copy-start(bf16[320,320]{1,0:T(8,128)(2,1)} %wk.1) | copy-start | bytes 614404
  14.5 41.3 %copy-start.3 = (bf16[320,320]{1,0:T(8,128)(2,1)S(1)}, bf16[320,320]{1,0:T(8,128)(2,1)}, u32[]{:S(2)}) copy-start(bf16[320,320]{1,0:T(8,128)(2,1)} %wv.1) | copy-start | bytes 614404
  16.1 0.9 copy-start.4
  19.9 35.9 %all-to-all-start = ((f32[64,1,128]{2,1,0:T(1,128)}), f32[64,1,128]{2,1,0:T(1,128)S(1)}, u32[]{:S(2)}, u32[]{:S(2)}) async-start(f32[64,1,128]{2,1,0:T(1,128)} %bitcast.1), calls=%async_computation | async-start | bytes 65536 | tf_op jit(solution)/shard_map/all_to_all | solution.py:238
  43.4 62.6 %all-gather.4.cloned.1.call-start = ((), (), s32[]{:S(2)}) async-start(), calls=%async_computation.3 | async-start | bytes 1638400 | tf_op jit(solution)/shard_map/all_gather | solution.py:249
  107.5 31.6 %copy-start.5 = (bf16[320,320]{1,0:T(8,128)(2,1)S(1)}, bf16[320,320]{1,0:T(8,128)(2,1)}, u32[]{:S(2)}) copy-start(bf16[320,320]{1,0:T(8,128)(2,1)} %attn_out.1) | copy-start | bytes 614404
  107.5 31.6 %copy-start.6 = (bf16[320,320]{1,0:T(8,128)(2,1)S(1)}, bf16[320,320]{1,0:T(8,128)(2,1)}, u32[]{:S(2)}) copy-start(bf16[320,320]{1,0:T(8,128)(2,1)} %proj_out.1) | copy-start | bytes 614404
Sparse Core Ops, SparseCore 0:
  78.5 27.4 all-gather.3

commit v2 on v1

--- a/solution.py
+++ b/solution.py
@@ -62,26 +62,29 @@
     return inside.astype(F32)
 
 
-def taps(row, weight, index):
-    tokens, channels = row.shape
-    wide = row.astype(F32)
+def turned(ref):
+    return ref[...].astype(F32).T
+
+
+def taps(wide, weight, index):
+    tokens, channels = wide.shape
     at = lax.broadcasted_iota(jnp.int32, (tokens, channels), 0)
     left = jnp.where(at == 0, 0.0, pltpu.roll(wide, 1, 0)).astype(BF16)
     right = jnp.where(at == tokens - 1, 0.0, pltpu.roll(wide, tokens - 1, 0)).astype(BF16)
     total = dot(left, weight[index, 0])
-    total += dot(row, weight[index, 1])
+    total += dot(wide.astype(BF16), weight[index, 1])
     return total + dot(right, weight[index, 2])
 
 
 def own_row_body(hint, weight, bias, out):
-    out[...] = taps(hint[...], weight, 0) + bias[...]
-
-
-def merge_body(partial, above, below, weight_up, weight_down, zero_weight, zero_bias, features, merged_out, stats_out):
-    conv = partial[...] + taps(above[...], weight_up, 0) + taps(below[...], weight_down, 0)
+    out[...] = taps(turned(hint), weight, 1) + bias[...]
+
+
+def merge_body(partial, above, below, weight, zero_weight, zero_bias, features, merged_out, stats_out):
+    conv = partial[...] + taps(turned(above), weight, 0) + taps(turned(below), weight, 2)
     control = (conv / (1.0 + jnp.exp(-conv))).astype(BF16)
     branch = dot(control, zero_weight[...]) + zero_bias[...]
-    merged = (features[...].astype(F32) + branch).astype(BF16)
+    merged = (turned(features) + branch).astype(BF16)
     merged_out[...] = merged
     wide = merged.astype(F32)
     tokens, channels = wide.shape
@@ -124,66 +127,68 @@
         send[h] = block.astype(BF16)
 
 
-def attend_body(head_dim, q_rows, first, last, *refs):
-    received, refs = refs[0], refs[1:]
+def attend_body(head_dim, q_rows, first, compact, n_queries, n_pieces, *refs):
+    query_refs, refs = refs[:n_queries], refs[n_queries:]
+    pieces, refs = refs[:n_pieces], refs[n_pieces:]
     if not first:
-        acc_in, max_in, refs = refs[0], refs[1], refs[2:]
-    outs = 1 if last else 2
-    pieces, outs = refs[: len(refs) - outs], refs[len(refs) - outs :]
-    blocks, _, tokens = received.shape
-    depth = received.shape[1] - pieces[0].shape[1]
+        states, refs = refs[: 2 * n_queries], refs[2 * n_queries :]
+    blocks, depth, tokens = query_refs[0].shape
     per_step = q_rows // tokens
 
     def step(i, carry):
         rows = pl.ds(pl.multiple_of(i * q_rows, q_rows), q_rows)
-        queries = jnp.concatenate(
-            [received[i * per_step + j, :depth, :].astype(F32).T for j in range(per_step)], axis=0
-        ).astype(BF16)
-        if first:
-            acc = top = None
-        else:
-            acc, top = acc_in[rows, :], max_in[rows, :1]
-        for piece in pieces:
-            pair = jnp.concatenate([piece[b] for b in range(piece.shape[0])], axis=1)
-            scores = dot(queries, pair[:depth])
-            high = jnp.max(scores, axis=1, keepdims=True)
-            new_top = high if top is None else jnp.maximum(top, high)
-            probs = jnp.exp2(scores - new_top).astype(BF16)
-            ones = jnp.ones((128 - pair.shape[0], pair.shape[1]), BF16)
-            product = lax.dot_general(
-                probs,
-                jnp.concatenate([pair, ones], axis=0),
-                (((1,), (1,)), ((), ())),
-                preferred_element_type=F32,
-            )
-            acc = product if acc is None else acc * jnp.exp2(top - new_top) + product
-            top = new_top
-        if last:
-            total = acc.T
-            result = total[head_dim : 2 * head_dim] / total[2 * head_dim : 2 * head_dim + 1]
-            for j in range(per_step):
-                outs[0][i * per_step + j] = result[:, j * tokens : (j + 1) * tokens].astype(BF16)
-        else:
-            outs[0][rows, :] = acc
-            outs[1][rows, :] = jnp.broadcast_to(top, (q_rows, 128))
+        for n, received in enumerate(query_refs):
+            queries = jnp.concatenate(
+                [received[i * per_step + j].astype(F32).T for j in range(per_step)], axis=0
+            ).astype(BF16)
+            if first:
+                acc = top = None
+            else:
+                acc, top = states[2 * n][rows, :], states[2 * n + 1][rows, :1]
+            for piece in pieces:
+                pair = jnp.concatenate([piece[b] for b in range(piece.shape[0])], axis=1)
+                scores = dot(queries, pair[:depth])
+                high = jnp.max(scores, axis=1, keepdims=True)
+                new_top = high if top is None else jnp.maximum(top, high)
+                probs = jnp.exp2(scores - new_top).astype(BF16)
+                ones = jnp.ones((128 - pair.shape[0], pair.shape[1]), BF16)
+                product = lax.dot_general(
+                    probs,
+                    jnp.concatenate([pair, ones], axis=0),
+                    (((1,), (1,)), ((), ())),
+                    preferred_element_type=F32,
+                )
+                acc = product if acc is None else acc * jnp.exp2(top - new_top) + product
+                top = new_top
+            if compact:
+                both = acc.T[head_dim : 2 * head_dim + 8]
+                tops = jnp.broadcast_to(top, (q_rows, 128)).T[:8]
+                for j in range(per_step):
+                    at = slice(j * tokens, (j + 1) * tokens)
+                    refs[n][i * per_step + j, : head_dim + 8] = both[:, at]
+                    refs[n][i * per_step + j, head_dim + 8 :] = tops[:, at]
+            else:
+                refs[2 * n][rows, :] = acc
+                refs[2 * n + 1][rows, :] = jnp.broadcast_to(top, (q_rows, 128))
         return carry
 
     lax.fori_loop(0, blocks // per_step, step, 0)
 
 
-def attend(received, pieces, state, last, head_dim, q_rows=512):
-    blocks, _, tokens = received.shape
-    args = [received, *(state or ()), *pieces]
+def attend(queries, pieces, states, compact, head_dim, q_rows=512):
+    blocks, _, tokens = queries[0].shape
     rows = blocks * tokens
-    if last:
-        out_shape = jax.ShapeDtypeStruct((blocks, head_dim, tokens), BF16)
+    if compact:
+        out_shape = [jax.ShapeDtypeStruct((blocks, head_dim + 16, tokens), F32)] * len(queries)
     else:
-        out_shape = [jax.ShapeDtypeStruct((rows, 128), F32)] * 2
-    keys = sum(p.shape[0] * p.shape[2] for p in pieces)
+        out_shape = [jax.ShapeDtypeStruct((rows, 128), F32)] * (2 * len(queries))
+    keys = sum(p.shape[0] * p.shape[2] for p in pieces) * len(queries)
     return call(
-        functools.partial(attend_body, head_dim, q_rows, state is None, last),
+        functools.partial(
+            attend_body, head_dim, q_rows, states is None, compact, len(queries), len(pieces)
+        ),
         out_shape,
-        args,
+        [*queries, *pieces, *(states or ())],
         limit=48,
         flops=2 * rows * keys * 512,
         read=keys * 160,
@@ -191,10 +196,18 @@
     )
 
 
+def combine_body(head_dim, mine, theirs, out):
+    a, b = mine[...], theirs[...]
+    a_top, b_top = a[:, head_dim + 8 : head_dim + 9], b[:, head_dim + 8 : head_dim + 9]
+    top = jnp.maximum(a_top, b_top)
+    both = a[:, : head_dim + 8] * jnp.exp2(a_top - top) + b[:, : head_dim + 8] * jnp.exp2(b_top - top)
+    out[...] = (both[:, :head_dim] / both[:, head_dim : head_dim + 1]).astype(BF16)
+
+
 def finish_body(attended, inner, merged, attn_out, proj_out, out):
-    rows = attended[...].astype(F32).T.astype(BF16)
+    rows = turned(attended).astype(BF16)
     after = (inner[...].astype(F32) + dot(rows, attn_out[...])).astype(BF16)
-    out[...] = (merged[...].astype(F32) + dot(after, proj_out[...])).astype(BF16)
+    out[...] = (merged[...].astype(F32) + dot(after, proj_out[...])).T.astype(BF16)
 
 
 def local(
@@ -218,20 +231,21 @@
     everyone = lax.axis_size(SEQ)
     shape = jax.ShapeDtypeStruct
     onward = [(i, i + 1) for i in range(everyone - 1)]
+    hint, features = hint.T, features.T
     above = lax.ppermute(hint, SEQ, onward)
     below = lax.ppermute(hint, SEQ, [(b, a) for a, b in onward])
     row = lambda v: v.reshape(1, channels)
     partial = call(
         own_row_body,
         shape((tokens, channels), F32),
-        (hint, conv_weight[1:2], row(conv_bias)),
+        (hint, conv_weight, row(conv_bias)),
         flops=2 * tokens * channels * channels * 3,
-        read=3 * channels * channels * 2,
+        read=9 * channels * channels * 2,
     )
     merged, stats = call(
         merge_body,
         [shape((tokens, channels), BF16), shape((everyone, 128), F32)],
-        (partial, above, below, conv_weight[:1], conv_weight[2:], zero_weight, row(zero_bias), features),
+        (partial, above, below, conv_weight, zero_weight, row(zero_bias), features),
         flops=2 * tokens * channels * channels * 7,
         read=7 * channels * channels * 2,
     )
@@ -244,19 +258,30 @@
         read=4 * channels * channels * 2,
     )
     received = lax.all_to_all(send, "z", 0, 0, tiled=True)
-    pair = received[:, 128 - 2 * head_dim :, :]
-    by_core = lax.all_gather(pair, "c")
-    by_chip = lax.all_gather(by_core, "x")
-    pieces = [by_chip[i, j] for i in range(by_chip.shape[0]) for j in range(by_chip.shape[1])]
-    result = attend(received, pieces, None, True, head_dim)
+    depth = 128 - 2 * head_dim
+    queries, pair = received[:, :depth, :], received[:, depth:, :]
+    swap = [(0, 1), (1, 0)]
+    chips = lax.axis_size("x")
+    ring = lambda by: [(i, (i + by) % chips) for i in range(chips)]
+    others = lax.ppermute(queries, "c", swap)
+    left, right, far = (lax.ppermute(pair, "x", ring(by)) for by in (1, chips - 1, 2))
+    mine = attend([queries], [pair], None, False, head_dim)
+    theirs = attend([others], [pair], None, False, head_dim)
+    states = attend([queries, others], [left, right], [*mine, *theirs], False, head_dim)
+    (theirs,) = attend([others], [far], states[2:], True, head_dim)
+    back = lax.ppermute(theirs, "c", swap)
+    (mine,) = attend([queries], [far], states[:2], True, head_dim)
+    result = call(
+        functools.partial(combine_body, head_dim), shape((HEADS, head_dim, tokens), BF16), (mine, back)
+    )
     attended = lax.all_to_all(result, "z", 0, 0, tiled=True).reshape(channels, tokens)
     return call(
         finish_body,
-        shape((tokens, channels), BF16),
+        shape((channels, tokens), BF16),
         (attended, inner, merged, attn_out, proj_out),
         flops=2 * tokens * channels * channels * 2,
         read=2 * channels * channels * 2,
-    )
+    ).T
 
 
 def solution(mesh):

time: 148 us -> 121 us (0.82)
  waiting for transfers between devices: 39.9 us -> 12.3 us
  between operations: 13.6 us -> 0.26 us
  starting transfers between devices: 28.7 us -> 41.6 us
  Pallas kernels: 15.4 us -> 23.4 us
  blocking collectives: 42.3 us -> 35.4 us
    all_gather x1 -> x0, waiting for transfers between devices: 27.6 us -> none  [local(): by_chip = lax.all_gather(by_core, 'x')]
    ppermute x0 -> x5, starting transfers between devices: none -> 13.1 us  [the longest x3 8.76 us: local(): lax.ppermute(pair, 'x', ring(by))]
    pallas_call x5 -> x10, Pallas kernels: 15.4 us -> 23.4 us  [call(): pl.pallas_call(body, out_shape=out_shape, in_specs=[VMEM] * len(args), ou...]
    all_to_all x1, blocking collectives: 20.8 us -> 16 us  [local(): lax.all_to_all(result, 'z', 0, 0, tiled=True).reshape(channels, tokens)]
    unnamed x24 -> x26, local copies, waits for them, and re-layouts: 3.12 us -> 5.56 us
    all_gather x1 -> x0, blocking collectives: 2.17 us -> none  [local(): by_core = lax.all_gather(pair, 'c')]
    slice x2, local copies, waits for them, and re-layouts: 1.79 us -> 0.02 us  [local(): queries, pair = (received[:, :depth, :], received[:, depth:, :])]
  transfers between devices with their start and end apart: 4 -> 8, of which waited for: 2 -> 1; matrix products, arithmetic and copies ran while one was open for 2% -> 1% of each run, Pallas kernels for 0% -> 14%
where the time goes in v2:
time: 121 us; the launch traced here: 120 us
  starting transfers between devices  41.6 us (34%)
  blocking collectives  35.4 us (29%)
  Pallas kernels  23.4 us (19%)
  waiting for transfers between devices  12.3 us (10%)
  local copies, waits for them, and re-layouts  6.97 us (6%)
    all_to_all x1, starting transfers between devices, local(): stats = lax.all_to_all(stats, SEQ, 0, 0, tiled=True)  24.2 us
    pallas_call x10, Pallas kernels, call(): pl.pallas_call(body, out_shape=out_shape, in_specs=[VMEM] * len(args), ou...  23.4 us
    all_to_all x1, blocking collectives, local(): received = lax.all_to_all(send, 'z', 0, 0, tiled=True)  19.4 us
    all_to_all x1, blocking collectives, local(): lax.all_to_all(result, 'z', 0, 0, tiled=True).reshape(channels, tokens)  16 us
    all_to_all x1, waiting for transfers between devices, local(): stats = lax.all_to_all(stats, SEQ, 0, 0, tiled=True)  12.3 us
    ppermute x3, starting transfers between devices, local(): lax.ppermute(pair, 'x', ring(by))  8.76 us
    unnamed x26, local copies, waits for them, and re-layouts  5.56 us
    ppermute x1, starting transfers between devices, local(): above = lax.ppermute(hint, SEQ, onward)  3.04 us
  transfers between devices with their start and end apart: 8, of which 1 were waited for; matrix products, arithmetic and copies ran while one was open for 1% of the time, Pallas kernels for 14%

profile of v2, /device:TPU:24, one launch (start us, length us, event | category | flops | bytes accessed | tf_op | source)
XLA Modules:
  0.0 119.9 jit_solution(4692286307003723473)
XLA Ops:
  0.0 1.3 %collective-permute-start.1 = (bf16[320,128]{1,0:T(8,128)(2,1)}, bf16[320,128]{1,0:T(8,128)(2,1)S(1)}, u32[]{:S(2)}, u32[]{:S(2)}) collective-permute-start(bf16[320,128]{1,0:T(8,128)(2,1)} %bitcast.10), channel_id=1, source_target_pairs={{1,0},{2,1},{3,2},{4,3},{5,4},{6,5},{7,6},{8,7},{9,8},{10,9},{11,1... | collective-permute-start | bytes 245768 | tf_op jit(solution)/shard_map/ppermute | solution.py:236
  1.3 3.0 %collective-permute-start = (bf16[320,128]{1,0:T(8,128)(2,1)}, bf16[320,128]{1,0:T(8,128)(2,1)S(1)}, u32[]{:S(2)}, u32[]{:S(2)}) collective-permute-start(bf16[320,128]{1,0:T(8,128)(2,1)} %bitcast.11), channel_id=1, source_target_pairs={{0,1},{1,2},{2,3},{3,4},{4,5},{5,6},{6,7},{7,8},{8,9},{9,10},{10,1... | collective-permute-start | bytes 245768 | tf_op jit(solution)/shard_map/ppermute | solution.py:235
  4.3 0.0 copy-start.12
  4.3 0.7 reshape.17.bias
  5.0 0.0 copy-start.11
  5.0 0.7 reshape.18.zero_bias
  5.7 1.6 %copy-done = bf16[3,3,320,320]{3,2,1,0:T(8,128)(2,1)S(1)} copy-done((bf16[3,3,320,320]{3,2,1,0:T(8,128)(2,1)S(1)}, bf16[3,3,320,320]{3,2,1,0:T(8,128)(2,1)}, u32[]{:S(2)}) %copy-start) | copy-done | bytes 1843224
  7.4 0.9 copy-done.9
  8.3 0.0 copy-start.5
  8.3 0.4 shard_map.136.partial
  8.7 0.0 collective-permute-done.1.below
  8.7 0.0 collective-permute-done.above
  8.7 1.2 copy-done.1
  9.9 0.9 copy-done.6
  10.8 0.9 copy-done.10
  11.7 2.0 %shard_map.137 = (bf16[128,320]{1,0:T(8,128)(2,1)S(1)}, f32[64,128]{1,0:T(8,128)}) custom-call(f32[128,320]{1,0:T(8,128)S(1)} %shard_map.136.partial, bf16[320,128]{1,0:T(8,128)(2,1)S(1)} %collective-permute-done.above, bf16[320,128]{1,0:T(8,128)(2,1)S(1)} %collective-permute-done.1.below, bf16[3,3,320,320]{3,2,1,0:T(8,128)(2,1)S(1)} %copy-done.1, ...), custom_call_target="tpu_custom_call" | custom-call | flops 183500800 | bytes 1433600 | tf_op jit(solution)/shard_map/pallas_call | solution.py:36
  13.7 24.2 %all-to-all-start = ((f32[64,1,128]{2,1,0:T(1,128)}), f32[64,1,128]{2,1,0:T(1,128)S(1)}, u32[]{:S(2)}, u32[]{:S(2)}) async-start(f32[64,1,128]{2,1,0:T(1,128)} %bitcast.3), calls=%async_computation | async-start | bytes 65536 | tf_op jit(solution)/shard_map/all_to_all | solution.py:252
  37.9 0.0 copy-done.11
  37.9 0.0 copy-done.12
  38.0 12.3 %all-to-all-done = f32[64,1,128]{2,1,0:T(1,128)S(1)} async-done(((f32[64,1,128]{2,1,0:T(1,128)}), f32[64,1,128]{2,1,0:T(1,128)S(1)}, u32[]{:S(2)}, u32[]{:S(2)}) %all-to-all-start) | async-done | bytes 32800 | tf_op jit(solution)/shard_map/all_to_all | solution.py:252
  50.3 0.0 copy-done.2
  50.3 0.0 copy-done.3
  50.3 0.0 copy-done.4
  50.3 0.0 copy-done.5
  50.3 1.0 shard_map.138
  51.3 19.4 %all_to_all.21 = bf16[8,128,128]{2,1,0:T(8,128)(2,1)S(1)} all-to-all(bf16[8,128,128]{2,1,0:T(8,128)(2,1)S(1)} %get-tuple-element.19), channel_id=1, replica_groups=mesh['dp'=8,'x'=4,'z'=8,'c'=2] {'z'}, dimensions={0} | all-to-all | bytes 524288 | tf_op jit(solution)/shard_map/all_to_all | solution.py:260
  70.7 3.0 %collective-permute-start.5 = (bf16[8,80,128]{2,1,0:T(8,128)(2,1)S(1)}, bf16[8,80,128]{2,1,0:T(8,128)(2,1)S(1)}, u32[]{:S(2)}, u32[]{:S(2)}) collective-permute-start(bf16[8,80,128]{2,1,0:T(8,128)(2,1)S(1)} %slice.9.refs_1_), channel_id=1, source_target_pairs={{0,48},{16,0},{32,16},{48,32},{1,49},{17,1},{33,17},{49,33},{2,50}... | collective-permute-start | bytes 491528 | tf_op jit(solution)/shard_map/ppermute | solution.py:267
  73.6 2.9 %collective-permute-start.4 = (bf16[8,80,128]{2,1,0:T(8,128)(2,1)S(1)}, bf16[8,80,128]{2,1,0:T(8,128)(2,1)S(1)}, u32[]{:S(2)}, u32[]{:S(2)}) collective-permute-start(bf16[8,80,128]{2,1,0:T(8,128)(2,1)S(1)} %slice.9.refs_1_), channel_id=1, source_target_pairs={{0,16},{16,32},{32,48},{48,0},{1,17},{17,33},{33,49},{49,1},{2,18}... | collective-permute-start | bytes 491528 | tf_op jit(solution)/shard_map/ppermute | solution.py:267
  76.5 2.9 %collective-permute-start.2 = (bf16[8,80,128]{2,1,0:T(8,128)(2,1)S(1)}, bf16[8,80,128]{2,1,0:T(8,128)(2,1)S(1)}, u32[]{:S(2)}, u32[]{:S(2)}) collective-permute-start(bf16[8,80,128]{2,1,0:T(8,128)(2,1)S(1)} %slice.9.refs_1_), channel_id=1, source_target_pairs={{0,32},{16,48},{32,0},{48,16},{1,33},{17,49},{33,1},{49,17},{2,34}... | collective-permute-start | bytes 491528 | tf_op jit(solution)/shard_map/ppermute | solution.py:267
  79.5 1.9 %collective-permute-start.3 = (bf16[8,48,128]{2,1,0:T(8,128)(2,1)S(1)}, bf16[8,48,128]{2,1,0:T(8,128)(2,1)S(1)}, u32[]{:S(2)}, u32[]{:S(2)}) collective-permute-start(bf16[8,48,128]{2,1,0:T(8,128)(2,1)S(1)} %slice.8.refs_0_), channel_id=1, source_target_pairs={{0,1},{1,0},{2,3},{3,2},{4,5},{5,4},{6,7},{7,6},{8,9},{9,8},{10,11... | collective-permute-start | bytes 294920 | tf_op jit(solution)/shard_map/ppermute | solution.py:266
  81.4 2.2 %shard_map.139 = (f32[1024,128]{1,0:T(8,128)S(1)}, f32[1024,128]{1,0:T(8,128)S(1)}) custom-call(bf16[8,48,128]{2,1,0:T(8,128)(2,1)S(1)} %slice.8.refs_0_, bf16[8,80,128]{2,1,0:T(8,128)(2,1)S(1)} %slice.9.refs_1_), custom_call_target="tpu_custom_call" | custom-call | flops 1073741824 | bytes 163840 | tf_op jit(solution)/shard_map/pallas_call | solution.py:36
  83.6 0.0 collective-permute-done.3.refs_0_.refs_1_
  83.6 2.2 %shard_map.140 = (f32[1024,128]{1,0:T(8,128)S(1)}, f32[1024,128]{1,0:T(8,128)S(1)}) custom-call(bf16[8,48,128]{2,1,0:T(8,128)(2,1)S(1)} %collective-permute-done.3.refs_0_.refs_1_, bf16[8,80,128]{2,1,0:T(8,128)(2,1)S(1)} %slice.9.refs_1_), custom_call_target="tpu_custom_call" | custom-call | flops 1073741824 | bytes 163840 | tf_op jit(solution)/shard_map/pallas_call | solution.py:36
  85.9 0.0 collective-permute-done.5.refs_3_
  85.9 0.0 collective-permute-done.4.refs_2_
  85.9 9.0 %shard_map.141 = (f32[1024,128]{1,0:T(8,128)S(1)}, f32[1024,128]{1,0:T(8,128)S(1)}, f32[1024,128]{1,0:T(8,128)S(1)}, f32[1024,128]{1,0:T(8,128)S(1)}) custom-call(bf16[8,48,128]{2,1,0:T(8,128)(2,1)S(1)} %slice.8.refs_0_, bf16[8,48,128]{2,1,0:T(8,128)(2,1)S(1)} %collective-permute-done.3.refs_0_.refs_1_, ...), custom_call_target="tpu_custom_call" | custom-call | flops 4294967296 | bytes 655360 | tf_op jit(solution)/shard_map/pallas_call | solution.py:36
  95.0 0.0 collective-permute-done.2.refs_1_
  95.0 2.6 %shard_map.143 = f32[8,56,128]{2,1,0:T(8,128)S(1)} custom-call(bf16[8,48,128]{2,1,0:T(8,128)(2,1)S(1)} %collective-permute-done.3.refs_0_.refs_1_, bf16[8,80,128]{2,1,0:T(8,128)(2,1)S(1)} %collective-permute-done.2.refs_1_, f32[1024,128]{1,0:T(8,128)S(1)} %get-tuple-element.26.refs_2_, f32[1024,128]{1,0:T(8,128)S(1)} %get-tuple-element.27.refs_3_), custom_call_target="tpu_custom_call" | custom-call | flops 1073741824 | bytes 163840 | tf_op jit(solution)/shard_map/pallas_call | solution.py:36
  97.6 2.4 %collective-permute-start.6 = (f32[8,56,128]{2,1,0:T(8,128)S(1)}, f32[8,56,128]{2,1,0:T(8,128)S(1)}, u32[]{:S(2)}, u32[]{:S(2)}) collective-permute-start(f32[8,56,128]{2,1,0:T(8,128)S(1)} %shard_map.143), channel_id=1, source_target_pairs={{0,1},{1,0},{2,3},{3,2},{4,5},{5,4},{6,7},{7,6},{8,9},{9,8},{10,11... | collective-permute-start | bytes 688136 | tf_op jit(solution)/shard_map/ppermute | solution.py:272
  100.0 0.0 copy-start.7
  100.0 0.0 copy-start.8
  100.0 2.6 %shard_map.142.mine = f32[8,56,128]{2,1,0:T(8,128)S(1)} custom-call(bf16[8,48,128]{2,1,0:T(8,128)(2,1)S(1)} %slice.8.refs_0_, bf16[8,80,128]{2,1,0:T(8,128)(2,1)S(1)} %collective-permute-done.2.refs_1_, f32[1024,128]{1,0:T(8,128)S(1)} %get-tuple-element.24.refs_2_, f32[1024,128]{1,0:T(8,128)S(1)} %get-tuple-element.25.refs_3_), custom_call_target="tpu_custom_call" | custom-call | flops 1073741824 | bytes 163840 | tf_op jit(solution)/shard_map/pallas_call | solution.py:36
  102.6 0.0 collective-permute-done.6.theirs
  102.6 0.1 shard_map.144
  102.7 16.0 %all_to_all.22 = bf16[8,40,128]{2,1,0:T(8,128)(2,1)S(1)} all-to-all(bf16[8,40,128]{2,1,0:T(8,128)(2,1)S(1)} %shard_map.144), channel_id=1, replica_groups=mesh['dp'=8,'x'=4,'z'=8,'c'=2] {'z'}, dimensions={0} | all-to-all | bytes 163840 | tf_op jit(solution)/shard_map/all_to_all | solution.py:277
  118.8 0.0 copy-done.7
  118.8 0.0 copy-done.8
  118.8 1.1 shard_map.145
  (12 shorter events, 0.0 us)
Async XLA Ops:
  0.0 8.7 %collective-permute-start.1 = (bf16[320,128]{1,0:T(8,128)(2,1)}, bf16[320,128]{1,0:T(8,128)(2,1)S(1)}, u32[]{:S(2)}, u32[]{:S(2)}) collective-permute-start(bf16[320,128]{1,0:T(8,128)(2,1)} %bitcast.10), channel_id=1, source_target_pairs={{1,0},{2,1},{3,2},{4,3},{5,4},{6,5},{7,6},{8,7},{9,8},{10,9},{11,1... | collective-permute-start | bytes 245768 | tf_op jit(solution)/shard_map/ppermute | solution.py:236
  1.3 7.4 %collective-permute-start = (bf16[320,128]{1,0:T(8,128)(2,1)}, bf16[320,128]{1,0:T(8,128)(2,1)S(1)}, u32[]{:S(2)}, u32[]{:S(2)}) collective-permute-start(bf16[320,128]{1,0:T(8,128)(2,1)} %bitcast.11), channel_id=1, source_target_pairs={{0,1},{1,2},{2,3},{3,4},{4,5},{5,6},{6,7},{7,8},{8,9},{9,10},{10,1... | collective-permute-start | bytes 245768 | tf_op jit(solution)/shard_map/ppermute | solution.py:235
  4.3 33.6 %copy-start.12 = (f32[320]{0:T(512)S(1)}, f32[320]{0:T(512)}, u32[]{:S(2)}) copy-start(f32[320]{0:T(512)} %param.22) | copy-start | bytes 3844
  5.0 32.9 %copy-start.11 = (f32[320]{0:T(512)S(1)}, f32[320]{0:T(512)}, u32[]{:S(2)}) copy-start(f32[320]{0:T(512)} %param.20) | copy-start | bytes 3844
  5.7 1.6 %copy-start = (bf16[3,3,320,320]{3,2,1,0:T(8,128)(2,1)S(1)}, bf16[3,3,320,320]{3,2,1,0:T(8,128)(2,1)}, u32[]{:S(2)}) copy-start(bf16[3,3,320,320]{3,2,1,0:T(8,128)(2,1)} %weight.3) | copy-start | bytes 5529604
  7.4 0.9 copy-start.9
  8.2 1.6 %copy-start.1 = (bf16[3,3,320,320]{3,2,1,0:T(8,128)(2,1)S(1)}, bf16[3,3,320,320]{3,2,1,0:T(8,128)(2,1)}, u32[]{:S(2)}) copy-start(bf16[3,3,320,320]{3,2,1,0:T(8,128)(2,1)} %weight.3) | copy-start | bytes 5529604
  8.2 42.0 %copy-start.2 = (bf16[320,320]{1,0:T(8,128)(2,1)S(1)}, bf16[320,320]{1,0:T(8,128)(2,1)}, u32[]{:S(2)}) copy-start(bf16[320,320]{1,0:T(8,128)(2,1)} %proj_in.1) | copy-start | bytes 614404
  8.2 42.0 %copy-start.3 = (bf16[320,320]{1,0:T(8,128)(2,1)S(1)}, bf16[320,320]{1,0:T(8,128)(2,1)}, u32[]{:S(2)}) copy-start(bf16[320,320]{1,0:T(8,128)(2,1)} %wq.1) | copy-start | bytes 614404
  8.3 42.0 %copy-start.4 = (bf16[320,320]{1,0:T(8,128)(2,1)S(1)}, bf16[320,320]{1,0:T(8,128)(2,1)}, u32[]{:S(2)}) copy-start(bf16[320,320]{1,0:T(8,128)(2,1)} %wk.1) | copy-start | bytes 614404
  8.3 42.0 %copy-start.5 = (bf16[320,320]{1,0:T(8,128)(2,1)S(1)}, bf16[320,320]{1,0:T(8,128)(2,1)}, u32[]{:S(2)}) copy-start(bf16[320,320]{1,0:T(8,128)(2,1)} %wv.1) | copy-start | bytes 614404
  9.9 0.9 copy-start.6
  10.8 0.9 copy-start.10
  13.7 36.5 %all-to-all-start = ((f32[64,1,128]{2,1,0:T(1,128)}), f32[64,1,128]{2,1,0:T(1,128)S(1)}, u32[]{:S(2)}, u32[]{:S(2)}) async-start(f32[64,1,128]{2,1,0:T(1,128)} %bitcast.3), calls=%async_computation | async-start | bytes 65536 | tf_op jit(solution)/shard_map/all_to_all | solution.py:252
  70.7 15.2 %collective-permute-start.5 = (bf16[8,80,128]{2,1,0:T(8,128)(2,1)S(1)}, bf16[8,80,128]{2,1,0:T(8,128)(2,1)S(1)}, u32[]{:S(2)}, u32[]{:S(2)}) collective-permute-start(bf16[8,80,128]{2,1,0:T(8,128)(2,1)S(1)} %slice.9.refs_1_), channel_id=1, source_target_pairs={{0,48},{16,0},{32,16},{48,32},{1,49},{17,1},{33,17},{49,33},{2,50}... | collective-permute-start | bytes 491528 | tf_op jit(solution)/shard_map/ppermute | solution.py:267
  73.6 12.3 %collective-permute-start.4 = (bf16[8,80,128]{2,1,0:T(8,128)(2,1)S(1)}, bf16[8,80,128]{2,1,0:T(8,128)(2,1)S(1)}, u32[]{:S(2)}, u32[]{:S(2)}) collective-permute-start(bf16[8,80,128]{2,1,0:T(8,128)(2,1)S(1)} %slice.9.refs_1_), channel_id=1, source_target_pairs={{0,16},{16,32},{32,48},{48,0},{1,17},{17,33},{33,49},{49,1},{2,18}... | collective-permute-start | bytes 491528 | tf_op jit(solution)/shard_map/ppermute | solution.py:267
  76.5 18.4 %collective-permute-start.2 = (bf16[8,80,128]{2,1,0:T(8,128)(2,1)S(1)}, bf16[8,80,128]{2,1,0:T(8,128)(2,1)S(1)}, u32[]{:S(2)}, u32[]{:S(2)}) collective-permute-start(bf16[8,80,128]{2,1,0:T(8,128)(2,1)S(1)} %slice.9.refs_1_), channel_id=1, source_target_pairs={{0,32},{16,48},{32,0},{48,16},{1,33},{17,49},{33,1},{49,17},{2,34}... | collective-permute-start | bytes 491528 | tf_op jit(solution)/shard_map/ppermute | solution.py:267
  79.5 4.2 %collective-permute-start.3 = (bf16[8,48,128]{2,1,0:T(8,128)(2,1)S(1)}, bf16[8,48,128]{2,1,0:T(8,128)(2,1)S(1)}, u32[]{:S(2)}, u32[]{:S(2)}) collective-permute-start(bf16[8,48,128]{2,1,0:T(8,128)(2,1)S(1)} %slice.8.refs_0_), channel_id=1, source_target_pairs={{0,1},{1,0},{2,3},{3,2},{4,5},{5,4},{6,7},{7,6},{8,9},{9,8},{10,11... | collective-permute-start | bytes 294920 | tf_op jit(solution)/shard_map/ppermute | solution.py:266
  97.6 5.1 %collective-permute-start.6 = (f32[8,56,128]{2,1,0:T(8,128)S(1)}, f32[8,56,128]{2,1,0:T(8,128)S(1)}, u32[]{:S(2)}, u32[]{:S(2)}) collective-permute-start(f32[8,56,128]{2,1,0:T(8,128)S(1)} %shard_map.143), channel_id=1, source_target_pairs={{0,1},{1,0},{2,3},{3,2},{4,5},{5,4},{6,7},{7,6},{8,9},{9,8},{10,11... | collective-permute-start | bytes 688136 | tf_op jit(solution)/shard_map/ppermute | solution.py:272
  100.0 18.8 %copy-start.7 = (bf16[320,320]{1,0:T(8,128)(2,1)S(1)}, bf16[320,320]{1,0:T(8,128)(2,1)}, u32[]{:S(2)}) copy-start(bf16[320,320]{1,0:T(8,128)(2,1)} %attn_out.1) | copy-start | bytes 614404
  100.0 18.8 %copy-start.8 = (bf16[320,320]{1,0:T(8,128)(2,1)S(1)}, bf16[320,320]{1,0:T(8,128)(2,1)}, u32[]{:S(2)}) copy-start(bf16[320,320]{1,0:T(8,128)(2,1)} %proj_out.1) | copy-start | bytes 614404

commit v3 on v2

--- a/solution.py
+++ b/solution.py
@@ -20,6 +20,7 @@
 F32 = jnp.float32
 BF16 = jnp.bfloat16
 VMEM = pl.BlockSpec(memory_space=pltpu.VMEM)
+SMEM = pl.BlockSpec(memory_space=pltpu.SMEM)
 MIB = 1024 * 1024
 
 
@@ -31,12 +32,12 @@
     return jnp.dot(a, b, precision=HIGHEST, preferred_element_type=F32)
 
 
-def call(body, out_shape, args, scratch=(), limit=24, flops=0, read=0, trans=0):
+def call(body, out_shape, args, scratch=(), limit=24, flops=0, read=0, trans=0, smem=0):
     many = isinstance(out_shape, (list, tuple))
     return pl.pallas_call(
         body,
         out_shape=out_shape,
-        in_specs=[VMEM] * len(args),
+        in_specs=[SMEM] * smem + [VMEM] * (len(args) - smem),
         out_specs=[VMEM] * len(out_shape) if many else VMEM,
         scratch_shapes=scratch,
         compiler_params=pltpu.CompilerParams(vmem_limit_bytes=limit * MIB),
@@ -68,23 +69,28 @@
 
 def taps(wide, weight, index):
     tokens, channels = wide.shape
-    at = lax.broadcasted_iota(jnp.int32, (tokens, channels), 0)
-    left = jnp.where(at == 0, 0.0, pltpu.roll(wide, 1, 0)).astype(BF16)
-    right = jnp.where(at == tokens - 1, 0.0, pltpu.roll(wide, tokens - 1, 0)).astype(BF16)
-    total = dot(left, weight[index, 0])
-    total += dot(wide.astype(BF16), weight[index, 1])
-    return total + dot(right, weight[index, 2])
-
-
-def own_row_body(hint, weight, bias, out):
-    out[...] = taps(turned(hint), weight, 1) + bias[...]
-
-
-def merge_body(partial, above, below, weight, zero_weight, zero_bias, features, merged_out, stats_out):
-    conv = partial[...] + taps(turned(above), weight, 0) + taps(turned(below), weight, 2)
+    column = lax.broadcasted_iota(jnp.int32, (tokens, channels), 0)
+    left = jnp.where(column == 0, 0.0, pltpu.roll(wide, 1, 0)).astype(BF16)
+    right = jnp.where(column == tokens - 1, 0.0, pltpu.roll(wide, tokens - 1, 0)).astype(BF16)
+    at = (lambda b: b) if index is None else (lambda b: (index, b))
+    total = dot(left, weight[at(0)])
+    total += dot(wide.astype(BF16), weight[at(1)])
+    return total + dot(right, weight[at(2)])
+
+
+def own_row_body(core, hint, pair, weight, bias, features, zero_weight, partial, odd_weight, features_out, zero_out):
+    pair_row = 2 - 2 * core[0]
+    partial[...] = taps(turned(hint), weight, 1) + taps(turned(pair), weight, pair_row) + bias[...]
+    odd_weight[...] = weight[2 - pair_row]
+    features_out[...] = turned(features)
+    zero_out[...] = zero_weight[...]
+
+
+def merge_body(partial, odd, odd_weight, zero_weight, zero_bias, features, merged_out, stats_out):
+    conv = partial[...] + taps(turned(odd), odd_weight, None)
     control = (conv / (1.0 + jnp.exp(-conv))).astype(BF16)
     branch = dot(control, zero_weight[...]) + zero_bias[...]
-    merged = (turned(features) + branch).astype(BF16)
+    merged = (features[...] + branch).astype(BF16)
     merged_out[...] = merged
     wide = merged.astype(F32)
     tokens, channels = wide.shape
@@ -135,8 +141,8 @@
     blocks, depth, tokens = query_refs[0].shape
     per_step = q_rows // tokens
 
-    def step(i, carry):
-        rows = pl.ds(pl.multiple_of(i * q_rows, q_rows), q_rows)
+    for i in range(blocks // per_step):
+        rows = slice(i * q_rows, (i + 1) * q_rows)
         for n, received in enumerate(query_refs):
             queries = jnp.concatenate(
                 [received[i * per_step + j].astype(F32).T for j in range(per_step)], axis=0
@@ -170,12 +176,9 @@
             else:
                 refs[2 * n][rows, :] = acc
                 refs[2 * n + 1][rows, :] = jnp.broadcast_to(top, (q_rows, 128))
-        return carry
-
-    lax.fori_loop(0, blocks // per_step, step, 0)
-
-
-def attend(queries, pieces, states, compact, head_dim, q_rows=512):
+
+
+def attend(queries, pieces, states, compact, head_dim, q_rows=1024):
     blocks, _, tokens = queries[0].shape
     rows = blocks * tokens
     if compact:
@@ -230,24 +233,32 @@
     head_dim = channels // HEADS
     everyone = lax.axis_size(SEQ)
     shape = jax.ShapeDtypeStruct
-    onward = [(i, i + 1) for i in range(everyone - 1)]
     hint, features = hint.T, features.T
-    above = lax.ppermute(hint, SEQ, onward)
-    below = lax.ppermute(hint, SEQ, [(b, a) for a, b in onward])
+    core = lax.axis_index("c").reshape(1)
+    swap = [(0, 1), (1, 0)]
+    ends = [(i, i + 1) for i in range(1, everyone - 1, 2)]
+    odd = lax.ppermute(hint, SEQ, ends + [(b, a) for a, b in ends])
+    pair = lax.ppermute(hint, "c", swap)
     row = lambda v: v.reshape(1, channels)
-    partial = call(
+    partial, odd_weight, features, zero_weight = call(
         own_row_body,
-        shape((tokens, channels), F32),
-        (hint, conv_weight, row(conv_bias)),
-        flops=2 * tokens * channels * channels * 3,
-        read=9 * channels * channels * 2,
+        [
+            shape((tokens, channels), F32),
+            shape(conv_weight.shape[1:], BF16),
+            shape((tokens, channels), F32),
+            shape(zero_weight.shape, BF16),
+        ],
+        (core, hint, pair, conv_weight, row(conv_bias), features, zero_weight),
+        smem=1,
+        flops=2 * tokens * channels * channels * 6,
+        read=10 * channels * channels * 2,
     )
     merged, stats = call(
         merge_body,
         [shape((tokens, channels), BF16), shape((everyone, 128), F32)],
-        (partial, above, below, conv_weight, zero_weight, row(zero_bias), features),
-        flops=2 * tokens * channels * channels * 7,
-        read=7 * channels * channels * 2,
+        (partial, odd, odd_weight, zero_weight, row(zero_bias), features),
+        flops=2 * tokens * channels * channels * 4,
+        read=4 * channels * channels * 2,
     )
     stats = lax.all_to_all(stats, SEQ, 0, 0, tiled=True)
     inner, send = call(
@@ -260,17 +271,14 @@
     received = lax.all_to_all(send, "z", 0, 0, tiled=True)
     depth = 128 - 2 * head_dim
     queries, pair = received[:, :depth, :], received[:, depth:, :]
-    swap = [(0, 1), (1, 0)]
     chips = lax.axis_size("x")
     ring = lambda by: [(i, (i + by) % chips) for i in range(chips)]
     others = lax.ppermute(queries, "c", swap)
-    left, right, far = (lax.ppermute(pair, "x", ring(by)) for by in (1, chips - 1, 2))
-    mine = attend([queries], [pair], None, False, head_dim)
-    theirs = attend([others], [pair], None, False, head_dim)
-    states = attend([queries, others], [left, right], [*mine, *theirs], False, head_dim)
-    (theirs,) = attend([others], [far], states[2:], True, head_dim)
+    pieces = [lax.ppermute(pair, "x", ring(by)) for by in (1, chips - 1, 2)]
+    states = attend([queries, others], [pair], None, False, head_dim)
+    (theirs,) = attend([others], pieces, states[2:], True, head_dim)
     back = lax.ppermute(theirs, "c", swap)
-    (mine,) = attend([queries], [far], states[:2], True, head_dim)
+    (mine,) = attend([queries], pieces, states[:2], True, head_dim)
     result = call(
         functools.partial(combine_body, head_dim), shape((HEADS, head_dim, tokens), BF16), (mine, back)
     )

time: 121 us -> 116 us (0.959)
  Pallas kernels: 23.4 us -> 19.4 us
  waiting for transfers between devices: 12.3 us -> 15.7 us
  starting transfers between devices: 41.6 us -> 38.6 us
    pallas_call x10 -> x8, Pallas kernels: 23.4 us -> 19.4 us  [call(): pl.pallas_call(body, out_shape=out_shape, in_specs=[SMEM] * smem + [VMEM]...]
    ppermute x5, waiting for transfers between devices: 0.01 us -> 3.4 us  [the longest x3 3.39 us: local(): pieces = [lax.ppermute(pair, 'x', ring(by)) for by in (1, chips - 1, 2)]]
    all_to_all x1, starting transfers between devices: 24.2 us -> 22.5 us  [local(): stats = lax.all_to_all(stats, SEQ, 0, 0, tiled=True)]
    unnamed x26 -> x24, local copies, waits for them, and re-layouts: 5.56 us -> 4.38 us
  transfers between devices with their start and end apart: 8 -> 8, of which waited for: 1 -> 2; matrix products, arithmetic and copies ran while one was open for 1% -> 1% of each run, Pallas kernels for 14% -> 9%
where the time goes in v3:
time: 116 us; the launch traced here: 115 us
  starting transfers between devices  38.6 us (33%)
  blocking collectives  35.5 us (31%)
  Pallas kernels  19.4 us (17%)
  waiting for transfers between devices  15.7 us (14%)
  local copies, waits for them, and re-layouts  5.77 us (5%)
    all_to_all x1, starting transfers between devices, local(): stats = lax.all_to_all(stats, SEQ, 0, 0, tiled=True)  22.5 us
    pallas_call x8, Pallas kernels, call(): pl.pallas_call(body, out_shape=out_shape, in_specs=[SMEM] * smem + [VMEM]...  19.4 us
    all_to_all x1, blocking collectives, local(): received = lax.all_to_all(send, 'z', 0, 0, tiled=True)  19.3 us
    all_to_all x1, blocking collectives, local(): lax.all_to_all(result, 'z', 0, 0, tiled=True).reshape(channels, tokens)  16.2 us
    all_to_all x1, waiting for transfers between devices, local(): stats = lax.all_to_all(stats, SEQ, 0, 0, tiled=True)  12.3 us
    ppermute x3, starting transfers between devices, local(): pieces = [lax.ppermute(pair, 'x', ring(by)) for by in (1, chips - 1, 2)]  9.27 us
    unnamed x24, local copies, waits for them, and re-layouts  4.38 us
    ppermute x3, waiting for transfers between devices, local(): pieces = [lax.ppermute(pair, 'x', ring(by)) for by in (1, chips - 1, 2)]  3.39 us
  transfers between devices with their start and end apart: 8, of which 2 were waited for; matrix products, arithmetic and copies ran while one was open for 1% of the time, Pallas kernels for 9%

profile of v3, /device:TPU:24, one launch (start us, length us, event | category | flops | bytes accessed | tf_op | source)
XLA Modules:
  0.0 115.2 jit_solution(12287099703248194827)
XLA Ops:
  0.0 0.0 copy-start.10
  0.0 0.0 copy-start.11
  0.0 2.0 %collective-permute-start = (bf16[320,128]{1,0:T(8,128)(2,1)}, bf16[320,128]{1,0:T(8,128)(2,1)S(1)}, u32[]{:S(2)}, u32[]{:S(2)}) collective-permute-start(bf16[320,128]{1,0:T(8,128)(2,1)} %bitcast.12), channel_id=1, source_target_pairs={{0,1},{1,0},{2,3},{3,2},{4,5},{5,4},{6,7},{7,6},{8,9},{9,8},{10,11... | collective-permute-start | bytes 245768 | tf_op jit(solution)/shard_map/ppermute | solution.py:241
  2.1 0.7 collective-permute-start.1
  2.7 0.7 reshape.21.bias
  3.4 0.7 reshape.22.zero_bias
  4.1 0.0 collective-permute-done.pair
  4.1 0.0 copy-start
  4.1 1.6 %copy-done = bf16[3,3,320,320]{3,2,1,0:T(8,128)(2,1)S(1)} copy-done((bf16[3,3,320,320]{3,2,1,0:T(8,128)(2,1)S(1)}, bf16[3,3,320,320]{3,2,1,0:T(8,128)(2,1)}, u32[]{:S(2)}) %copy-start) | copy-done | bytes 1843224
  5.7 0.0 copy-start.5
  5.7 0.9 copy-done.5
  6.7 0.0 copy-start.8
  6.7 0.9 copy-done.8
  7.6 0.0 copy-start.9
  7.6 0.9 copy-done.9
  8.5 0.6 shard_map.136
  9.1 0.0 collective-permute-done.1.odd
  9.1 1.8 %shard_map.137 = (bf16[128,320]{1,0:T(8,128)(2,1)S(1)}, f32[64,128]{1,0:T(8,128)}) custom-call(f32[128,320]{1,0:T(8,128)S(1)} %get-tuple-element.17.partial, bf16[320,128]{1,0:T(8,128)(2,1)S(1)} %collective-permute-done.1.odd, bf16[3,320,320]{2,1,0:T(8,128)(2,1)S(1)} %get-tuple-element.18.odd_weight, bf16[320,320]{1,0:T(8,128)(2,1)S(1)} %get-tuple-element.19.zero_weight, ...), custom_call_target="tpu_custom_call" | custom-call | flops 104857600 | bytes 819200 | tf_op jit(solution)/shard_map/pallas_call | solution.py:37
  10.9 22.5 %all-to-all-start = ((f32[64,1,128]{2,1,0:T(1,128)}), f32[64,1,128]{2,1,0:T(1,128)S(1)}, u32[]{:S(2)}, u32[]{:S(2)}) async-start(f32[64,1,128]{2,1,0:T(1,128)} %bitcast.4), calls=%async_computation | async-start | bytes 65536 | tf_op jit(solution)/shard_map/all_to_all | solution.py:263
  33.4 0.0 copy-done.10
  33.5 0.0 copy-done.11
  33.5 12.3 %all-to-all-done = f32[64,1,128]{2,1,0:T(1,128)S(1)} async-done(((f32[64,1,128]{2,1,0:T(1,128)}), f32[64,1,128]{2,1,0:T(1,128)S(1)}, u32[]{:S(2)}, u32[]{:S(2)}) %all-to-all-start) | async-done | bytes 32800 | tf_op jit(solution)/shard_map/all_to_all | solution.py:263
  45.8 0.0 copy-done.1
  45.8 0.0 copy-done.2
  45.8 0.0 copy-done.3
  45.8 0.0 copy-done.4
  45.8 1.0 shard_map.138
  46.8 19.3 %all_to_all.21 = bf16[8,128,128]{2,1,0:T(8,128)(2,1)S(1)} all-to-all(bf16[8,128,128]{2,1,0:T(8,128)(2,1)S(1)} %get-tuple-element.23), channel_id=1, replica_groups=mesh['dp'=8,'x'=4,'z'=8,'c'=2] {'z'}, dimensions={0} | all-to-all | bytes 524288 | tf_op jit(solution)/shard_map/all_to_all | solution.py:271
  66.2 1.9 %collective-permute-start.5 = (bf16[8,48,128]{2,1,0:T(8,128)(2,1)S(1)}, bf16[8,48,128]{2,1,0:T(8,128)(2,1)S(1)}, u32[]{:S(2)}, u32[]{:S(2)}) collective-permute-start(bf16[8,48,128]{2,1,0:T(8,128)(2,1)S(1)} %slice.8.refs_0_), channel_id=1, source_target_pairs={{0,1},{1,0},{2,3},{3,2},{4,5},{5,4},{6,7},{7,6},{8,9},{9,8},{10,11... | collective-permute-start | bytes 294920 | tf_op jit(solution)/shard_map/ppermute | solution.py:276
  68.1 2.9 %collective-permute-start.4 = (bf16[8,80,128]{2,1,0:T(8,128)(2,1)S(1)}, bf16[8,80,128]{2,1,0:T(8,128)(2,1)S(1)}, u32[]{:S(2)}, u32[]{:S(2)}) collective-permute-start(bf16[8,80,128]{2,1,0:T(8,128)(2,1)S(1)} %slice.9.refs_2_), channel_id=1, source_target_pairs={{0,32},{16,48},{32,0},{48,16},{1,33},{17,49},{33,1},{49,17},{2,34}... | collective-permute-start | bytes 491528 | tf_op jit(solution)/shard_map/ppermute | solution.py:277
  71.1 4.2 %collective-permute-start.3 = (bf16[8,80,128]{2,1,0:T(8,128)(2,1)S(1)}, bf16[8,80,128]{2,1,0:T(8,128)(2,1)S(1)}, u32[]{:S(2)}, u32[]{:S(2)}) collective-permute-start(bf16[8,80,128]{2,1,0:T(8,128)(2,1)S(1)} %slice.9.refs_2_), channel_id=1, source_target_pairs={{0,48},{16,0},{32,16},{48,32},{1,49},{17,1},{33,17},{49,33},{2,50}... | collective-permute-start | bytes 491528 | tf_op jit(solution)/shard_map/ppermute | solution.py:277
  75.3 2.1 %collective-permute-start.2 = (bf16[8,80,128]{2,1,0:T(8,128)(2,1)S(1)}, bf16[8,80,128]{2,1,0:T(8,128)(2,1)S(1)}, u32[]{:S(2)}, u32[]{:S(2)}) collective-permute-start(bf16[8,80,128]{2,1,0:T(8,128)(2,1)S(1)} %slice.9.refs_2_), channel_id=1, source_target_pairs={{0,16},{16,32},{32,48},{48,0},{1,17},{17,33},{33,49},{49,1},{2,18}... | collective-permute-start | bytes 491528 | tf_op jit(solution)/shard_map/ppermute | solution.py:277
  77.4 0.0 collective-permute-done.5.refs_1_.refs_0_
  77.4 3.6 %shard_map.139 = (f32[1024,128]{1,0:T(8,128)S(1)}, f32[1024,128]{1,0:T(8,128)S(1)}, f32[1024,128]{1,0:T(8,128)S(1)}, f32[1024,128]{1,0:T(8,128)S(1)}) custom-call(bf16[8,48,128]{2,1,0:T(8,128)(2,1)S(1)} %slice.8.refs_0_, bf16[8,48,128]{2,1,0:T(8,128)(2,1)S(1)} %collective-permute-done.5.refs_1_.refs_0_, bf16[8,80,128]{2,1,0:T(8,128)(2,1)S(1)} %slice.9.refs_2_), custom_call_target="tpu_custom_call" | custom-call | flops 2147483648 | bytes 327680 | tf_op jit(solution)/shard_map/pallas_call | solution.py:37
  81.1 0.0 collective-permute-done.4.refs_3_
  81.1 0.0 collective-permute-done.3.refs_2_
  81.1 3.4 %collective-permute-done.2.refs_1_ = bf16[8,80,128]{2,1,0:T(8,128)(2,1)S(1)} collective-permute-done((bf16[8,80,128]{2,1,0:T(8,128)(2,1)S(1)}, bf16[8,80,128]{2,1,0:T(8,128)(2,1)S(1)}, u32[]{:S(2)}, u32[]{:S(2)}) %collective-permute-start.2) | collective-permute-done | bytes 163872 | tf_op jit(solution)/shard_map/ppermute | solution.py:277
  84.5 5.6 %shard_map.141 = f32[8,56,128]{2,1,0:T(8,128)S(1)} custom-call(bf16[8,48,128]{2,1,0:T(8,128)(2,1)S(1)} %collective-permute-done.5.refs_1_.refs_0_, bf16[8,80,128]{2,1,0:T(8,128)(2,1)S(1)} %collective-permute-done.2.refs_1_, bf16[8,80,128]{2,1,0:T(8,128)(2,1)S(1)} %collective-permute-done.3.refs_2_, bf16[8,80,128]{2,1,0:T(8,128)(2,1)S(1)} %collective-permute-done.4.refs_3_, ...), custom_call_target="tpu_custom_call" | custom-call | flops 3221225472 | bytes 491520 | tf_op jit(solution)/shard_map/pallas_call | solution.py:37
  90.0 2.2 %collective-permute-start.6 = (f32[8,56,128]{2,1,0:T(8,128)S(1)}, f32[8,56,128]{2,1,0:T(8,128)S(1)}, u32[]{:S(2)}, u32[]{:S(2)}) collective-permute-start(f32[8,56,128]{2,1,0:T(8,128)S(1)} %shard_map.141), channel_id=1, source_target_pairs={{0,1},{1,0},{2,3},{3,2},{4,5},{5,4},{6,7},{7,6},{8,9},{9,8},{10,11... | collective-permute-start | bytes 688136 | tf_op jit(solution)/shard_map/ppermute | solution.py:280
  92.2 0.0 copy-start.6
  92.2 0.0 copy-start.7
  92.2 5.6 %shard_map.140.mine = f32[8,56,128]{2,1,0:T(8,128)S(1)} custom-call(bf16[8,48,128]{2,1,0:T(8,128)(2,1)S(1)} %slice.8.refs_0_, bf16[8,80,128]{2,1,0:T(8,128)(2,1)S(1)} %collective-permute-done.2.refs_1_, bf16[8,80,128]{2,1,0:T(8,128)(2,1)S(1)} %collective-permute-done.3.refs_2_, bf16[8,80,128]{2,1,0:T(8,128)(2,1)S(1)} %collective-permute-done.4.refs_3_, ...), custom_call_target="tpu_custom_call" | custom-call | flops 3221225472 | bytes 491520 | tf_op jit(solution)/shard_map/pallas_call | solution.py:37
  97.8 0.0 collective-permute-done.6.theirs
  97.8 0.1 shard_map.142
  97.9 16.2 %all_to_all.22 = bf16[8,40,128]{2,1,0:T(8,128)(2,1)S(1)} all-to-all(bf16[8,40,128]{2,1,0:T(8,128)(2,1)S(1)} %shard_map.142), channel_id=1, replica_groups=mesh['dp'=8,'x'=4,'z'=8,'c'=2] {'z'}, dimensions={0} | all-to-all | bytes 163840 | tf_op jit(solution)/shard_map/all_to_all | solution.py:285
  114.1 0.0 copy-done.6
  114.1 0.0 copy-done.7
  114.1 1.1 shard_map.143
  (8 shorter events, 0.0 us)
Async XLA Ops:
  0.0 33.4 %copy-start.10 = (f32[320]{0:T(512)S(1)}, f32[320]{0:T(512)}, u32[]{:S(2)}) copy-start(f32[320]{0:T(512)} %param.20) | copy-start | bytes 3844
  0.0 33.5 %copy-start.11 = (f32[320]{0:T(512)S(1)}, f32[320]{0:T(512)}, u32[]{:S(2)}) copy-start(f32[320]{0:T(512)} %param.22) | copy-start | bytes 3844
  0.0 4.1 %collective-permute-start = (bf16[320,128]{1,0:T(8,128)(2,1)}, bf16[320,128]{1,0:T(8,128)(2,1)S(1)}, u32[]{:S(2)}, u32[]{:S(2)}) collective-permute-start(bf16[320,128]{1,0:T(8,128)(2,1)} %bitcast.12), channel_id=1, source_target_pairs={{0,1},{1,0},{2,3},{3,2},{4,5},{5,4},{6,7},{7,6},{8,9},{9,8},{10,11... | collective-permute-start | bytes 245768 | tf_op jit(solution)/shard_map/ppermute | solution.py:241
  2.1 7.0 %collective-permute-start.1 = (bf16[320,128]{1,0:T(8,128)(2,1)}, bf16[320,128]{1,0:T(8,128)(2,1)S(1)}, u32[]{:S(2)}, u32[]{:S(2)}) collective-permute-start(bf16[320,128]{1,0:T(8,128)(2,1)} %bitcast.13), channel_id=1, source_target_pairs={{1,2},{3,4},{5,6},{7,8},{9,10},{11,12},{13,14},{15,16},{17,18},{19... | collective-permute-start | bytes 245768 | tf_op jit(solution)/shard_map/ppermute | solution.py:240
  4.1 1.6 %copy-start = (bf16[3,3,320,320]{3,2,1,0:T(8,128)(2,1)S(1)}, bf16[3,3,320,320]{3,2,1,0:T(8,128)(2,1)}, u32[]{:S(2)}) copy-start(bf16[3,3,320,320]{3,2,1,0:T(8,128)(2,1)} %weight.1) | copy-start | bytes 5529604
  5.7 0.9 copy-start.5
  6.7 0.9 copy-start.8
  7.6 0.9 copy-start.9
  8.4 37.3 %copy-start.1 = (bf16[320,320]{1,0:T(8,128)(2,1)S(1)}, bf16[320,320]{1,0:T(8,128)(2,1)}, u32[]{:S(2)}) copy-start(bf16[320,320]{1,0:T(8,128)(2,1)} %proj_in.1) | copy-start | bytes 614404
  8.5 37.3 %copy-start.2 = (bf16[320,320]{1,0:T(8,128)(2,1)S(1)}, bf16[320,320]{1,0:T(8,128)(2,1)}, u32[]{:S(2)}) copy-start(bf16[320,320]{1,0:T(8,128)(2,1)} %wq.1) | copy-start | bytes 614404
  8.5 37.3 %copy-start.3 = (bf16[320,320]{1,0:T(8,128)(2,1)S(1)}, bf16[320,320]{1,0:T(8,128)(2,1)}, u32[]{:S(2)}) copy-start(bf16[320,320]{1,0:T(8,128)(2,1)} %wk.1) | copy-start | bytes 614404
  8.5 37.3 %copy-start.4 = (bf16[320,320]{1,0:T(8,128)(2,1)S(1)}, bf16[320,320]{1,0:T(8,128)(2,1)}, u32[]{:S(2)}) copy-start(bf16[320,320]{1,0:T(8,128)(2,1)} %wv.1) | copy-start | bytes 614404
  10.9 34.9 %all-to-all-start = ((f32[64,1,128]{2,1,0:T(1,128)}), f32[64,1,128]{2,1,0:T(1,128)S(1)}, u32[]{:S(2)}, u32[]{:S(2)}) async-start(f32[64,1,128]{2,1,0:T(1,128)} %bitcast.4), calls=%async_computation | async-start | bytes 65536 | tf_op jit(solution)/shard_map/all_to_all | solution.py:263
  66.2 11.2 %collective-permute-start.5 = (bf16[8,48,128]{2,1,0:T(8,128)(2,1)S(1)}, bf16[8,48,128]{2,1,0:T(8,128)(2,1)S(1)}, u32[]{:S(2)}, u32[]{:S(2)}) collective-permute-start(bf16[8,48,128]{2,1,0:T(8,128)(2,1)S(1)} %slice.8.refs_0_), channel_id=1, source_target_pairs={{0,1},{1,0},{2,3},{3,2},{4,5},{5,4},{6,7},{7,6},{8,9},{9,8},{10,11... | collective-permute-start | bytes 294920 | tf_op jit(solution)/shard_map/ppermute | solution.py:276
  68.1 12.9 %collective-permute-start.4 = (bf16[8,80,128]{2,1,0:T(8,128)(2,1)S(1)}, bf16[8,80,128]{2,1,0:T(8,128)(2,1)S(1)}, u32[]{:S(2)}, u32[]{:S(2)}) collective-permute-start(bf16[8,80,128]{2,1,0:T(8,128)(2,1)S(1)} %slice.9.refs_2_), channel_id=1, source_target_pairs={{0,32},{16,48},{32,0},{48,16},{1,33},{17,49},{33,1},{49,17},{2,34}... | collective-permute-start | bytes 491528 | tf_op jit(solution)/shard_map/ppermute | solution.py:277
  71.1 10.0 %collective-permute-start.3 = (bf16[8,80,128]{2,1,0:T(8,128)(2,1)S(1)}, bf16[8,80,128]{2,1,0:T(8,128)(2,1)S(1)}, u32[]{:S(2)}, u32[]{:S(2)}) collective-permute-start(bf16[8,80,128]{2,1,0:T(8,128)(2,1)S(1)} %slice.9.refs_2_), channel_id=1, source_target_pairs={{0,48},{16,0},{32,16},{48,32},{1,49},{17,1},{33,17},{49,33},{2,50}... | collective-permute-start | bytes 491528 | tf_op jit(solution)/shard_map/ppermute | solution.py:277
  75.3 9.1 %collective-permute-start.2 = (bf16[8,80,128]{2,1,0:T(8,128)(2,1)S(1)}, bf16[8,80,128]{2,1,0:T(8,128)(2,1)S(1)}, u32[]{:S(2)}, u32[]{:S(2)}) collective-permute-start(bf16[8,80,128]{2,1,0:T(8,128)(2,1)S(1)} %slice.9.refs_2_), channel_id=1, source_target_pairs={{0,16},{16,32},{32,48},{48,0},{1,17},{17,33},{33,49},{49,1},{2,18}... | collective-permute-start | bytes 491528 | tf_op jit(solution)/shard_map/ppermute | solution.py:277
  90.0 7.8 %collective-permute-start.6 = (f32[8,56,128]{2,1,0:T(8,128)S(1)}, f32[8,56,128]{2,1,0:T(8,128)S(1)}, u32[]{:S(2)}, u32[]{:S(2)}) collective-permute-start(f32[8,56,128]{2,1,0:T(8,128)S(1)} %shard_map.141), channel_id=1, source_target_pairs={{0,1},{1,0},{2,3},{3,2},{4,5},{5,4},{6,7},{7,6},{8,9},{9,8},{10,11... | collective-permute-start | bytes 688136 | tf_op jit(solution)/shard_map/ppermute | solution.py:280
  92.2 21.9 %copy-start.6 = (bf16[320,320]{1,0:T(8,128)(2,1)S(1)}, bf16[320,320]{1,0:T(8,128)(2,1)}, u32[]{:S(2)}) copy-start(bf16[320,320]{1,0:T(8,128)(2,1)} %attn_out.1) | copy-start | bytes 614404
  92.2 21.8 %copy-start.7 = (bf16[320,320]{1,0:T(8,128)(2,1)S(1)}, bf16[320,320]{1,0:T(8,128)(2,1)}, u32[]{:S(2)}) copy-start(bf16[320,320]{1,0:T(8,128)(2,1)} %proj_out.1) | copy-start | bytes 614404

commit v4 on v3

--- a/solution.py
+++ b/solution.py
@@ -21,6 +21,7 @@
 BF16 = jnp.bfloat16
 VMEM = pl.BlockSpec(memory_space=pltpu.VMEM)
 SMEM = pl.BlockSpec(memory_space=pltpu.SMEM)
+AWAY = pl.BlockSpec(memory_space=pltpu.HBM)
 MIB = 1024 * 1024
 
 
@@ -32,12 +33,12 @@
     return jnp.dot(a, b, precision=HIGHEST, preferred_element_type=F32)
 
 
-def call(body, out_shape, args, scratch=(), limit=24, flops=0, read=0, trans=0, smem=0):
+def call(body, out_shape, args, scratch=(), limit=24, flops=0, read=0, trans=0, smem=0, away=0):
     many = isinstance(out_shape, (list, tuple))
     return pl.pallas_call(
         body,
         out_shape=out_shape,
-        in_specs=[SMEM] * smem + [VMEM] * (len(args) - smem),
+        in_specs=[SMEM] * smem + [VMEM] * (len(args) - smem - away) + [AWAY] * away,
         out_specs=[VMEM] * len(out_shape) if many else VMEM,
         scratch_shapes=scratch,
         compiler_params=pltpu.CompilerParams(vmem_limit_bytes=limit * MIB),
@@ -78,12 +79,40 @@
     return total + dot(right, weight[at(2)])
 
 
-def own_row_body(core, hint, pair, weight, bias, features, zero_weight, partial, odd_weight, features_out, zero_out):
+def own_row_body(
+    core, pair, conv_bias, zero_bias, group_gain, norm_gain, hint, weight, features, zero_weight,
+    partial, odd_weight, features_out, zero_out, bias_out, group_out, norm_out,
+    hint_here, weight_here, features_here, sems,
+):
     pair_row = 2 - 2 * core[0]
-    partial[...] = taps(turned(hint), weight, 1) + taps(turned(pair), weight, pair_row) + bias[...]
-    odd_weight[...] = weight[2 - pair_row]
-    features_out[...] = turned(features)
-    zero_out[...] = zero_weight[...]
+    copies = [
+        pltpu.make_async_copy(source, target, sems.at[i])
+        for i, (source, target) in enumerate(
+            (
+                (hint, hint_here),
+                (weight.at[1], weight_here.at[0]),
+                (weight.at[pair_row], weight_here.at[1]),
+                (features, features_here),
+                (zero_weight, zero_out),
+                (weight.at[2 - pair_row], odd_weight),
+            )
+        )
+    ]
+    for copy in copies:
+        copy.start()
+    width = conv_bias.shape[0]
+    bias_out[...] = zero_bias[...].reshape(1, width)
+    group_out[...] = group_gain[...].reshape(1, width)
+    norm_out[...] = norm_gain[...].reshape(1, width)
+    copies[0].wait()
+    copies[1].wait()
+    total = taps(turned(hint_here), weight_here, 0) + conv_bias[...].reshape(1, width)
+    copies[2].wait()
+    partial[...] = total + taps(turned(pair), weight_here, 1)
+    copies[3].wait()
+    features_out[...] = turned(features_here)
+    copies[4].wait()
+    copies[5].wait()
 
 
 def merge_body(partial, odd, odd_weight, zero_weight, zero_bias, features, merged_out, stats_out):
@@ -133,78 +162,58 @@
         send[h] = block.astype(BF16)
 
 
-def attend_body(head_dim, q_rows, first, compact, n_queries, n_pieces, *refs):
+def attend_body(head_dim, first, n_queries, n_pieces, *refs):
     query_refs, refs = refs[:n_queries], refs[n_queries:]
     pieces, refs = refs[:n_pieces], refs[n_pieces:]
     if not first:
-        states, refs = refs[: 2 * n_queries], refs[2 * n_queries :]
-    blocks, depth, tokens = query_refs[0].shape
-    per_step = q_rows // tokens
-
-    for i in range(blocks // per_step):
-        rows = slice(i * q_rows, (i + 1) * q_rows)
-        for n, received in enumerate(query_refs):
-            queries = jnp.concatenate(
-                [received[i * per_step + j].astype(F32).T for j in range(per_step)], axis=0
-            ).astype(BF16)
-            if first:
-                acc = top = None
-            else:
-                acc, top = states[2 * n][rows, :], states[2 * n + 1][rows, :1]
-            for piece in pieces:
-                pair = jnp.concatenate([piece[b] for b in range(piece.shape[0])], axis=1)
-                scores = dot(queries, pair[:depth])
-                high = jnp.max(scores, axis=1, keepdims=True)
-                new_top = high if top is None else jnp.maximum(top, high)
-                probs = jnp.exp2(scores - new_top).astype(BF16)
-                ones = jnp.ones((128 - pair.shape[0], pair.shape[1]), BF16)
-                product = lax.dot_general(
-                    probs,
-                    jnp.concatenate([pair, ones], axis=0),
-                    (((1,), (1,)), ((), ())),
-                    preferred_element_type=F32,
-                )
-                acc = product if acc is None else acc * jnp.exp2(top - new_top) + product
-                top = new_top
-            if compact:
-                both = acc.T[head_dim : 2 * head_dim + 8]
-                tops = jnp.broadcast_to(top, (q_rows, 128)).T[:8]
-                for j in range(per_step):
-                    at = slice(j * tokens, (j + 1) * tokens)
-                    refs[n][i * per_step + j, : head_dim + 8] = both[:, at]
-                    refs[n][i * per_step + j, head_dim + 8 :] = tops[:, at]
-            else:
-                refs[2 * n][rows, :] = acc
-                refs[2 * n + 1][rows, :] = jnp.broadcast_to(top, (q_rows, 128))
-
-
-def attend(queries, pieces, states, compact, head_dim, q_rows=1024):
+        states, refs = refs[:n_queries], refs[n_queries:]
+    depth = query_refs[0].shape[1]
+    side_by_side = lambda ref: jnp.concatenate([ref[b] for b in range(ref.shape[0])], axis=1)
+    pairs = [side_by_side(piece) for piece in pieces]
+    keys = [pair[:depth].astype(F32).T.astype(BF16) for pair in pairs]
+    ones = jnp.ones((16, pairs[0].shape[1]), BF16)
+    summed = jnp.concatenate([jnp.concatenate([pair, ones], axis=0) for pair in pairs], axis=1)
+    rows = summed.shape[0] - head_dim
+    for n, query_ref in enumerate(query_refs):
+        queries = side_by_side(query_ref)
+        scores = [dot(k, queries) for k in keys]
+        top = functools.reduce(jnp.maximum, [jnp.max(s, axis=0, keepdims=True) for s in scores])
+        if not first:
+            before = states[n][rows : rows + 1, :]
+            top = jnp.maximum(top, before)
+        probs = jnp.concatenate([jnp.exp2(s - top).astype(BF16) for s in scores], axis=0)
+        total = dot(summed, probs)[head_dim:]
+        if not first:
+            total += states[n][:rows, :] * jnp.exp2(before - top)
+        refs[n][:rows, :] = total
+        refs[n][rows:, :] = jnp.broadcast_to(top, (8, top.shape[1]))
+
+
+def attend(queries, pieces, states, head_dim):
     blocks, _, tokens = queries[0].shape
-    rows = blocks * tokens
-    if compact:
-        out_shape = [jax.ShapeDtypeStruct((blocks, head_dim + 16, tokens), F32)] * len(queries)
-    else:
-        out_shape = [jax.ShapeDtypeStruct((rows, 128), F32)] * (2 * len(queries))
+    columns = blocks * tokens
     keys = sum(p.shape[0] * p.shape[2] for p in pieces) * len(queries)
     return call(
-        functools.partial(
-            attend_body, head_dim, q_rows, states is None, compact, len(queries), len(pieces)
-        ),
-        out_shape,
+        functools.partial(attend_body, head_dim, states is None, len(queries), len(pieces)),
+        [jax.ShapeDtypeStruct((head_dim + 24, columns), F32)] * len(queries),
         [*queries, *pieces, *(states or ())],
         limit=48,
-        flops=2 * rows * keys * 512,
+        flops=2 * columns * keys * 512,
         read=keys * 160,
-        trans=rows * keys,
+        trans=columns * keys,
     )
 
 
 def combine_body(head_dim, mine, theirs, out):
-    a, b = mine[...], theirs[...]
-    a_top, b_top = a[:, head_dim + 8 : head_dim + 9], b[:, head_dim + 8 : head_dim + 9]
+    blocks, _, tokens = out.shape
+    at = head_dim + 16
+    a_top, b_top = mine[at : at + 1], theirs[at : at + 1]
     top = jnp.maximum(a_top, b_top)
-    both = a[:, : head_dim + 8] * jnp.exp2(a_top - top) + b[:, : head_dim + 8] * jnp.exp2(b_top - top)
-    out[...] = (both[:, :head_dim] / both[:, head_dim : head_dim + 1]).astype(BF16)
+    a_part, b_part = jnp.exp2(a_top - top), jnp.exp2(b_top - top)
+    total = mine[head_dim : head_dim + 1] * a_part + theirs[head_dim : head_dim + 1] * b_part
+    result = (mine[:head_dim] * a_part + theirs[:head_dim] * b_part) / total
+    for b in range(blocks):
+        out[b] = result[:, b * tokens : (b + 1) * tokens].astype(BF16)
 
 
 def finish_body(attended, inner, merged, attn_out, proj_out, out):
@@ -239,24 +248,35 @@
     ends = [(i, i + 1) for i in range(1, everyone - 1, 2)]
     odd = lax.ppermute(hint, SEQ, ends + [(b, a) for a, b in ends])
     pair = lax.ppermute(hint, "c", swap)
-    row = lambda v: v.reshape(1, channels)
-    partial, odd_weight, features, zero_weight = call(
+    line = shape((1, channels), F32)
+    partial, odd_weight, features, zero_weight, zero_bias, group_gain, norm_gain = call(
         own_row_body,
         [
             shape((tokens, channels), F32),
             shape(conv_weight.shape[1:], BF16),
             shape((tokens, channels), F32),
             shape(zero_weight.shape, BF16),
+            line,
+            line,
+            line,
         ],
-        (core, hint, pair, conv_weight, row(conv_bias), features, zero_weight),
+        (core, pair, conv_bias, zero_bias, group_gain, norm_gain, hint, conv_weight, features, zero_weight),
+        scratch=[
+            pltpu.VMEM(hint.shape, BF16),
+            pltpu.VMEM((2, *conv_weight.shape[1:]), BF16),
+            pltpu.VMEM(features.shape, BF16),
+            pltpu.SemaphoreType.DMA((6,)),
+        ],
         smem=1,
+        away=4,
+        limit=53,
         flops=2 * tokens * channels * channels * 6,
         read=10 * channels * channels * 2,
     )
     merged, stats = call(
         merge_body,
         [shape((tokens, channels), BF16), shape((everyone, 128), F32)],
-        (partial, odd, odd_weight, zero_weight, row(zero_bias), features),
+        (partial, odd, odd_weight, zero_weight, zero_bias, features),
         flops=2 * tokens * channels * channels * 4,
         read=4 * channels * channels * 2,
     )
@@ -264,7 +284,7 @@
     inner, send = call(
         project_body,
         [shape((tokens, channels), BF16), shape((HEADS, 128, tokens), BF16)],
-        (stats, merged, row(group_gain), proj_in, row(norm_gain), query_weight, key_weight, value_weight),
+        (stats, merged, group_gain, proj_in, norm_gain, query_weight, key_weight, value_weight),
         flops=2 * tokens * channels * channels * 4,
         read=4 * channels * channels * 2,
     )
@@ -273,12 +293,12 @@
     queries, pair = received[:, :depth, :], received[:, depth:, :]
     chips = lax.axis_size("x")
     ring = lambda by: [(i, (i + by) % chips) for i in range(chips)]
+    pieces = [lax.ppermute(pair, "x", ring(by)) for by in (chips - 1, 2, 1)]
     others = lax.ppermute(queries, "c", swap)
-    pieces = [lax.ppermute(pair, "x", ring(by)) for by in (1, chips - 1, 2)]
-    states = attend([queries, others], [pair], None, False, head_dim)
-    (theirs,) = attend([others], pieces, states[2:], True, head_dim)
+    states = attend([queries, others], [pair], None, head_dim)
+    (theirs,) = attend([others], pieces, states[1:], head_dim)
     back = lax.ppermute(theirs, "c", swap)
-    (mine,) = attend([queries], pieces, states[:2], True, head_dim)
+    (mine,) = attend([queries], pieces, states[:1], head_dim)
     result = call(
         functools.partial(combine_body, head_dim), shape((HEADS, head_dim, tokens), BF16), (mine, back)
     )

time: 116 us -> 113 us (0.974)
  blocking collectives: 35.5 us -> 68.3 us
  starting transfers between devices: 38.6 us -> 16.1 us
  waiting for transfers between devices: 15.7 us -> 4.17 us
  Pallas kernels: 19.4 us -> 18.2 us
    all_to_all x0 -> x1, blocking collectives: none -> 32.8 us  [local(): stats = lax.all_to_all(stats, SEQ, 0, 0, tiled=True)]
    all_to_all x1 -> x0, starting transfers between devices: 22.5 us -> none  [local(): stats = lax.all_to_all(stats, SEQ, 0, 0, tiled=True)]
    all_to_all x1 -> x0, waiting for transfers between devices: 12.3 us -> none  [local(): stats = lax.all_to_all(stats, SEQ, 0, 0, tiled=True)]
    reshape x4 -> x0, local copies, waits for them, and re-layouts: 1.37 us -> none  [local(): row = lambda v: v.reshape(1, channels)]
    unnamed x24 -> x26, local copies, waits for them, and re-layouts: 4.38 us -> 5.63 us
    pallas_call x8, Pallas kernels: 19.4 us -> 18.2 us  [call(): pl.pallas_call(body, out_shape=out_shape, in_specs=[SMEM] * smem + [VMEM]...]
  transfers between devices with their start and end apart: 8 -> 7, of which waited for: 2 -> 3; matrix products, arithmetic and copies ran while one was open for 1% -> 0% of each run, Pallas kernels for 9% -> 9%
where the time goes in v4:
time: 113 us
  blocking collectives  68.3 us (60%)
  Pallas kernels  18.2 us (16%)
  starting transfers between devices  16.1 us (14%)
  local copies, waits for them, and re-layouts  5.66 us (5%)
  waiting for transfers between devices  4.17 us (4%)
    all_to_all x1, blocking collectives, local(): stats = lax.all_to_all(stats, SEQ, 0, 0, tiled=True)  32.8 us
    all_to_all x1, blocking collectives, local(): received = lax.all_to_all(send, 'z', 0, 0, tiled=True)  19.3 us
    pallas_call x8, Pallas kernels, call(): pl.pallas_call(body, out_shape=out_shape, in_specs=[SMEM] * smem + [VMEM]...  18.2 us
    all_to_all x1, blocking collectives, local(): lax.all_to_all(result, 'z', 0, 0, tiled=True).reshape(channels, tokens)  16.2 us
    ppermute x3, starting transfers between devices, local(): pieces = [lax.ppermute(pair, 'x', ring(by)) for by in (chips - 1, 2, 1)]  9.36 us
    unnamed x26, local copies, waits for them, and re-layouts  5.63 us
    ppermute x3, waiting for transfers between devices, local(): pieces = [lax.ppermute(pair, 'x', ring(by)) for by in (chips - 1, 2, 1)]  3.38 us
  transfers between devices with their start and end apart: 7, of which 3 were waited for; matrix products, arithmetic and copies ran while one was open for 0% of the time, Pallas kernels for 9%

profile of v4, /device:TPU:24, one launch (start us, length us, event | category | flops | bytes accessed | tf_op | source)
XLA Modules:
  0.0 112.6 jit_solution(14074069071426682819)
XLA Ops:
  0.0 0.0 copy-start.4
  0.0 0.0 copy-start.3
  0.0 0.0 copy-start.2
  0.0 0.0 copy-start.1
  0.0 2.1 %collective-permute-start = (bf16[320,128]{1,0:T(8,128)(2,1)}, bf16[320,128]{1,0:T(8,128)(2,1)S(1)}, u32[]{:S(2)}, u32[]{:S(2)}) collective-permute-start(bf16[320,128]{1,0:T(8,128)(2,1)} %bitcast.12), channel_id=1, source_target_pairs={{0,1},{1,0},{2,3},{3,2},{4,5},{5,4},{6,7},{7,6},{8,9},{9,8},{10,11... | collective-permute-start | bytes 245768 | tf_op jit(solution)/shard_map/ppermute | solution.py:250
  2.1 0.7 collective-permute-start.1
  2.8 0.8 collective-permute-done.pair
  3.5 0.0 copy-start.7
  3.5 0.9 copy-done.7
  4.4 0.0 copy-start.8
  4.4 0.9 copy-done.8
  5.3 0.0 copy-start.9
  5.3 0.7 copy-done.9
  6.0 0.0 copy-start.10
  6.0 0.7 copy-done.10
  6.7 0.7 copy-done.11
  7.4 0.7 copy-done.12
  8.0 3.0 %shard_map.136 = (f32[128,320]{1,0:T(8,128)S(1)}, bf16[3,320,320]{2,1,0:T(8,128)(2,1)}, f32[128,320]{1,0:T(8,128)S(1)}, bf16[320,320]{1,0:T(8,128)(2,1)S(1)}, f3...) custom-call(s32[1]{0:T(128)} %bitcast.core, bf16[320,128]{1,0:T(8,128)(2,1)S(1)} %collective-permute-done.pair, ...), custom_call_target="tpu_custom_call" | custom-call | flops 157286400 | bytes 2048000 | tf_op jit(solution)/shard_map/pallas_call | solution.py:38
  11.1 0.0 collective-permute-done.1.odd
  11.1 0.0 copy-start
  11.1 1.1 copy-done
  12.2 1.2 %shard_map.137 = (bf16[128,320]{1,0:T(8,128)(2,1)S(1)}, f32[64,128]{1,0:T(8,128)S(1)}) custom-call(f32[128,320]{1,0:T(8,128)S(1)} %get-tuple-element.18.partial, bf16[320,128]{1,0:T(8,128)(2,1)S(1)} %collective-permute-done.1.odd, bf16[3,320,320]{2,1,0:T(8,128)(2,1)S(1)} %copy-done, bf16[320,320]{1,0:T(8,128)(2,1)S(1)} %get-tuple-element.20.zero_weight, ...), custom_call_target="tpu_custom_call" | custom-call | flops 104857600 | bytes 819200 | tf_op jit(solution)/shard_map/pallas_call | solution.py:38
  13.3 32.8 %all_to_all.21 = f32[64,1,128]{2,1,0:T(1,128)S(1)} all-to-all(f32[64,1,128]{2,1,0:T(1,128)S(1)} %bitcast.15), channel_id=1, replica_groups=mesh['dp'=8,'x'=4,'z'=8,'c'=2] {'x','z','c'}, dimensions={0} | all-to-all | bytes 65536 | tf_op jit(solution)/shard_map/all_to_all | solution.py:283
  46.2 0.0 copy-done.4
  46.2 0.0 copy-done.3
  46.2 0.0 copy-done.2
  46.2 0.0 copy-done.1
  46.2 1.0 shard_map.138
  47.2 19.3 %all_to_all.22 = bf16[8,128,128]{2,1,0:T(8,128)(2,1)S(1)} all-to-all(bf16[8,128,128]{2,1,0:T(8,128)(2,1)S(1)} %get-tuple-element.27), channel_id=1, replica_groups=mesh['dp'=8,'x'=4,'z'=8,'c'=2] {'z'}, dimensions={0} | all-to-all | bytes 524288 | tf_op jit(solution)/shard_map/all_to_all | solution.py:291
  66.6 1.9 %collective-permute-start.5 = (bf16[8,48,128]{2,1,0:T(8,128)(2,1)S(1)}, bf16[8,48,128]{2,1,0:T(8,128)(2,1)S(1)}, u32[]{:S(2)}, u32[]{:S(2)}) collective-permute-start(bf16[8,48,128]{2,1,0:T(8,128)(2,1)S(1)} %slice.8.refs_0_), channel_id=1, source_target_pairs={{0,1},{1,0},{2,3},{3,2},{4,5},{5,4},{6,7},{7,6},{8,9},{9,8},{10,11... | collective-permute-start | bytes 294920 | tf_op jit(solution)/shard_map/ppermute | solution.py:297
  68.5 2.6 %collective-permute-start.4 = (bf16[8,80,128]{2,1,0:T(8,128)(2,1)S(1)}, bf16[8,80,128]{2,1,0:T(8,128)(2,1)S(1)}, u32[]{:S(2)}, u32[]{:S(2)}) collective-permute-start(bf16[8,80,128]{2,1,0:T(8,128)(2,1)S(1)} %slice.9.refs_2_), channel_id=1, source_target_pairs={{0,16},{16,32},{32,48},{48,0},{1,17},{17,33},{33,49},{49,1},{2,18}... | collective-permute-start | bytes 491528 | tf_op jit(solution)/shard_map/ppermute | solution.py:296
  71.1 3.8 %collective-permute-start.3 = (bf16[8,80,128]{2,1,0:T(8,128)(2,1)S(1)}, bf16[8,80,128]{2,1,0:T(8,128)(2,1)S(1)}, u32[]{:S(2)}, u32[]{:S(2)}) collective-permute-start(bf16[8,80,128]{2,1,0:T(8,128)(2,1)S(1)} %slice.9.refs_2_), channel_id=1, source_target_pairs={{0,32},{16,48},{32,0},{48,16},{1,33},{17,49},{33,1},{49,17},{2,34}... | collective-permute-start | bytes 491528 | tf_op jit(solution)/shard_map/ppermute | solution.py:296
  74.9 3.0 %collective-permute-start.2 = (bf16[8,80,128]{2,1,0:T(8,128)(2,1)S(1)}, bf16[8,80,128]{2,1,0:T(8,128)(2,1)S(1)}, u32[]{:S(2)}, u32[]{:S(2)}) collective-permute-start(bf16[8,80,128]{2,1,0:T(8,128)(2,1)S(1)} %slice.9.refs_2_), channel_id=1, source_target_pairs={{0,48},{16,0},{32,16},{48,32},{1,49},{17,1},{33,17},{49,33},{2,50}... | collective-permute-start | bytes 491528 | tf_op jit(solution)/shard_map/ppermute | solution.py:296
  77.9 0.0 collective-permute-done.5.refs_1_.refs_0_
  77.9 2.9 %shard_map.139 = (f32[64,1024]{1,0:T(8,128)S(1)}, f32[64,1024]{1,0:T(8,128)S(1)}) custom-call(bf16[8,48,128]{2,1,0:T(8,128)(2,1)S(1)} %slice.8.refs_0_, bf16[8,48,128]{2,1,0:T(8,128)(2,1)S(1)} %collective-permute-done.5.refs_1_.refs_0_, bf16[8,80,128]{2,1,0:T(8,128)(2,1)S(1)} %slice.9.refs_2_), custom_call_target="tpu_custom_call" | custom-call | flops 2147483648 | bytes 327680 | tf_op jit(solution)/shard_map/pallas_call | solution.py:38
  80.8 0.9 collective-permute-done.4.refs_3_
  81.7 0.0 collective-permute-done.3.refs_2_
  81.7 2.5 %collective-permute-done.2.refs_1_ = bf16[8,80,128]{2,1,0:T(8,128)(2,1)S(1)} collective-permute-done((bf16[8,80,128]{2,1,0:T(8,128)(2,1)S(1)}, bf16[8,80,128]{2,1,0:T(8,128)(2,1)S(1)}, u32[]{:S(2)}, u32[]{:S(2)}) %collective-permute-start.2) | collective-permute-done | bytes 163872 | tf_op jit(solution)/shard_map/ppermute | solution.py:296
  84.2 4.4 %shard_map.141 = f32[64,1024]{1,0:T(8,128)S(1)} custom-call(bf16[8,48,128]{2,1,0:T(8,128)(2,1)S(1)} %collective-permute-done.5.refs_1_.refs_0_, bf16[8,80,128]{2,1,0:T(8,128)(2,1)S(1)} %collective-permute-done.2.refs_1_, bf16[8,80,128]{2,1,0:T(8,128)(2,1)S(1)} %collective-permute-done.3.refs_2_, bf16[8,80,128]{2,1,0:T(8,128)(2,1)S(1)} %collective-permute-done.4.refs_3_, ...), custom_call_target="tpu_custom_call" | custom-call | flops 3221225472 | bytes 491520 | tf_op jit(solution)/shard_map/pallas_call | solution.py:38
  88.7 2.1 %collective-permute-start.6 = (f32[64,1024]{1,0:T(8,128)S(1)}, f32[64,1024]{1,0:T(8,128)S(1)}, u32[]{:S(2)}, u32[]{:S(2)}) collective-permute-start(f32[64,1024]{1,0:T(8,128)S(1)} %shard_map.141), channel_id=1, source_target_pairs={{0,1},{1,0},{2,3},{3,2},{4,5},{5,4},{6,7},{7,6},{8,9},{9,8},{10,11... | collective-permute-start | bytes 786440 | tf_op jit(solution)/shard_map/ppermute | solution.py:300
  90.8 0.0 copy-start.5
  90.8 0.0 copy-start.6
  90.8 4.4 %shard_map.140.mine = f32[64,1024]{1,0:T(8,128)S(1)} custom-call(bf16[8,48,128]{2,1,0:T(8,128)(2,1)S(1)} %slice.8.refs_0_, bf16[8,80,128]{2,1,0:T(8,128)(2,1)S(1)} %collective-permute-done.2.refs_1_, bf16[8,80,128]{2,1,0:T(8,128)(2,1)S(1)} %collective-permute-done.3.refs_2_, bf16[8,80,128]{2,1,0:T(8,128)(2,1)S(1)} %collective-permute-done.4.refs_3_, ...), custom_call_target="tpu_custom_call" | custom-call | flops 3221225472 | bytes 491520 | tf_op jit(solution)/shard_map/pallas_call | solution.py:38
  95.2 0.0 collective-permute-done.6.theirs
  95.3 16.2 %all_to_all.23 = bf16[8,40,128]{2,1,0:T(8,128)(2,1)S(1)} all-to-all(bf16[8,40,128]{2,1,0:T(8,128)(2,1)S(1)} %shard_map.142), channel_id=1, replica_groups=mesh['dp'=8,'x'=4,'z'=8,'c'=2] {'z'}, dimensions={0} | all-to-all | bytes 163840 | tf_op jit(solution)/shard_map/all_to_all | solution.py:305
  111.4 0.0 copy-done.5
  111.4 0.0 copy-done.6
  111.4 1.1 %shard_map.143 = bf16[320,128]{1,0:T(8,128)(2,1)} custom-call(bf16[320,128]{1,0:T(8,128)(2,1)S(1)} %bitcast.9, bf16[128,320]{1,0:T(8,128)(2,1)S(1)} %get-tuple-element.30.inner, bf16[128,320]{1,0:T(8,128)(2,1)S(1)} %get-tuple-element.24.merged, bf16[320,320]{1,0:T(8,128)(2,1)S(1)} %copy-done.5, bf16[320,320]{1,0:T(8,128)(2,1)S(1)} %copy-done.6), custom_call_target="tpu_custom_call" | custom-call | flops 52428800 | bytes 409600 | tf_op jit(solution)/shard_map/pallas_call | solution.py:38
  (5 shorter events, 0.1 us)
Async XLA Ops:
  0.0 46.2 %copy-start.4 = (bf16[320,320]{1,0:T(8,128)(2,1)S(1)}, bf16[320,320]{1,0:T(8,128)(2,1)}, u32[]{:S(2)}) copy-start(bf16[320,320]{1,0:T(8,128)(2,1)} %wv.1) | copy-start | bytes 614404
  0.0 46.2 %copy-start.3 = (bf16[320,320]{1,0:T(8,128)(2,1)S(1)}, bf16[320,320]{1,0:T(8,128)(2,1)}, u32[]{:S(2)}) copy-start(bf16[320,320]{1,0:T(8,128)(2,1)} %wk.1) | copy-start | bytes 614404
  0.0 46.2 %copy-start.2 = (bf16[320,320]{1,0:T(8,128)(2,1)S(1)}, bf16[320,320]{1,0:T(8,128)(2,1)}, u32[]{:S(2)}) copy-start(bf16[320,320]{1,0:T(8,128)(2,1)} %wq.1) | copy-start | bytes 614404
  0.0 46.2 %copy-start.1 = (bf16[320,320]{1,0:T(8,128)(2,1)S(1)}, bf16[320,320]{1,0:T(8,128)(2,1)}, u32[]{:S(2)}) copy-start(bf16[320,320]{1,0:T(8,128)(2,1)} %proj_in.1) | copy-start | bytes 614404
  0.0 3.5 %collective-permute-start = (bf16[320,128]{1,0:T(8,128)(2,1)}, bf16[320,128]{1,0:T(8,128)(2,1)S(1)}, u32[]{:S(2)}, u32[]{:S(2)}) collective-permute-start(bf16[320,128]{1,0:T(8,128)(2,1)} %bitcast.12), channel_id=1, source_target_pairs={{0,1},{1,0},{2,3},{3,2},{4,5},{5,4},{6,7},{7,6},{8,9},{9,8},{10,11... | collective-permute-start | bytes 245768 | tf_op jit(solution)/shard_map/ppermute | solution.py:250
  2.1 9.0 %collective-permute-start.1 = (bf16[320,128]{1,0:T(8,128)(2,1)}, bf16[320,128]{1,0:T(8,128)(2,1)S(1)}, u32[]{:S(2)}, u32[]{:S(2)}) collective-permute-start(bf16[320,128]{1,0:T(8,128)(2,1)} %bitcast.13), channel_id=1, source_target_pairs={{1,2},{3,4},{5,6},{7,8},{9,10},{11,12},{13,14},{15,16},{17,18},{19... | collective-permute-start | bytes 245768 | tf_op jit(solution)/shard_map/ppermute | solution.py:249
  3.5 0.9 copy-start.7
  4.4 0.9 copy-start.8
  5.3 0.7 copy-start.9
  6.0 0.7 copy-start.10
  6.7 0.7 copy-start.11
  7.4 0.7 copy-start.12
  11.1 1.1 copy-start
  66.6 11.3 %collective-permute-start.5 = (bf16[8,48,128]{2,1,0:T(8,128)(2,1)S(1)}, bf16[8,48,128]{2,1,0:T(8,128)(2,1)S(1)}, u32[]{:S(2)}, u32[]{:S(2)}) collective-permute-start(bf16[8,48,128]{2,1,0:T(8,128)(2,1)S(1)} %slice.8.refs_0_), channel_id=1, source_target_pairs={{0,1},{1,0},{2,3},{3,2},{4,5},{5,4},{6,7},{7,6},{8,9},{9,8},{10,11... | collective-permute-start | bytes 294920 | tf_op jit(solution)/shard_map/ppermute | solution.py:297
  68.5 13.2 %collective-permute-start.4 = (bf16[8,80,128]{2,1,0:T(8,128)(2,1)S(1)}, bf16[8,80,128]{2,1,0:T(8,128)(2,1)S(1)}, u32[]{:S(2)}, u32[]{:S(2)}) collective-permute-start(bf16[8,80,128]{2,1,0:T(8,128)(2,1)S(1)} %slice.9.refs_2_), channel_id=1, source_target_pairs={{0,16},{16,32},{32,48},{48,0},{1,17},{17,33},{33,49},{49,1},{2,18}... | collective-permute-start | bytes 491528 | tf_op jit(solution)/shard_map/ppermute | solution.py:296
  71.1 10.6 %collective-permute-start.3 = (bf16[8,80,128]{2,1,0:T(8,128)(2,1)S(1)}, bf16[8,80,128]{2,1,0:T(8,128)(2,1)S(1)}, u32[]{:S(2)}, u32[]{:S(2)}) collective-permute-start(bf16[8,80,128]{2,1,0:T(8,128)(2,1)S(1)} %slice.9.refs_2_), channel_id=1, source_target_pairs={{0,32},{16,48},{32,0},{48,16},{1,33},{17,49},{33,1},{49,17},{2,34}... | collective-permute-start | bytes 491528 | tf_op jit(solution)/shard_map/ppermute | solution.py:296
  74.9 9.4 %collective-permute-start.2 = (bf16[8,80,128]{2,1,0:T(8,128)(2,1)S(1)}, bf16[8,80,128]{2,1,0:T(8,128)(2,1)S(1)}, u32[]{:S(2)}, u32[]{:S(2)}) collective-permute-start(bf16[8,80,128]{2,1,0:T(8,128)(2,1)S(1)} %slice.9.refs_2_), channel_id=1, source_target_pairs={{0,48},{16,0},{32,16},{48,32},{1,49},{17,1},{33,17},{49,33},{2,50}... | collective-permute-start | bytes 491528 | tf_op jit(solution)/shard_map/ppermute | solution.py:296
  88.7 6.6 %collective-permute-start.6 = (f32[64,1024]{1,0:T(8,128)S(1)}, f32[64,1024]{1,0:T(8,128)S(1)}, u32[]{:S(2)}, u32[]{:S(2)}) collective-permute-start(f32[64,1024]{1,0:T(8,128)S(1)} %shard_map.141), channel_id=1, source_target_pairs={{0,1},{1,0},{2,3},{3,2},{4,5},{5,4},{6,7},{7,6},{8,9},{9,8},{10,11... | collective-permute-start | bytes 786440 | tf_op jit(solution)/shard_map/ppermute | solution.py:300
  90.8 20.7 %copy-start.5 = (bf16[320,320]{1,0:T(8,128)(2,1)S(1)}, bf16[320,320]{1,0:T(8,128)(2,1)}, u32[]{:S(2)}) copy-start(bf16[320,320]{1,0:T(8,128)(2,1)} %attn_out.1) | copy-start | bytes 614404
  90.8 20.7 %copy-start.6 = (bf16[320,320]{1,0:T(8,128)(2,1)S(1)}, bf16[320,320]{1,0:T(8,128)(2,1)}, u32[]{:S(2)}) copy-start(bf16[320,320]{1,0:T(8,128)(2,1)} %proj_out.1) | copy-start | bytes 614404

commit v5 on v4

--- a/solution.py
+++ b/solution.py
@@ -21,7 +21,6 @@
 BF16 = jnp.bfloat16
 VMEM = pl.BlockSpec(memory_space=pltpu.VMEM)
 SMEM = pl.BlockSpec(memory_space=pltpu.SMEM)
-AWAY = pl.BlockSpec(memory_space=pltpu.HBM)
 MIB = 1024 * 1024
 
 
@@ -33,12 +32,12 @@
     return jnp.dot(a, b, precision=HIGHEST, preferred_element_type=F32)
 
 
-def call(body, out_shape, args, scratch=(), limit=24, flops=0, read=0, trans=0, smem=0, away=0):
+def call(body, out_shape, args, scratch=(), limit=24, flops=0, read=0, trans=0, smem=0):
     many = isinstance(out_shape, (list, tuple))
     return pl.pallas_call(
         body,
         out_shape=out_shape,
-        in_specs=[SMEM] * smem + [VMEM] * (len(args) - smem - away) + [AWAY] * away,
+        in_specs=[SMEM] * smem + [VMEM] * (len(args) - smem),
         out_specs=[VMEM] * len(out_shape) if many else VMEM,
         scratch_shapes=scratch,
         compiler_params=pltpu.CompilerParams(vmem_limit_bytes=limit * MIB),
@@ -66,6 +65,14 @@
 
 def turned(ref):
     return ref[...].astype(F32).T
+
+
+def masks_body(_, gather_low, gather_high, spread_low, spread_high):
+    channels, lanes = gather_low.shape
+    gather_low[...] = group_gather(channels, lanes, 0)
+    gather_high[...] = group_gather(channels, lanes, GROUPS)
+    spread_low[...] = group_spread(channels, lanes, 0)
+    spread_high[...] = group_spread(channels, lanes, GROUPS)
 
 
 def taps(wide, weight, index):
@@ -79,86 +86,59 @@
     return total + dot(right, weight[at(2)])
 
 
-def own_row_body(
-    core, pair, conv_bias, zero_bias, group_gain, norm_gain, hint, weight, features, zero_weight,
-    partial, odd_weight, features_out, zero_out, bias_out, group_out, norm_out,
-    hint_here, weight_here, features_here, sems,
+def own_row_body(core, hint, pair, weight, bias, features, mask, partial, odd_weight, features_out):
+    pair_row = 2 - 2 * core[0]
+    partial[...] = (
+        taps(turned(hint), weight, 1)
+        + taps(turned(pair), weight, pair_row)
+        + bias[...].reshape(1, partial.shape[1])
+    )
+    odd_weight[...] = weight[2 - pair_row]
+    features_out[...] = turned(features)
+
+
+def merge_body(
+    partial, odd, odd_weight, zero_weight, zero_bias, features, gather_low, gather_high, spread_low, merged_out, stats_out
 ):
-    pair_row = 2 - 2 * core[0]
-    copies = [
-        pltpu.make_async_copy(source, target, sems.at[i])
-        for i, (source, target) in enumerate(
-            (
-                (hint, hint_here),
-                (weight.at[1], weight_here.at[0]),
-                (weight.at[pair_row], weight_here.at[1]),
-                (features, features_here),
-                (zero_weight, zero_out),
-                (weight.at[2 - pair_row], odd_weight),
-            )
-        )
-    ]
-    for copy in copies:
-        copy.start()
-    width = conv_bias.shape[0]
-    bias_out[...] = zero_bias[...].reshape(1, width)
-    group_out[...] = group_gain[...].reshape(1, width)
-    norm_out[...] = norm_gain[...].reshape(1, width)
-    copies[0].wait()
-    copies[1].wait()
-    total = taps(turned(hint_here), weight_here, 0) + conv_bias[...].reshape(1, width)
-    copies[2].wait()
-    partial[...] = total + taps(turned(pair), weight_here, 1)
-    copies[3].wait()
-    features_out[...] = turned(features_here)
-    copies[4].wait()
-    copies[5].wait()
-
-
-def merge_body(partial, odd, odd_weight, zero_weight, zero_bias, features, merged_out, stats_out):
     conv = partial[...] + taps(turned(odd), odd_weight, None)
     control = (conv / (1.0 + jnp.exp(-conv))).astype(BF16)
-    branch = dot(control, zero_weight[...]) + zero_bias[...]
+    branch = dot(control, zero_weight[...]) + zero_bias[...].reshape(1, partial.shape[1])
     merged = (features[...] + branch).astype(BF16)
     merged_out[...] = merged
     wide = merged.astype(F32)
     tokens, channels = wide.shape
-    lanes = stats_out.shape[1]
     entries = tokens * (channels // GROUPS)
-    mean = exact_dot(jnp.sum(wide, axis=0, keepdims=True), group_gather(channels, lanes, 0)) / entries
-    centred = wide - exact_dot(mean, group_spread(channels, lanes, 0))
-    square = exact_dot(
-        jnp.sum(centred * centred, axis=0, keepdims=True), group_gather(channels, lanes, GROUPS)
-    )
+    mean = exact_dot(jnp.sum(wide, axis=0, keepdims=True), gather_low[...]) / entries
+    centred = wide - exact_dot(mean, spread_low[...])
+    square = exact_dot(jnp.sum(centred * centred, axis=0, keepdims=True), gather_high[...])
     stats_out[...] = jnp.broadcast_to(mean + square / entries, stats_out.shape)
 
 
-def project_body(stats, merged, group_gain, proj_in, norm_gain, wq, wk, wv, inner_out, send):
+def project_body(
+    stats, merged, group_gain, proj_in, norm_gain, wq, wk, wv, spread_low, spread_high, inner_out, send
+):
     channels = merged.shape[1]
-    lanes = stats.shape[1]
     head_dim = channels // HEADS
     everyone = stats[...]
     average = jnp.mean(everyone, axis=0, keepdims=True)
     between = jnp.mean(jnp.square(everyone - average), axis=0, keepdims=True)
-    spread = group_spread(channels, lanes, 0)
-    mean = exact_dot(average, spread)
-    variance = exact_dot(average, group_spread(channels, lanes, GROUPS)) + exact_dot(between, spread)
+    mean = exact_dot(average, spread_low[...])
+    variance = exact_dot(average, spread_high[...]) + exact_dot(between, spread_low[...])
     factor = lax.rsqrt(variance + NORM_EPS)
-    grouped = ((merged[...].astype(F32) - mean) * factor * group_gain[...]).astype(BF16)
+    grouped = ((merged[...].astype(F32) - mean) * factor * group_gain[...].reshape(1, channels)).astype(BF16)
     inner = dot(grouped, proj_in[...]).astype(BF16)
     inner_out[...] = inner
     wide = inner.astype(F32)
     centred = wide - jnp.mean(wide, axis=1, keepdims=True)
     variance = jnp.mean(centred * centred, axis=1, keepdims=True)
-    normed = (centred * lax.rsqrt(variance + LAYER_EPS) * norm_gain[...]).astype(BF16)
+    normed = (centred * lax.rsqrt(variance + LAYER_EPS) * norm_gain[...].reshape(1, channels)).astype(BF16)
     scale = math.log2(math.e) / math.sqrt(head_dim)
     queries = (dot(normed, wq[...]) * scale).T
     keys = dot(normed, wk[...]).T
     values = dot(normed, wv[...]).T
-    gap = jnp.zeros((send.shape[1] - 3 * head_dim, queries.shape[1]), F32)
     for h in range(HEADS):
         rows = slice(h * head_dim, (h + 1) * head_dim)
-        block = jnp.concatenate([queries[rows], gap, keys[rows], values[rows]], axis=0)
+        block = jnp.concatenate([queries[rows], keys[rows], values[rows]], axis=0)
         send[h] = block.astype(BF16)
 
 
@@ -167,7 +147,7 @@
     pieces, refs = refs[:n_pieces], refs[n_pieces:]
     if not first:
         states, refs = refs[:n_queries], refs[n_queries:]
-    depth = query_refs[0].shape[1]
+    depth = head_dim + 8
     side_by_side = lambda ref: jnp.concatenate([ref[b] for b in range(ref.shape[0])], axis=1)
     pairs = [side_by_side(piece) for piece in pieces]
     keys = [pair[:depth].astype(F32).T.astype(BF16) for pair in pairs]
@@ -176,6 +156,7 @@
     rows = summed.shape[0] - head_dim
     for n, query_ref in enumerate(query_refs):
         queries = side_by_side(query_ref)
+        queries = jnp.concatenate([queries, jnp.zeros((8, queries.shape[1]), BF16)], axis=0)
         scores = [dot(k, queries) for k in keys]
         top = functools.reduce(jnp.maximum, [jnp.max(s, axis=0, keepdims=True) for s in scores])
         if not first:
@@ -248,57 +229,42 @@
     ends = [(i, i + 1) for i in range(1, everyone - 1, 2)]
     odd = lax.ppermute(hint, SEQ, ends + [(b, a) for a, b in ends])
     pair = lax.ppermute(hint, "c", swap)
-    line = shape((1, channels), F32)
-    partial, odd_weight, features, zero_weight, zero_bias, group_gain, norm_gain = call(
+    masks = call(
+        masks_body, [shape((channels, 128), F32)] * 2 + [shape((128, channels), F32)] * 2, (pair,), flops=2000000000
+    )
+    partial, odd_weight, features = call(
         own_row_body,
-        [
-            shape((tokens, channels), F32),
-            shape(conv_weight.shape[1:], BF16),
-            shape((tokens, channels), F32),
-            shape(zero_weight.shape, BF16),
-            line,
-            line,
-            line,
-        ],
-        (core, pair, conv_bias, zero_bias, group_gain, norm_gain, hint, conv_weight, features, zero_weight),
-        scratch=[
-            pltpu.VMEM(hint.shape, BF16),
-            pltpu.VMEM((2, *conv_weight.shape[1:]), BF16),
-            pltpu.VMEM(features.shape, BF16),
-            pltpu.SemaphoreType.DMA((6,)),
-        ],
+        [shape((tokens, channels), F32), shape(conv_weight.shape[1:], BF16), shape((tokens, channels), F32)],
+        (core, hint, pair, conv_weight, conv_bias, features, masks[0]),
         smem=1,
-        away=4,
-        limit=53,
         flops=2 * tokens * channels * channels * 6,
         read=10 * channels * channels * 2,
     )
     merged, stats = call(
         merge_body,
         [shape((tokens, channels), BF16), shape((everyone, 128), F32)],
-        (partial, odd, odd_weight, zero_weight, zero_bias, features),
+        (partial, odd, odd_weight, zero_weight, zero_bias, features, *masks[:3]),
         flops=2 * tokens * channels * channels * 4,
         read=4 * channels * channels * 2,
     )
     stats = lax.all_to_all(stats, SEQ, 0, 0, tiled=True)
     inner, send = call(
         project_body,
-        [shape((tokens, channels), BF16), shape((HEADS, 128, tokens), BF16)],
-        (stats, merged, group_gain, proj_in, norm_gain, query_weight, key_weight, value_weight),
+        [shape((tokens, channels), BF16), shape((HEADS, 3 * head_dim, tokens), BF16)],
+        (stats, merged, group_gain, proj_in, norm_gain, query_weight, key_weight, value_weight, *masks[2:]),
         flops=2 * tokens * channels * channels * 4,
         read=4 * channels * channels * 2,
     )
     received = lax.all_to_all(send, "z", 0, 0, tiled=True)
-    depth = 128 - 2 * head_dim
-    queries, pair = received[:, :depth, :], received[:, depth:, :]
+    queries, pair = received[:, :head_dim, :], received[:, head_dim:, :]
     chips = lax.axis_size("x")
     ring = lambda by: [(i, (i + by) % chips) for i in range(chips)]
     pieces = [lax.ppermute(pair, "x", ring(by)) for by in (chips - 1, 2, 1)]
     others = lax.ppermute(queries, "c", swap)
-    states = attend([queries, others], [pair], None, head_dim)
-    (theirs,) = attend([others], pieces, states[1:], head_dim)
+    state = attend([queries], [pair], None, head_dim)
+    (theirs,) = attend([others], [pair, *pieces], None, head_dim)
     back = lax.ppermute(theirs, "c", swap)
-    (mine,) = attend([queries], pieces, states[:1], head_dim)
+    (mine,) = attend([queries], pieces, state, head_dim)
     result = call(
         functools.partial(combine_body, head_dim), shape((HEADS, head_dim, tokens), BF16), (mine, back)
     )

time: 113 us -> 110 us (0.973)
  blocking collectives: 68.3 us -> 74.7 us
  local copies, waits for them, and re-layouts: 5.66 us -> 0.83 us
  waiting for transfers between devices: 4.17 us -> 1.38 us
  Pallas kernels: 18.2 us -> 16.2 us
    all_to_all x1, blocking collectives: 32.8 us -> 38.8 us  [local(): stats = lax.all_to_all(stats, SEQ, 0, 0, tiled=True)]
    unnamed x26 -> x28, local copies, waits for them, and re-layouts: 5.63 us -> 0.81 us
    ppermute x3, waiting for transfers between devices: 3.38 us -> 0.64 us  [local(): pieces = [lax.ppermute(pair, 'x', ring(by)) for by in (chips - 1, 2, 1)]]
    pallas_call x8 -> x9, Pallas kernels: 18.2 us -> 16.2 us  [call(): pl.pallas_call(body, out_shape=out_shape, in_specs=[SMEM] * smem + [VMEM]...]
  transfers between devices with their start and end apart: 7 -> 7, of which waited for: 3 -> 2; matrix products, arithmetic and copies ran while one was open for 0% -> 0% of each run, Pallas kernels for 9% -> 6%
where the time goes in v5:
time: 110 us; the launch traced here: 109 us
  blocking collectives  74.7 us (68%)
  Pallas kernels  16.2 us (15%)
  starting transfers between devices  16.1 us (15%)
  waiting for transfers between devices  1.38 us (1%)
    all_to_all x1, blocking collectives, local(): stats = lax.all_to_all(stats, SEQ, 0, 0, tiled=True)  38.8 us
    all_to_all x1, blocking collectives, local(): received = lax.all_to_all(send, 'z', 0, 0, tiled=True)  18.8 us
    all_to_all x1, blocking collectives, local(): lax.all_to_all(result, 'z', 0, 0, tiled=True).reshape(channels, tokens)  17.2 us
    pallas_call x9, Pallas kernels, call(): pl.pallas_call(body, out_shape=out_shape, in_specs=[SMEM] * smem + [VMEM]...  16.2 us
    ppermute x3, starting transfers between devices, local(): pieces = [lax.ppermute(pair, 'x', ring(by)) for by in (chips - 1, 2, 1)]  9.36 us
    ppermute x1, starting transfers between devices, local(): back = lax.ppermute(theirs, 'c', swap)  2.23 us
  transfers between devices with their start and end apart: 7, of which 2 were waited for; matrix products, arithmetic and copies ran while one was open for 0% of the time, Pallas kernels for 6%

profile of v5, /device:TPU:24, one launch (start us, length us, event | category | flops | bytes accessed | tf_op | source)
XLA Modules:
  0.0 109.5 jit_solution(12194201764424816920)
XLA Ops:
  0.0 1.9 %collective-permute-start = (bf16[320,128]{1,0:T(8,128)(2,1)}, bf16[320,128]{1,0:T(8,128)(2,1)S(1)}, u32[]{:S(2)}, u32[]{:S(2)}) collective-permute-start(bf16[320,128]{1,0:T(8,128)(2,1)} %bitcast.12), channel_id=1, source_target_pairs={{0,1},{1,0},{2,3},{3,2},{4,5},{5,4},{6,7},{7,6},{8,9},{9,8},{10,11... | collective-permute-start | bytes 245768 | tf_op jit(solution)/shard_map/ppermute | solution.py:231
  1.9 0.7 collective-permute-start.1
  2.6 0.0 copy-start
  2.6 0.0 copy-start.8
  2.6 0.0 copy-start.9
  2.6 0.0 copy-start.10
  2.6 0.7 collective-permute-done._.pair
  3.4 0.1 shard_map.136
  3.5 0.0 copy-start.1
  3.5 0.0 copy-start.11
  3.5 0.7 copy-done
  4.2 0.0 copy-done.8
  4.2 0.0 copy-done.9
  4.2 0.0 copy-done.10
  4.2 0.0 copy-start.3
  4.2 0.0 copy-start.4
  4.3 0.0 copy-start.5
  4.3 0.0 copy-start.12
  4.3 0.0 copy-start.13
  4.3 0.6 shard_map.137
  4.9 0.0 collective-permute-done.1.odd
  4.9 0.0 copy-done.1
  4.9 0.0 copy-done.11
  5.0 1.3 %shard_map.138 = (bf16[128,320]{1,0:T(8,128)(2,1)S(1)}, f32[64,128]{1,0:T(8,128)S(1)}) custom-call(f32[128,320]{1,0:T(8,128)S(1)} %get-tuple-element.17.partial, bf16[320,128]{1,0:T(8,128)(2,1)S(1)} %collective-permute-done.1.odd, bf16[3,320,320]{2,1,0:T(8,128)(2,1)S(1)} %get-tuple-element.18.odd_weight, bf16[320,320]{1,0:T(8,128)(2,1)S(1)} %copy-done.1, ...), custom_call_target="tpu_custom_call" | custom-call | flops 104857600 | bytes 819200 | tf_op jit(solution)/shard_map/pallas_call | solution.py:37
  6.2 38.8 %all_to_all.21 = f32[64,1,128]{2,1,0:T(1,128)S(1)} all-to-all(f32[64,1,128]{2,1,0:T(1,128)S(1)} %bitcast.15), channel_id=1, replica_groups=mesh['dp'=8,'x'=4,'z'=8,'c'=2] {'x','z','c'}, dimensions={0} | all-to-all | bytes 65536 | tf_op jit(solution)/shard_map/all_to_all | solution.py:250
  45.0 0.0 copy-done.2
  45.0 0.0 copy-done.5
  45.0 0.0 copy-done.12
  45.0 0.0 copy-done.13
  45.0 1.2 %shard_map.139 = (bf16[128,320]{1,0:T(8,128)(2,1)S(1)}, bf16[8,120,128]{2,1,0:T(8,128)(2,1)S(1)}) custom-call(f32[64,128]{1,0:T(8,128)S(1)} %bitcast.10, bf16[128,320]{1,0:T(8,128)(2,1)S(1)} %get-tuple-element.23.merged, f32[320]{0:T(512)S(1)} %copy-done.12, bf16[320,320]{1,0:T(8,128)(2,1)S(1)} %copy-done.2, f32[320]{0:T(512)S(1)} %copy-done.13, ...), custom_call_target="tpu_custom_call" | custom-call | flops 104857600 | bytes 819200 | tf_op jit(solution)/shard_map/pallas_call | solution.py:37
  46.3 18.8 %all_to_all.22 = bf16[8,120,128]{2,1,0:T(8,128)(2,1)S(1)} all-to-all(bf16[8,120,128]{2,1,0:T(8,128)(2,1)S(1)} %get-tuple-element.25), channel_id=1, replica_groups=mesh['dp'=8,'x'=4,'z'=8,'c'=2] {'z'}, dimensions={0} | all-to-all | bytes 491520 | tf_op jit(solution)/shard_map/all_to_all | solution.py:258
  65.1 2.6 %collective-permute-start.4 = (bf16[8,80,128]{2,1,0:T(8,128)(2,1)S(1)}, bf16[8,80,128]{2,1,0:T(8,128)(2,1)S(1)}, u32[]{:S(2)}, u32[]{:S(2)}) collective-permute-start(bf16[8,80,128]{2,1,0:T(8,128)(2,1)S(1)} %slice.9.refs_1_), channel_id=1, source_target_pairs={{0,16},{16,32},{32,48},{48,0},{1,17},{17,33},{33,49},{49,1},{2,18}... | collective-permute-start | bytes 491528 | tf_op jit(solution)/shard_map/ppermute | solution.py:262
  67.6 3.8 %collective-permute-start.3 = (bf16[8,80,128]{2,1,0:T(8,128)(2,1)S(1)}, bf16[8,80,128]{2,1,0:T(8,128)(2,1)S(1)}, u32[]{:S(2)}, u32[]{:S(2)}) collective-permute-start(bf16[8,80,128]{2,1,0:T(8,128)(2,1)S(1)} %slice.9.refs_1_), channel_id=1, source_target_pairs={{0,32},{16,48},{32,0},{48,16},{1,33},{17,49},{33,1},{49,17},{2,34}... | collective-permute-start | bytes 491528 | tf_op jit(solution)/shard_map/ppermute | solution.py:262
  71.4 3.0 %collective-permute-start.2 = (bf16[8,80,128]{2,1,0:T(8,128)(2,1)S(1)}, bf16[8,80,128]{2,1,0:T(8,128)(2,1)S(1)}, u32[]{:S(2)}, u32[]{:S(2)}) collective-permute-start(bf16[8,80,128]{2,1,0:T(8,128)(2,1)S(1)} %slice.9.refs_1_), channel_id=1, source_target_pairs={{0,48},{16,0},{32,16},{48,32},{1,49},{17,1},{33,17},{49,33},{2,50}... | collective-permute-start | bytes 491528 | tf_op jit(solution)/shard_map/ppermute | solution.py:262
  74.5 1.9 %collective-permute-start.5 = (bf16[8,40,128]{2,1,0:T(8,128)(2,1)S(1)}, bf16[8,40,128]{2,1,0:T(8,128)(2,1)S(1)}, u32[]{:S(2)}, u32[]{:S(2)}) collective-permute-start(bf16[8,40,128]{2,1,0:T(8,128)(2,1)S(1)} %slice.8.refs_0_), channel_id=1, source_target_pairs={{0,1},{1,0},{2,3},{3,2},{4,5},{5,4},{6,7},{7,6},{8,9},{9,8},{10,11... | collective-permute-start | bytes 245768 | tf_op jit(solution)/shard_map/ppermute | solution.py:263
  76.4 1.6 %shard_map.140.refs_4_ = f32[64,1024]{1,0:T(8,128)S(1)} custom-call(bf16[8,40,128]{2,1,0:T(8,128)(2,1)S(1)} %slice.8.refs_0_, bf16[8,80,128]{2,1,0:T(8,128)(2,1)S(1)} %slice.9.refs_1_), custom_call_target="tpu_custom_call" | custom-call | flops 1073741824 | bytes 163840 | tf_op jit(solution)/shard_map/pallas_call | solution.py:37
  78.0 0.0 collective-permute-done.5.refs_0_
  78.0 0.0 collective-permute-done.4.refs_3_.refs_4_
  78.0 0.0 collective-permute-done.3.refs_2_.refs_3_
  78.0 0.6 collective-permute-done.2.refs_1_.refs_2_
  78.6 5.8 %shard_map.142 = f32[64,1024]{1,0:T(8,128)S(1)} custom-call(bf16[8,40,128]{2,1,0:T(8,128)(2,1)S(1)} %collective-permute-done.5.refs_0_, bf16[8,80,128]{2,1,0:T(8,128)(2,1)S(1)} %slice.9.refs_1_, bf16[8,80,128]{2,1,0:T(8,128)(2,1)S(1)} %collective-permute-done.2.refs_1_.refs_2_, bf16[8,80,128]{2,1,0:T(8,128)(2,1)S(1)} %collective-permute-done.3.refs_2_.refs_3_, ...), custom_call_target="tpu_custom_call" | custom-call | flops 4294967296 | bytes 655360 | tf_op jit(solution)/shard_map/pallas_call | solution.py:37
  84.4 0.0 copy-start.6
  84.4 0.0 copy-start.7
  84.4 2.2 %collective-permute-start.6 = (f32[64,1024]{1,0:T(8,128)S(1)}, f32[64,1024]{1,0:T(8,128)S(1)}, u32[]{:S(2)}, u32[]{:S(2)}) collective-permute-start(f32[64,1024]{1,0:T(8,128)S(1)} %shard_map.142), channel_id=1, source_target_pairs={{0,1},{1,0},{2,3},{3,2},{4,5},{5,4},{6,7},{7,6},{8,9},{9,8},{10,11... | collective-permute-start | bytes 786440 | tf_op jit(solution)/shard_map/ppermute | solution.py:266
  86.7 4.4 %shard_map.141.mine = f32[64,1024]{1,0:T(8,128)S(1)} custom-call(bf16[8,40,128]{2,1,0:T(8,128)(2,1)S(1)} %slice.8.refs_0_, bf16[8,80,128]{2,1,0:T(8,128)(2,1)S(1)} %collective-permute-done.2.refs_1_.refs_2_, bf16[8,80,128]{2,1,0:T(8,128)(2,1)S(1)} %collective-permute-done.3.refs_2_.refs_3_, bf16[8,80,128]{2,1,0:T(8,128)(2,1)S(1)} %collective-permute-done.4.refs_3_.refs_4_, ...), custom_call_target="tpu_custom_call" | custom-call | flops 3221225472 | bytes 491520 | tf_op jit(solution)/shard_map/pallas_call | solution.py:37
  91.1 0.0 collective-permute-done.6.theirs
  91.1 17.2 %all_to_all.23 = bf16[8,40,128]{2,1,0:T(8,128)(2,1)S(1)} all-to-all(bf16[8,40,128]{2,1,0:T(8,128)(2,1)S(1)} %shard_map.143), channel_id=1, replica_groups=mesh['dp'=8,'x'=4,'z'=8,'c'=2] {'z'}, dimensions={0} | all-to-all | bytes 163840 | tf_op jit(solution)/shard_map/all_to_all | solution.py:271
  108.3 1.2 %shard_map.144 = bf16[320,128]{1,0:T(8,128)(2,1)} custom-call(bf16[320,128]{1,0:T(8,128)(2,1)S(1)} %bitcast.9, bf16[128,320]{1,0:T(8,128)(2,1)S(1)} %get-tuple-element.26.inner, bf16[128,320]{1,0:T(8,128)(2,1)S(1)} %get-tuple-element.23.merged, bf16[320,320]{1,0:T(8,128)(2,1)S(1)} %copy-done.6, bf16[320,320]{1,0:T(8,128)(2,1)S(1)} %copy-done.7), custom_call_target="tpu_custom_call" | custom-call | flops 52428800 | bytes 409600 | tf_op jit(solution)/shard_map/pallas_call | solution.py:37
  (8 shorter events, 0.1 us)
Async XLA Ops:
  0.0 3.4 %collective-permute-start = (bf16[320,128]{1,0:T(8,128)(2,1)}, bf16[320,128]{1,0:T(8,128)(2,1)S(1)}, u32[]{:S(2)}, u32[]{:S(2)}) collective-permute-start(bf16[320,128]{1,0:T(8,128)(2,1)} %bitcast.12), channel_id=1, source_target_pairs={{0,1},{1,0},{2,3},{3,2},{4,5},{5,4},{6,7},{7,6},{8,9},{9,8},{10,11... | collective-permute-start | bytes 245768 | tf_op jit(solution)/shard_map/ppermute | solution.py:231
  1.9 3.0 %collective-permute-start.1 = (bf16[320,128]{1,0:T(8,128)(2,1)}, bf16[320,128]{1,0:T(8,128)(2,1)S(1)}, u32[]{:S(2)}, u32[]{:S(2)}) collective-permute-start(bf16[320,128]{1,0:T(8,128)(2,1)} %bitcast.13), channel_id=1, source_target_pairs={{1,2},{3,4},{5,6},{7,8},{9,10},{11,12},{13,14},{15,16},{17,18},{19... | collective-permute-start | bytes 245768 | tf_op jit(solution)/shard_map/ppermute | solution.py:230
  2.6 1.6 %copy-start = (bf16[3,3,320,320]{3,2,1,0:T(8,128)(2,1)S(1)}, bf16[3,3,320,320]{3,2,1,0:T(8,128)(2,1)}, u32[]{:S(2)}) copy-start(bf16[3,3,320,320]{3,2,1,0:T(8,128)(2,1)} %weight.1) | copy-start | bytes 5529604
  2.6 1.6 %copy-start.8 = (bf16[128,320]{0,1:T(8,128)(2,1)S(1)}, bf16[128,320]{0,1:T(8,128)(2,1)}, u32[]{:S(2)}) copy-start(bf16[128,320]{0,1:T(8,128)(2,1)} %param.14) | copy-start | bytes 245764
  2.6 1.6 %copy-start.9 = (bf16[128,320]{0,1:T(8,128)(2,1)S(1)}, bf16[128,320]{0,1:T(8,128)(2,1)}, u32[]{:S(2)}) copy-start(bf16[128,320]{0,1:T(8,128)(2,1)} %param.15) | copy-start | bytes 245764
  2.6 1.6 %copy-start.10 = (f32[320]{0:T(512)S(1)}, f32[320]{0:T(512)}, u32[]{:S(2)}) copy-start(f32[320]{0:T(512)} %bias.1) | copy-start | bytes 3844
  3.5 1.5 %copy-start.1 = (bf16[320,320]{1,0:T(8,128)(2,1)S(1)}, bf16[320,320]{1,0:T(8,128)(2,1)}, u32[]{:S(2)}) copy-start(bf16[320,320]{1,0:T(8,128)(2,1)} %zero_weight.1) | copy-start | bytes 614404
  3.5 1.5 %copy-start.11 = (f32[320]{0:T(512)S(1)}, f32[320]{0:T(512)}, u32[]{:S(2)}) copy-start(f32[320]{0:T(512)} %zero_bias.1) | copy-start | bytes 3844
  4.2 40.8 %copy-start.2 = (bf16[320,320]{1,0:T(8,128)(2,1)S(1)}, bf16[320,320]{1,0:T(8,128)(2,1)}, u32[]{:S(2)}) copy-start(bf16[320,320]{1,0:T(8,128)(2,1)} %proj_in.1) | copy-start | bytes 614404
  4.2 40.8 %copy-start.3 = (bf16[320,320]{1,0:T(8,128)(2,1)S(1)}, bf16[320,320]{1,0:T(8,128)(2,1)}, u32[]{:S(2)}) copy-start(bf16[320,320]{1,0:T(8,128)(2,1)} %wq.1) | copy-start | bytes 614404
  4.2 40.8 %copy-start.4 = (bf16[320,320]{1,0:T(8,128)(2,1)S(1)}, bf16[320,320]{1,0:T(8,128)(2,1)}, u32[]{:S(2)}) copy-start(bf16[320,320]{1,0:T(8,128)(2,1)} %wk.1) | copy-start | bytes 614404
  4.3 40.8 %copy-start.5 = (bf16[320,320]{1,0:T(8,128)(2,1)S(1)}, bf16[320,320]{1,0:T(8,128)(2,1)}, u32[]{:S(2)}) copy-start(bf16[320,320]{1,0:T(8,128)(2,1)} %wv.1) | copy-start | bytes 614404
  4.3 40.8 %copy-start.12 = (f32[320]{0:T(512)S(1)}, f32[320]{0:T(512)}, u32[]{:S(2)}) copy-start(f32[320]{0:T(512)} %group_gain.1) | copy-start | bytes 3844
  4.3 40.8 %copy-start.13 = (f32[320]{0:T(512)S(1)}, f32[320]{0:T(512)}, u32[]{:S(2)}) copy-start(f32[320]{0:T(512)} %norm_gain.1) | copy-start | bytes 3844
  65.1 12.9 %collective-permute-start.4 = (bf16[8,80,128]{2,1,0:T(8,128)(2,1)S(1)}, bf16[8,80,128]{2,1,0:T(8,128)(2,1)S(1)}, u32[]{:S(2)}, u32[]{:S(2)}) collective-permute-start(bf16[8,80,128]{2,1,0:T(8,128)(2,1)S(1)} %slice.9.refs_1_), channel_id=1, source_target_pairs={{0,16},{16,32},{32,48},{48,0},{1,17},{17,33},{33,49},{49,1},{2,18}... | collective-permute-start | bytes 491528 | tf_op jit(solution)/shard_map/ppermute | solution.py:262
  67.6 10.3 %collective-permute-start.3 = (bf16[8,80,128]{2,1,0:T(8,128)(2,1)S(1)}, bf16[8,80,128]{2,1,0:T(8,128)(2,1)S(1)}, u32[]{:S(2)}, u32[]{:S(2)}) collective-permute-start(bf16[8,80,128]{2,1,0:T(8,128)(2,1)S(1)} %slice.9.refs_1_), channel_id=1, source_target_pairs={{0,32},{16,48},{32,0},{48,16},{1,33},{17,49},{33,1},{49,17},{2,34}... | collective-permute-start | bytes 491528 | tf_op jit(solution)/shard_map/ppermute | solution.py:262
  71.4 7.2 %collective-permute-start.2 = (bf16[8,80,128]{2,1,0:T(8,128)(2,1)S(1)}, bf16[8,80,128]{2,1,0:T(8,128)(2,1)S(1)}, u32[]{:S(2)}, u32[]{:S(2)}) collective-permute-start(bf16[8,80,128]{2,1,0:T(8,128)(2,1)S(1)} %slice.9.refs_1_), channel_id=1, source_target_pairs={{0,48},{16,0},{32,16},{48,32},{1,49},{17,1},{33,17},{49,33},{2,50}... | collective-permute-start | bytes 491528 | tf_op jit(solution)/shard_map/ppermute | solution.py:262
  74.5 3.5 %collective-permute-start.5 = (bf16[8,40,128]{2,1,0:T(8,128)(2,1)S(1)}, bf16[8,40,128]{2,1,0:T(8,128)(2,1)S(1)}, u32[]{:S(2)}, u32[]{:S(2)}) collective-permute-start(bf16[8,40,128]{2,1,0:T(8,128)(2,1)S(1)} %slice.8.refs_0_), channel_id=1, source_target_pairs={{0,1},{1,0},{2,3},{3,2},{4,5},{5,4},{6,7},{7,6},{8,9},{9,8},{10,11... | collective-permute-start | bytes 245768 | tf_op jit(solution)/shard_map/ppermute | solution.py:263
  84.4 23.9 %copy-start.6 = (bf16[320,320]{1,0:T(8,128)(2,1)S(1)}, bf16[320,320]{1,0:T(8,128)(2,1)}, u32[]{:S(2)}) copy-start(bf16[320,320]{1,0:T(8,128)(2,1)} %attn_out.1) | copy-start | bytes 614404
  84.4 23.9 %copy-start.7 = (bf16[320,320]{1,0:T(8,128)(2,1)S(1)}, bf16[320,320]{1,0:T(8,128)(2,1)}, u32[]{:S(2)}) copy-start(bf16[320,320]{1,0:T(8,128)(2,1)} %proj_out.1) | copy-start | bytes 614404
  84.4 6.7 %collective-permute-start.6 = (f32[64,1024]{1,0:T(8,128)S(1)}, f32[64,1024]{1,0:T(8,128)S(1)}, u32[]{:S(2)}, u32[]{:S(2)}) collective-permute-start(f32[64,1024]{1,0:T(8,128)S(1)} %shard_map.142), channel_id=1, source_target_pairs={{0,1},{1,0},{2,3},{3,2},{4,5},{5,4},{6,7},{7,6},{8,9},{9,8},{10,11... | collective-permute-start | bytes 786440 | tf_op jit(solution)/shard_map/ppermute | solution.py:266

commit v6 on v5

--- a/solution.py
+++ b/solution.py
@@ -16,6 +16,7 @@
 DP_SEQ = ("dp", "x", "z", "c")
 NORM_EPS = 1e-06
 LAYER_EPS = 1e-05
+BOUND_LIMIT = 56.0
 HIGHEST = lax.Precision.HIGHEST
 F32 = jnp.float32
 BF16 = jnp.bfloat16
@@ -67,7 +68,7 @@
     return ref[...].astype(F32).T
 
 
-def masks_body(_, gather_low, gather_high, spread_low, spread_high):
+def masks_body(gather_low, gather_high, spread_low, spread_high):
     channels, lanes = gather_low.shape
     gather_low[...] = group_gather(channels, lanes, 0)
     gather_high[...] = group_gather(channels, lanes, GROUPS)
@@ -142,6 +143,11 @@
         send[h] = block.astype(BF16)
 
 
+def squared(vectors):
+    wide = vectors.astype(F32)
+    return jnp.sum(wide * wide, axis=0, keepdims=True)
+
+
 def attend_body(head_dim, first, n_queries, n_pieces, *refs):
     query_refs, refs = refs[:n_queries], refs[n_queries:]
     pieces, refs = refs[:n_pieces], refs[n_pieces:]
@@ -154,20 +160,36 @@
     ones = jnp.ones((16, pairs[0].shape[1]), BF16)
     summed = jnp.concatenate([jnp.concatenate([pair, ones], axis=0) for pair in pairs], axis=1)
     rows = summed.shape[0] - head_dim
+    squares = functools.reduce(jnp.maximum, [squared(pair[:head_dim]) for pair in pairs])
+    longest = jnp.sqrt(jnp.max(squares, axis=1, keepdims=True)) * (1.0 + 2.0**-10)
     for n, query_ref in enumerate(query_refs):
         queries = side_by_side(query_ref)
+        bound = jnp.sqrt(squared(queries)) * longest
         queries = jnp.concatenate([queries, jnp.zeros((8, queries.shape[1]), BF16)], axis=0)
-        scores = [dot(k, queries) for k in keys]
-        top = functools.reduce(jnp.maximum, [jnp.max(s, axis=0, keepdims=True) for s in scores])
-        if not first:
-            before = states[n][rows : rows + 1, :]
-            top = jnp.maximum(top, before)
-        probs = jnp.concatenate([jnp.exp2(s - top).astype(BF16) for s in scores], axis=0)
-        total = dot(summed, probs)[head_dim:]
-        if not first:
-            total += states[n][:rows, :] * jnp.exp2(before - top)
-        refs[n][:rows, :] = total
-        refs[n][rows:, :] = jnp.broadcast_to(top, (8, top.shape[1]))
+
+        def store(top, probs):
+            if not first:
+                before = states[n][rows : rows + 1, :]
+                new_top = jnp.maximum(top, before)
+            else:
+                new_top = top
+            total = dot(summed, jnp.concatenate(probs, axis=0))[head_dim:]
+            if not first:
+                total = total * jnp.exp2(top - new_top) + states[n][:rows, :] * jnp.exp2(before - new_top)
+            refs[n][:rows, :] = total
+            refs[n][rows:, :] = jnp.broadcast_to(new_top, (8, new_top.shape[1]))
+
+        safe = jnp.max(bound) <= BOUND_LIMIT
+
+        @pl.when(safe)
+        def _():
+            store(bound, [jnp.exp2(dot(k, queries) - bound).astype(BF16) for k in keys])
+
+        @pl.when(jnp.logical_not(safe))
+        def _():
+            scores = [dot(k, queries) for k in keys]
+            top = functools.reduce(jnp.maximum, [jnp.max(s, axis=0, keepdims=True) for s in scores])
+            store(top, [jnp.exp2(s - top).astype(BF16) for s in scores])
 
 
 def attend(queries, pieces, states, head_dim):
@@ -230,7 +252,7 @@
     odd = lax.ppermute(hint, SEQ, ends + [(b, a) for a, b in ends])
     pair = lax.ppermute(hint, "c", swap)
     masks = call(
-        masks_body, [shape((channels, 128), F32)] * 2 + [shape((128, channels), F32)] * 2, (pair,), flops=2000000000
+        masks_body, [shape((channels, 128), F32)] * 2 + [shape((128, channels), F32)] * 2, (), flops=2000000000
     )
     partial, odd_weight, features = call(
         own_row_body,

time: 110 us -> 108 us (0.982)
  blocking collectives: 74.7 us -> 69.3 us
  starting transfers between devices: 16.1 us -> 19.4 us
    all_to_all x1, blocking collectives: 38.8 us -> 33.5 us  [local(): stats = lax.all_to_all(stats, SEQ, 0, 0, tiled=True)]
    ppermute x1, starting transfers between devices: 1.91 us -> 5.18 us  [local(): pair = lax.ppermute(hint, 'c', swap)]
  transfers between devices with their start and end apart: 7 -> 7, of which waited for: 2 -> 2; matrix products, arithmetic and copies ran while one was open for 0% -> 0% of each run, Pallas kernels for 6% -> 7%
where the time goes in v6:
time: 108 us
  blocking collectives  69.3 us (64%)
  starting transfers between devices  19.4 us (18%)
  Pallas kernels  17.1 us (16%)
  waiting for transfers between devices  1.45 us (1%)
    all_to_all x1, blocking collectives, local(): stats = lax.all_to_all(stats, SEQ, 0, 0, tiled=True)  33.5 us
    all_to_all x1, blocking collectives, local(): received = lax.all_to_all(send, 'z', 0, 0, tiled=True)  18.8 us
    all_to_all x1, blocking collectives, local(): lax.all_to_all(result, 'z', 0, 0, tiled=True).reshape(channels, tokens)  17.1 us
    pallas_call x9, Pallas kernels, call(): pl.pallas_call(body, out_shape=out_shape, in_specs=[SMEM] * smem + [VMEM]...  17.1 us
    ppermute x3, starting transfers between devices, local(): pieces = [lax.ppermute(pair, 'x', ring(by)) for by in (chips - 1, 2, 1)]  9.36 us
    ppermute x1, starting transfers between devices, local(): pair = lax.ppermute(hint, 'c', swap)  5.18 us
  transfers between devices with their start and end apart: 7, of which 2 were waited for; matrix products, arithmetic and copies ran while one was open for 0% of the time, Pallas kernels for 7%

profile of v6, /device:TPU:24, one launch (start us, length us, event | category | flops | bytes accessed | tf_op | source)
XLA Modules:
  0.0 107.6 jit_solution(13318814195173813696)
XLA Ops:
  0.0 0.0 copy-start.10
  0.0 0.8 collective-permute-start.1
  0.8 5.2 %collective-permute-start = (bf16[320,128]{1,0:T(8,128)(2,1)}, bf16[320,128]{1,0:T(8,128)(2,1)S(1)}, u32[]{:S(2)}, u32[]{:S(2)}) collective-permute-start(bf16[320,128]{1,0:T(8,128)(2,1)} %bitcast.13), channel_id=1, source_target_pairs={{0,1},{1,0},{2,3},{3,2},{4,5},{5,4},{6,7},{7,6},{8,9},{9,8},{10,11... | collective-permute-start | bytes 245768 | tf_op jit(solution)/shard_map/ppermute | solution.py:253
  6.0 0.1 shard_map.136
  6.1 0.0 copy-start.1
  6.1 0.0 copy-start.11
  6.1 1.0 collective-permute-done.pair
  7.1 0.0 copy-done
  7.1 0.0 copy-done.8
  7.1 0.0 copy-done.9
  7.1 0.0 copy-done.10
  7.1 0.0 copy-start.2
  7.2 0.0 copy-start.3
  7.2 0.0 copy-start.4
  7.2 0.0 copy-start.5
  7.2 0.0 copy-start.12
  7.2 0.0 copy-start.13
  7.2 0.6 shard_map.137
  7.8 0.0 collective-permute-done.1.odd
  7.8 0.0 copy-done.1
  7.8 0.0 copy-done.11
  7.9 1.3 %shard_map.138 = (bf16[128,320]{1,0:T(8,128)(2,1)S(1)}, f32[64,128]{1,0:T(8,128)S(1)}) custom-call(f32[128,320]{1,0:T(8,128)S(1)} %get-tuple-element.17.partial, bf16[320,128]{1,0:T(8,128)(2,1)S(1)} %collective-permute-done.1.odd, bf16[3,320,320]{2,1,0:T(8,128)(2,1)S(1)} %get-tuple-element.18.odd_weight, bf16[320,320]{1,0:T(8,128)(2,1)S(1)} %copy-done.1, ...), custom_call_target="tpu_custom_call" | custom-call | flops 104857600 | bytes 819200 | tf_op jit(solution)/shard_map/pallas_call | solution.py:38
  9.1 33.5 %all_to_all.21 = f32[64,1,128]{2,1,0:T(1,128)S(1)} all-to-all(f32[64,1,128]{2,1,0:T(1,128)S(1)} %bitcast.15), channel_id=1, replica_groups=mesh['dp'=8,'x'=4,'z'=8,'c'=2] {'x','z','c'}, dimensions={0} | all-to-all | bytes 65536 | tf_op jit(solution)/shard_map/all_to_all | solution.py:272
  42.6 0.0 copy-done.2
  42.6 0.0 copy-done.3
  42.6 0.0 copy-done.4
  42.6 0.0 copy-done.5
  42.6 0.0 copy-done.12
  42.6 0.0 copy-done.13
  42.6 1.2 %shard_map.139 = (bf16[128,320]{1,0:T(8,128)(2,1)S(1)}, bf16[8,120,128]{2,1,0:T(8,128)(2,1)S(1)}) custom-call(f32[64,128]{1,0:T(8,128)S(1)} %bitcast.10, bf16[128,320]{1,0:T(8,128)(2,1)S(1)} %get-tuple-element.23.merged, f32[320]{0:T(512)S(1)} %copy-done.12, bf16[320,320]{1,0:T(8,128)(2,1)S(1)} %copy-done.2, f32[320]{0:T(512)S(1)} %copy-done.13, ...), custom_call_target="tpu_custom_call" | custom-call | flops 104857600 | bytes 819200 | tf_op jit(solution)/shard_map/pallas_call | solution.py:38
  43.9 18.8 %all_to_all.22 = bf16[8,120,128]{2,1,0:T(8,128)(2,1)S(1)} all-to-all(bf16[8,120,128]{2,1,0:T(8,128)(2,1)S(1)} %get-tuple-element.25), channel_id=1, replica_groups=mesh['dp'=8,'x'=4,'z'=8,'c'=2] {'z'}, dimensions={0} | all-to-all | bytes 491520 | tf_op jit(solution)/shard_map/all_to_all | solution.py:280
  62.6 2.6 %collective-permute-start.4 = (bf16[8,80,128]{2,1,0:T(8,128)(2,1)S(1)}, bf16[8,80,128]{2,1,0:T(8,128)(2,1)S(1)}, u32[]{:S(2)}, u32[]{:S(2)}) collective-permute-start(bf16[8,80,128]{2,1,0:T(8,128)(2,1)S(1)} %slice.9.refs_1_), channel_id=1, source_target_pairs={{0,16},{16,32},{32,48},{48,0},{1,17},{17,33},{33,49},{49,1},{2,18}... | collective-permute-start | bytes 491528 | tf_op jit(solution)/shard_map/ppermute | solution.py:284
  65.2 3.8 %collective-permute-start.3 = (bf16[8,80,128]{2,1,0:T(8,128)(2,1)S(1)}, bf16[8,80,128]{2,1,0:T(8,128)(2,1)S(1)}, u32[]{:S(2)}, u32[]{:S(2)}) collective-permute-start(bf16[8,80,128]{2,1,0:T(8,128)(2,1)S(1)} %slice.9.refs_1_), channel_id=1, source_target_pairs={{0,32},{16,48},{32,0},{48,16},{1,33},{17,49},{33,1},{49,17},{2,34}... | collective-permute-start | bytes 491528 | tf_op jit(solution)/shard_map/ppermute | solution.py:284
  69.0 3.0 %collective-permute-start.2 = (bf16[8,80,128]{2,1,0:T(8,128)(2,1)S(1)}, bf16[8,80,128]{2,1,0:T(8,128)(2,1)S(1)}, u32[]{:S(2)}, u32[]{:S(2)}) collective-permute-start(bf16[8,80,128]{2,1,0:T(8,128)(2,1)S(1)} %slice.9.refs_1_), channel_id=1, source_target_pairs={{0,48},{16,0},{32,16},{48,32},{1,49},{17,1},{33,17},{49,33},{2,50}... | collective-permute-start | bytes 491528 | tf_op jit(solution)/shard_map/ppermute | solution.py:284
  72.0 1.9 %collective-permute-start.5 = (bf16[8,40,128]{2,1,0:T(8,128)(2,1)S(1)}, bf16[8,40,128]{2,1,0:T(8,128)(2,1)S(1)}, u32[]{:S(2)}, u32[]{:S(2)}) collective-permute-start(bf16[8,40,128]{2,1,0:T(8,128)(2,1)S(1)} %slice.8.refs_0_), channel_id=1, source_target_pairs={{0,1},{1,0},{2,3},{3,2},{4,5},{5,4},{6,7},{7,6},{8,9},{9,8},{10,11... | collective-permute-start | bytes 245768 | tf_op jit(solution)/shard_map/ppermute | solution.py:285
  74.0 1.8 %shard_map.140.refs_4_ = f32[64,1024]{1,0:T(8,128)S(1)} custom-call(bf16[8,40,128]{2,1,0:T(8,128)(2,1)S(1)} %slice.8.refs_0_, bf16[8,80,128]{2,1,0:T(8,128)(2,1)S(1)} %slice.9.refs_1_), custom_call_target="tpu_custom_call" | custom-call | flops 1073741824 | bytes 163840 | tf_op jit(solution)/shard_map/pallas_call | solution.py:38
  75.7 0.0 collective-permute-done.5.refs_0_
  75.7 0.0 collective-permute-done.4.refs_3_.refs_4_
  75.7 0.0 collective-permute-done.3.refs_2_.refs_3_
  75.7 0.4 collective-permute-done.2.refs_1_.refs_2_
  76.2 6.3 %shard_map.142 = f32[64,1024]{1,0:T(8,128)S(1)} custom-call(bf16[8,40,128]{2,1,0:T(8,128)(2,1)S(1)} %collective-permute-done.5.refs_0_, bf16[8,80,128]{2,1,0:T(8,128)(2,1)S(1)} %slice.9.refs_1_, bf16[8,80,128]{2,1,0:T(8,128)(2,1)S(1)} %collective-permute-done.2.refs_1_.refs_2_, bf16[8,80,128]{2,1,0:T(8,128)(2,1)S(1)} %collective-permute-done.3.refs_2_.refs_3_, ...), custom_call_target="tpu_custom_call" | custom-call | flops 4294967296 | bytes 655360 | tf_op jit(solution)/shard_map/pallas_call | solution.py:38
  82.5 0.0 copy-start.6
  82.5 0.0 copy-start.7
  82.6 2.1 %collective-permute-start.6 = (f32[64,1024]{1,0:T(8,128)S(1)}, f32[64,1024]{1,0:T(8,128)S(1)}, u32[]{:S(2)}, u32[]{:S(2)}) collective-permute-start(f32[64,1024]{1,0:T(8,128)S(1)} %shard_map.142), channel_id=1, source_target_pairs={{0,1},{1,0},{2,3},{3,2},{4,5},{5,4},{6,7},{7,6},{8,9},{9,8},{10,11... | collective-permute-start | bytes 786440 | tf_op jit(solution)/shard_map/ppermute | solution.py:288
  84.7 4.6 %shard_map.141.mine = f32[64,1024]{1,0:T(8,128)S(1)} custom-call(bf16[8,40,128]{2,1,0:T(8,128)(2,1)S(1)} %slice.8.refs_0_, bf16[8,80,128]{2,1,0:T(8,128)(2,1)S(1)} %collective-permute-done.2.refs_1_.refs_2_, bf16[8,80,128]{2,1,0:T(8,128)(2,1)S(1)} %collective-permute-done.3.refs_2_.refs_3_, bf16[8,80,128]{2,1,0:T(8,128)(2,1)S(1)} %collective-permute-done.4.refs_3_.refs_4_, ...), custom_call_target="tpu_custom_call" | custom-call | flops 3221225472 | bytes 491520 | tf_op jit(solution)/shard_map/pallas_call | solution.py:38
  89.3 0.0 collective-permute-done.6.theirs
  89.3 17.1 %all_to_all.23 = bf16[8,40,128]{2,1,0:T(8,128)(2,1)S(1)} all-to-all(bf16[8,40,128]{2,1,0:T(8,128)(2,1)S(1)} %shard_map.143), channel_id=1, replica_groups=mesh['dp'=8,'x'=4,'z'=8,'c'=2] {'z'}, dimensions={0} | all-to-all | bytes 163840 | tf_op jit(solution)/shard_map/all_to_all | solution.py:293
  106.5 1.1 %shard_map.144 = bf16[320,128]{1,0:T(8,128)(2,1)} custom-call(bf16[320,128]{1,0:T(8,128)(2,1)S(1)} %bitcast.9, bf16[128,320]{1,0:T(8,128)(2,1)S(1)} %get-tuple-element.26.inner, bf16[128,320]{1,0:T(8,128)(2,1)S(1)} %get-tuple-element.23.merged, bf16[320,320]{1,0:T(8,128)(2,1)S(1)} %copy-done.6, bf16[320,320]{1,0:T(8,128)(2,1)S(1)} %copy-done.7), custom_call_target="tpu_custom_call" | custom-call | flops 52428800 | bytes 409600 | tf_op jit(solution)/shard_map/pallas_call | solution.py:38
  (8 shorter events, 0.1 us)
Async XLA Ops:
  0.0 7.1 %copy-start = (bf16[3,3,320,320]{3,2,1,0:T(8,128)(2,1)S(1)}, bf16[3,3,320,320]{3,2,1,0:T(8,128)(2,1)}, u32[]{:S(2)}) copy-start(bf16[3,3,320,320]{3,2,1,0:T(8,128)(2,1)} %weight.1) | copy-start | bytes 5529604
  0.0 7.1 %copy-start.8 = (bf16[128,320]{0,1:T(8,128)(2,1)S(1)}, bf16[128,320]{0,1:T(8,128)(2,1)}, u32[]{:S(2)}) copy-start(bf16[128,320]{0,1:T(8,128)(2,1)} %param.14) | copy-start | bytes 245764
  0.0 7.1 %copy-start.9 = (bf16[128,320]{0,1:T(8,128)(2,1)S(1)}, bf16[128,320]{0,1:T(8,128)(2,1)}, u32[]{:S(2)}) copy-start(bf16[128,320]{0,1:T(8,128)(2,1)} %param.15) | copy-start | bytes 245764
  0.0 7.1 %copy-start.10 = (f32[320]{0:T(512)S(1)}, f32[320]{0:T(512)}, u32[]{:S(2)}) copy-start(f32[320]{0:T(512)} %bias.1) | copy-start | bytes 3844
  0.0 7.8 %collective-permute-start.1 = (bf16[320,128]{1,0:T(8,128)(2,1)}, bf16[320,128]{1,0:T(8,128)(2,1)S(1)}, u32[]{:S(2)}, u32[]{:S(2)}) collective-permute-start(bf16[320,128]{1,0:T(8,128)(2,1)} %bitcast.12), channel_id=1, source_target_pairs={{1,2},{3,4},{5,6},{7,8},{9,10},{11,12},{13,14},{15,16},{17,18},{19... | collective-permute-start | bytes 245768 | tf_op jit(solution)/shard_map/ppermute | solution.py:252
  0.8 6.3 %collective-permute-start = (bf16[320,128]{1,0:T(8,128)(2,1)}, bf16[320,128]{1,0:T(8,128)(2,1)S(1)}, u32[]{:S(2)}, u32[]{:S(2)}) collective-permute-start(bf16[320,128]{1,0:T(8,128)(2,1)} %bitcast.13), channel_id=1, source_target_pairs={{0,1},{1,0},{2,3},{3,2},{4,5},{5,4},{6,7},{7,6},{8,9},{9,8},{10,11... | collective-permute-start | bytes 245768 | tf_op jit(solution)/shard_map/ppermute | solution.py:253
  6.1 1.7 %copy-start.1 = (bf16[320,320]{1,0:T(8,128)(2,1)S(1)}, bf16[320,320]{1,0:T(8,128)(2,1)}, u32[]{:S(2)}) copy-start(bf16[320,320]{1,0:T(8,128)(2,1)} %zero_weight.1) | copy-start | bytes 614404
  6.1 1.7 %copy-start.11 = (f32[320]{0:T(512)S(1)}, f32[320]{0:T(512)}, u32[]{:S(2)}) copy-start(f32[320]{0:T(512)} %zero_bias.1) | copy-start | bytes 3844
  7.1 35.4 %copy-start.2 = (bf16[320,320]{1,0:T(8,128)(2,1)S(1)}, bf16[320,320]{1,0:T(8,128)(2,1)}, u32[]{:S(2)}) copy-start(bf16[320,320]{1,0:T(8,128)(2,1)} %proj_in.1) | copy-start | bytes 614404
  7.2 35.4 %copy-start.3 = (bf16[320,320]{1,0:T(8,128)(2,1)S(1)}, bf16[320,320]{1,0:T(8,128)(2,1)}, u32[]{:S(2)}) copy-start(bf16[320,320]{1,0:T(8,128)(2,1)} %wq.1) | copy-start | bytes 614404
  7.2 35.4 %copy-start.4 = (bf16[320,320]{1,0:T(8,128)(2,1)S(1)}, bf16[320,320]{1,0:T(8,128)(2,1)}, u32[]{:S(2)}) copy-start(bf16[320,320]{1,0:T(8,128)(2,1)} %wk.1) | copy-start | bytes 614404
  7.2 35.4 %copy-start.5 = (bf16[320,320]{1,0:T(8,128)(2,1)S(1)}, bf16[320,320]{1,0:T(8,128)(2,1)}, u32[]{:S(2)}) copy-start(bf16[320,320]{1,0:T(8,128)(2,1)} %wv.1) | copy-start | bytes 614404
  7.2 35.4 %copy-start.12 = (f32[320]{0:T(512)S(1)}, f32[320]{0:T(512)}, u32[]{:S(2)}) copy-start(f32[320]{0:T(512)} %group_gain.1) | copy-start | bytes 3844
  7.2 35.4 %copy-start.13 = (f32[320]{0:T(512)S(1)}, f32[320]{0:T(512)}, u32[]{:S(2)}) copy-start(f32[320]{0:T(512)} %norm_gain.1) | copy-start | bytes 3844
  62.6 13.1 %collective-permute-start.4 = (bf16[8,80,128]{2,1,0:T(8,128)(2,1)S(1)}, bf16[8,80,128]{2,1,0:T(8,128)(2,1)S(1)}, u32[]{:S(2)}, u32[]{:S(2)}) collective-permute-start(bf16[8,80,128]{2,1,0:T(8,128)(2,1)S(1)} %slice.9.refs_1_), channel_id=1, source_target_pairs={{0,16},{16,32},{32,48},{48,0},{1,17},{17,33},{33,49},{49,1},{2,18}... | collective-permute-start | bytes 491528 | tf_op jit(solution)/shard_map/ppermute | solution.py:284
  65.2 10.5 %collective-permute-start.3 = (bf16[8,80,128]{2,1,0:T(8,128)(2,1)S(1)}, bf16[8,80,128]{2,1,0:T(8,128)(2,1)S(1)}, u32[]{:S(2)}, u32[]{:S(2)}) collective-permute-start(bf16[8,80,128]{2,1,0:T(8,128)(2,1)S(1)} %slice.9.refs_1_), channel_id=1, source_target_pairs={{0,32},{16,48},{32,0},{48,16},{1,33},{17,49},{33,1},{49,17},{2,34}... | collective-permute-start | bytes 491528 | tf_op jit(solution)/shard_map/ppermute | solution.py:284
  69.0 7.2 %collective-permute-start.2 = (bf16[8,80,128]{2,1,0:T(8,128)(2,1)S(1)}, bf16[8,80,128]{2,1,0:T(8,128)(2,1)S(1)}, u32[]{:S(2)}, u32[]{:S(2)}) collective-permute-start(bf16[8,80,128]{2,1,0:T(8,128)(2,1)S(1)} %slice.9.refs_1_), channel_id=1, source_target_pairs={{0,48},{16,0},{32,16},{48,32},{1,49},{17,1},{33,17},{49,33},{2,50}... | collective-permute-start | bytes 491528 | tf_op jit(solution)/shard_map/ppermute | solution.py:284
  72.0 3.7 %collective-permute-start.5 = (bf16[8,40,128]{2,1,0:T(8,128)(2,1)S(1)}, bf16[8,40,128]{2,1,0:T(8,128)(2,1)S(1)}, u32[]{:S(2)}, u32[]{:S(2)}) collective-permute-start(bf16[8,40,128]{2,1,0:T(8,128)(2,1)S(1)} %slice.8.refs_0_), channel_id=1, source_target_pairs={{0,1},{1,0},{2,3},{3,2},{4,5},{5,4},{6,7},{7,6},{8,9},{9,8},{10,11... | collective-permute-start | bytes 245768 | tf_op jit(solution)/shard_map/ppermute | solution.py:285
  82.5 23.9 %copy-start.6 = (bf16[320,320]{1,0:T(8,128)(2,1)S(1)}, bf16[320,320]{1,0:T(8,128)(2,1)}, u32[]{:S(2)}) copy-start(bf16[320,320]{1,0:T(8,128)(2,1)} %attn_out.1) | copy-start | bytes 614404
  82.5 23.9 %copy-start.7 = (bf16[320,320]{1,0:T(8,128)(2,1)S(1)}, bf16[320,320]{1,0:T(8,128)(2,1)}, u32[]{:S(2)}) copy-start(bf16[320,320]{1,0:T(8,128)(2,1)} %proj_out.1) | copy-start | bytes 614404
  82.6 6.7 %collective-permute-start.6 = (f32[64,1024]{1,0:T(8,128)S(1)}, f32[64,1024]{1,0:T(8,128)S(1)}, u32[]{:S(2)}, u32[]{:S(2)}) collective-permute-start(f32[64,1024]{1,0:T(8,128)S(1)} %shard_map.142), channel_id=1, source_target_pairs={{0,1},{1,0},{2,3},{3,2},{4,5},{5,4},{6,7},{7,6},{8,9},{9,8},{10,11... | collective-permute-start | bytes 786440 | tf_op jit(solution)/shard_map/ppermute | solution.py:288

commit v7 on v6

--- a/solution.py
+++ b/solution.py
@@ -17,7 +17,6 @@
 NORM_EPS = 1e-06
 LAYER_EPS = 1e-05
 BOUND_LIMIT = 56.0
-HIGHEST = lax.Precision.HIGHEST
 F32 = jnp.float32
 BF16 = jnp.bfloat16
 VMEM = pl.BlockSpec(memory_space=pltpu.VMEM)
@@ -29,8 +28,12 @@
     return jnp.dot(a, b, preferred_element_type=F32)
 
 
-def exact_dot(a, b):
-    return jnp.dot(a, b, precision=HIGHEST, preferred_element_type=F32)
+def masked_sums(row, mask):
+    high = row.astype(BF16).astype(F32)
+    middle = (row - high).astype(BF16).astype(F32)
+    low = row - high - middle
+    parts = jnp.concatenate([high, middle, low, jnp.zeros((5, row.shape[1]), F32)], axis=0).astype(BF16)
+    return jnp.sum(dot(parts, mask), axis=0, keepdims=True)
 
 
 def call(body, out_shape, args, scratch=(), limit=24, flops=0, read=0, trans=0, smem=0):
@@ -52,7 +55,7 @@
     chan = lax.broadcasted_iota(jnp.int32, (lanes, channels), 1)
     low = (lane - first) * per_group
     inside = (chan >= low) & (chan < low + per_group) & (lane >= first) & (lane < first + GROUPS)
-    return inside.astype(F32)
+    return inside.astype(F32).astype(BF16)
 
 
 def group_gather(channels, lanes, first):
@@ -61,7 +64,7 @@
     chan = lax.broadcasted_iota(jnp.int32, (channels, lanes), 0)
     low = (lane - first) * per_group
     inside = (chan >= low) & (chan < low + per_group) & (lane >= first) & (lane < first + GROUPS)
-    return inside.astype(F32)
+    return inside.astype(F32).astype(BF16)
 
 
 def turned(ref):
@@ -109,9 +112,9 @@
     wide = merged.astype(F32)
     tokens, channels = wide.shape
     entries = tokens * (channels // GROUPS)
-    mean = exact_dot(jnp.sum(wide, axis=0, keepdims=True), gather_low[...]) / entries
-    centred = wide - exact_dot(mean, spread_low[...])
-    square = exact_dot(jnp.sum(centred * centred, axis=0, keepdims=True), gather_high[...])
+    mean = masked_sums(jnp.sum(wide, axis=0, keepdims=True), gather_low[...]) / entries
+    centred = wide - masked_sums(mean, spread_low[...])
+    square = masked_sums(jnp.sum(centred * centred, axis=0, keepdims=True), gather_high[...])
     stats_out[...] = jnp.broadcast_to(mean + square / entries, stats_out.shape)
 
 
@@ -123,8 +126,8 @@
     everyone = stats[...]
     average = jnp.mean(everyone, axis=0, keepdims=True)
     between = jnp.mean(jnp.square(everyone - average), axis=0, keepdims=True)
-    mean = exact_dot(average, spread_low[...])
-    variance = exact_dot(average, spread_high[...]) + exact_dot(between, spread_low[...])
+    mean = masked_sums(average, spread_low[...])
+    variance = masked_sums(average, spread_high[...]) + masked_sums(between, spread_low[...])
     factor = lax.rsqrt(variance + NORM_EPS)
     grouped = ((merged[...].astype(F32) - mean) * factor * group_gain[...].reshape(1, channels)).astype(BF16)
     inner = dot(grouped, proj_in[...]).astype(BF16)
@@ -252,7 +255,7 @@
     odd = lax.ppermute(hint, SEQ, ends + [(b, a) for a, b in ends])
     pair = lax.ppermute(hint, "c", swap)
     masks = call(
-        masks_body, [shape((channels, 128), F32)] * 2 + [shape((128, channels), F32)] * 2, (), flops=2000000000
+        masks_body, [shape((channels, 128), BF16)] * 2 + [shape((128, channels), BF16)] * 2, (), flops=2000000000
     )
     partial, odd_weight, features = call(
         own_row_body,
@@ -284,7 +287,8 @@
     pieces = [lax.ppermute(pair, "x", ring(by)) for by in (chips - 1, 2, 1)]
     others = lax.ppermute(queries, "c", swap)
     state = attend([queries], [pair], None, head_dim)
-    (theirs,) = attend([others], [pair, *pieces], None, head_dim)
+    other_state = attend([others], [pair], None, head_dim)
+    (theirs,) = attend([others], pieces, other_state, head_dim)
     back = lax.ppermute(theirs, "c", swap)
     (mine,) = attend([queries], pieces, state, head_dim)
     result = call(

time: 108 us -> 108 us (level)
  blocking collectives: 69.3 us -> 65.6 us
  local copies, waits for them, and re-layouts: 0.1 us -> 2.31 us
  Pallas kernels: 17.1 us -> 18.6 us
    all_to_all x1, blocking collectives: 33.5 us -> 30.9 us  [local(): stats = lax.all_to_all(stats, SEQ, 0, 0, tiled=True)]
    unnamed x28 -> x32, local copies, waits for them, and re-layouts: 0.08 us -> 2.29 us
    pallas_call x9 -> x10, Pallas kernels: 17.1 us -> 18.6 us  [call(): pl.pallas_call(body, out_shape=out_shape, in_specs=[SMEM] * smem + [VMEM]...]
    all_to_all x1, blocking collectives: 17.1 us -> 15.9 us  [local(): lax.all_to_all(result, 'z', 0, 0, tiled=True).reshape(channels, tokens)]
  transfers between devices with their start and end apart: 7 -> 7, of which waited for: 2 -> 1; matrix products, arithmetic and copies ran while one was open for 0% -> 0% of each run, Pallas kernels for 7% -> 9%
where the time goes in v7:
time: 108 us; the launch traced here: 107 us
  blocking collectives  65.6 us (61%)
  starting transfers between devices  19.8 us (18%)
  Pallas kernels  18.6 us (17%)
  local copies, waits for them, and re-layouts  2.31 us (2%)
    all_to_all x1, blocking collectives, local(): stats = lax.all_to_all(stats, SEQ, 0, 0, tiled=True)  30.9 us
    all_to_all x1, blocking collectives, local(): received = lax.all_to_all(send, 'z', 0, 0, tiled=True)  18.8 us
    pallas_call x10, Pallas kernels, call(): pl.pallas_call(body, out_shape=out_shape, in_specs=[SMEM] * smem + [VMEM]...  18.6 us
    all_to_all x1, blocking collectives, local(): lax.all_to_all(result, 'z', 0, 0, tiled=True).reshape(channels, tokens)  15.9 us
    ppermute x3, starting transfers between devices, local(): pieces = [lax.ppermute(pair, 'x', ring(by)) for by in (chips - 1, 2, 1)]  9.36 us
    ppermute x1, starting transfers between devices, local(): pair = lax.ppermute(hint, 'c', swap)  4.57 us
    ppermute x1, starting transfers between devices, local(): back = lax.ppermute(theirs, 'c', swap)  2.55 us
    unnamed x32, local copies, waits for them, and re-layouts  2.29 us
  transfers between devices with their start and end apart: 7, of which 1 were waited for; matrix products, arithmetic and copies ran while one was open for 0% of the time, Pallas kernels for 9%

profile of v7, /device:TPU:24, one launch (start us, length us, event | category | flops | bytes accessed | tf_op | source)
XLA Modules:
  0.0 107.1 jit_solution(18014992085889541470)
XLA Ops:
  0.0 0.0 copy-start
  0.0 0.0 copy-start.8
  0.0 1.4 %collective-permute-start.1 = (bf16[320,128]{1,0:T(8,128)(2,1)}, bf16[320,128]{1,0:T(8,128)(2,1)}, u32[]{:S(2)}, u32[]{:S(2)}) collective-permute-start(bf16[320,128]{1,0:T(8,128)(2,1)} %bitcast.12), channel_id=1, source_target_pairs={{1,2},{3,4},{5,6},{7,8},{9,10},{11,12},{13,14},{15,16},{17,18},{19... | collective-permute-start | bytes 245768 | tf_op jit(solution)/shard_map/ppermute | solution.py:255
  1.4 4.6 %collective-permute-start = (bf16[320,128]{1,0:T(8,128)(2,1)}, bf16[320,128]{1,0:T(8,128)(2,1)}, u32[]{:S(2)}, u32[]{:S(2)}) collective-permute-start(bf16[320,128]{1,0:T(8,128)(2,1)} %bitcast.13), channel_id=1, source_target_pairs={{0,1},{1,0},{2,3},{3,2},{4,5},{5,4},{6,7},{7,6},{8,9},{9,8},{10,11... | collective-permute-start | bytes 245768 | tf_op jit(solution)/shard_map/ppermute | solution.py:256
  6.0 0.1 shard_map.136
  6.1 0.0 copy-start.10
  6.1 0.6 copy-done.10
  6.8 0.0 copy-start.5
  6.8 0.5 collective-permute-done.pair
  7.2 0.0 copy-done
  7.2 0.0 copy-done.8
  7.2 0.9 copy-done.9
  8.2 0.7 copy-done.12
  8.9 1.6 %shard_map.137 = (f32[128,320]{1,0:T(8,128)S(1)}, bf16[3,320,320]{2,1,0:T(8,128)(2,1)S(1)}, f32[128,320]{1,0:T(8,128)S(1)}) custom-call(s32[1]{0:T(128)} %bitcast.core, bf16[320,128]{1,0:T(8,128)(2,1)S(1)} %bitcast.14, bf16[320,128]{1,0:T(8,128)(2,1)} %collective-permute-done.pair, bf16[3,3,320,320]{3,2,1,0:T(8,128)(2,1)S(1)} %copy-done, f32[320]{0:T(512)S(1)} %copy-done.12, ...), custom_call_target="tpu_custom_call" | custom-call | flops 157286400 | bytes 2048000 | tf_op jit(solution)/shard_map/pallas_call | solution.py:41
  10.4 0.0 collective-permute-done.1.odd
  10.4 0.0 copy-done.5
  10.5 0.0 copy-done.11
  10.5 0.0 copy-done.13
  10.5 1.9 %shard_map.138 = (bf16[128,320]{1,0:T(8,128)(2,1)S(1)}, f32[64,128]{1,0:T(8,128)S(1)}) custom-call(f32[128,320]{1,0:T(8,128)S(1)} %get-tuple-element.17.partial, bf16[320,128]{1,0:T(8,128)(2,1)} %collective-permute-done.1.odd, bf16[3,320,320]{2,1,0:T(8,128)(2,1)S(1)} %get-tuple-element.18.odd_weight, bf16[320,320]{1,0:T(8,128)(2,1)S(1)} %copy-done.5, ...), custom_call_target="tpu_custom_call" | custom-call | flops 104857600 | bytes 819200 | tf_op jit(solution)/shard_map/pallas_call | solution.py:41
  12.4 30.9 %all_to_all.21 = f32[64,1,128]{2,1,0:T(1,128)S(1)} all-to-all(f32[64,1,128]{2,1,0:T(1,128)S(1)} %bitcast.15), channel_id=1, replica_groups=mesh['dp'=8,'x'=4,'z'=8,'c'=2] {'x','z','c'}, dimensions={0} | all-to-all | bytes 65536 | tf_op jit(solution)/shard_map/all_to_all | solution.py:275
  43.3 0.0 copy-done.1
  43.3 0.0 copy-done.2
  43.3 0.0 copy-done.3
  43.3 0.0 copy-done.4
  43.4 0.0 copy-done.14
  43.4 0.0 copy-done.15
  43.4 1.0 shard_map.139
  44.3 18.8 %all_to_all.22 = bf16[8,120,128]{2,1,0:T(8,128)(2,1)S(1)} all-to-all(bf16[8,120,128]{2,1,0:T(8,128)(2,1)S(1)} %get-tuple-element.25), channel_id=1, replica_groups=mesh['dp'=8,'x'=4,'z'=8,'c'=2] {'z'}, dimensions={0} | all-to-all | bytes 491520 | tf_op jit(solution)/shard_map/all_to_all | solution.py:283
  63.1 2.6 %collective-permute-start.4 = (bf16[8,80,128]{2,1,0:T(8,128)(2,1)S(1)}, bf16[8,80,128]{2,1,0:T(8,128)(2,1)S(1)}, u32[]{:S(2)}, u32[]{:S(2)}) collective-permute-start(bf16[8,80,128]{2,1,0:T(8,128)(2,1)S(1)} %slice.9.refs_1_), channel_id=1, source_target_pairs={{0,16},{16,32},{32,48},{48,0},{1,17},{17,33},{33,49},{49,1},{2,18}... | collective-permute-start | bytes 491528 | tf_op jit(solution)/shard_map/ppermute | solution.py:287
  65.7 3.8 %collective-permute-start.3 = (bf16[8,80,128]{2,1,0:T(8,128)(2,1)S(1)}, bf16[8,80,128]{2,1,0:T(8,128)(2,1)S(1)}, u32[]{:S(2)}, u32[]{:S(2)}) collective-permute-start(bf16[8,80,128]{2,1,0:T(8,128)(2,1)S(1)} %slice.9.refs_1_), channel_id=1, source_target_pairs={{0,32},{16,48},{32,0},{48,16},{1,33},{17,49},{33,1},{49,17},{2,34}... | collective-permute-start | bytes 491528 | tf_op jit(solution)/shard_map/ppermute | solution.py:287
  69.5 3.0 %collective-permute-start.2 = (bf16[8,80,128]{2,1,0:T(8,128)(2,1)S(1)}, bf16[8,80,128]{2,1,0:T(8,128)(2,1)S(1)}, u32[]{:S(2)}, u32[]{:S(2)}) collective-permute-start(bf16[8,80,128]{2,1,0:T(8,128)(2,1)S(1)} %slice.9.refs_1_), channel_id=1, source_target_pairs={{0,48},{16,0},{32,16},{48,32},{1,49},{17,1},{33,17},{49,33},{2,50}... | collective-permute-start | bytes 491528 | tf_op jit(solution)/shard_map/ppermute | solution.py:287
  72.5 1.9 %collective-permute-start.5 = (bf16[8,40,128]{2,1,0:T(8,128)(2,1)S(1)}, bf16[8,40,128]{2,1,0:T(8,128)(2,1)S(1)}, u32[]{:S(2)}, u32[]{:S(2)}) collective-permute-start(bf16[8,40,128]{2,1,0:T(8,128)(2,1)S(1)} %slice.8.refs_0_), channel_id=1, source_target_pairs={{0,1},{1,0},{2,3},{3,2},{4,5},{5,4},{6,7},{7,6},{8,9},{9,8},{10,11... | collective-permute-start | bytes 245768 | tf_op jit(solution)/shard_map/ppermute | solution.py:288
  74.5 1.8 %shard_map.140.refs_4_ = f32[64,1024]{1,0:T(8,128)S(1)} custom-call(bf16[8,40,128]{2,1,0:T(8,128)(2,1)S(1)} %slice.8.refs_0_, bf16[8,80,128]{2,1,0:T(8,128)(2,1)S(1)} %slice.9.refs_1_), custom_call_target="tpu_custom_call" | custom-call | flops 1073741824 | bytes 163840 | tf_op jit(solution)/shard_map/pallas_call | solution.py:41
  76.2 0.0 collective-permute-done.5.refs_0_
  76.2 1.8 %shard_map.142.refs_4_ = f32[64,1024]{1,0:T(8,128)S(1)} custom-call(bf16[8,40,128]{2,1,0:T(8,128)(2,1)S(1)} %collective-permute-done.5.refs_0_, bf16[8,80,128]{2,1,0:T(8,128)(2,1)S(1)} %slice.9.refs_1_), custom_call_target="tpu_custom_call" | custom-call | flops 1073741824 | bytes 163840 | tf_op jit(solution)/shard_map/pallas_call | solution.py:41
  78.0 0.0 collective-permute-done.4.refs_3_
  78.0 0.0 collective-permute-done.3.refs_2_
  78.0 0.0 collective-permute-done.2.refs_1_
  78.0 4.7 %shard_map.143 = f32[64,1024]{1,0:T(8,128)S(1)} custom-call(bf16[8,40,128]{2,1,0:T(8,128)(2,1)S(1)} %collective-permute-done.5.refs_0_, bf16[8,80,128]{2,1,0:T(8,128)(2,1)S(1)} %collective-permute-done.2.refs_1_, bf16[8,80,128]{2,1,0:T(8,128)(2,1)S(1)} %collective-permute-done.3.refs_2_, bf16[8,80,128]{2,1,0:T(8,128)(2,1)S(1)} %collective-permute-done.4.refs_3_, ...), custom_call_target="tpu_custom_call" | custom-call | flops 3221225472 | bytes 491520 | tf_op jit(solution)/shard_map/pallas_call | solution.py:41
  82.8 0.0 copy-start.6
  82.8 0.0 copy-start.7
  82.8 2.6 %collective-permute-start.6 = (f32[64,1024]{1,0:T(8,128)S(1)}, f32[64,1024]{1,0:T(8,128)S(1)}, u32[]{:S(2)}, u32[]{:S(2)}) collective-permute-start(f32[64,1024]{1,0:T(8,128)S(1)} %shard_map.143), channel_id=1, source_target_pairs={{0,1},{1,0},{2,3},{3,2},{4,5},{5,4},{6,7},{7,6},{8,9},{9,8},{10,11... | collective-permute-start | bytes 786440 | tf_op jit(solution)/shard_map/ppermute | solution.py:292
  85.4 4.6 %shard_map.141.mine = f32[64,1024]{1,0:T(8,128)S(1)} custom-call(bf16[8,40,128]{2,1,0:T(8,128)(2,1)S(1)} %slice.8.refs_0_, bf16[8,80,128]{2,1,0:T(8,128)(2,1)S(1)} %collective-permute-done.2.refs_1_, bf16[8,80,128]{2,1,0:T(8,128)(2,1)S(1)} %collective-permute-done.3.refs_2_, bf16[8,80,128]{2,1,0:T(8,128)(2,1)S(1)} %collective-permute-done.4.refs_3_, ...), custom_call_target="tpu_custom_call" | custom-call | flops 3221225472 | bytes 491520 | tf_op jit(solution)/shard_map/pallas_call | solution.py:41
  89.9 0.0 collective-permute-done.6.theirs
  90.0 15.9 %all_to_all.23 = bf16[8,40,128]{2,1,0:T(8,128)(2,1)S(1)} all-to-all(bf16[8,40,128]{2,1,0:T(8,128)(2,1)S(1)} %shard_map.144), channel_id=1, replica_groups=mesh['dp'=8,'x'=4,'z'=8,'c'=2] {'z'}, dimensions={0} | all-to-all | bytes 163840 | tf_op jit(solution)/shard_map/all_to_all | solution.py:297
  105.9 0.0 copy-done.6
  105.9 0.0 copy-done.7
  105.9 1.1 %shard_map.145 = bf16[320,128]{1,0:T(8,128)(2,1)} custom-call(bf16[320,128]{1,0:T(8,128)(2,1)S(1)} %bitcast.9, bf16[128,320]{1,0:T(8,128)(2,1)S(1)} %get-tuple-element.26.inner, bf16[128,320]{1,0:T(8,128)(2,1)S(1)} %get-tuple-element.23.merged, bf16[320,320]{1,0:T(8,128)(2,1)S(1)} %copy-done.6, bf16[320,320]{1,0:T(8,128)(2,1)S(1)} %copy-done.7), custom_call_target="tpu_custom_call" | custom-call | flops 52428800 | bytes 409600 | tf_op jit(solution)/shard_map/pallas_call | solution.py:41
  (13 shorter events, 0.1 us)
Async XLA Ops:
  0.0 7.2 %copy-start = (bf16[3,3,320,320]{3,2,1,0:T(8,128)(2,1)S(1)}, bf16[3,3,320,320]{3,2,1,0:T(8,128)(2,1)}, u32[]{:S(2)}) copy-start(bf16[3,3,320,320]{3,2,1,0:T(8,128)(2,1)} %weight.1) | copy-start | bytes 5529604
  0.0 7.2 %copy-start.8 = (bf16[128,320]{0,1:T(8,128)(2,1)S(1)}, bf16[128,320]{0,1:T(8,128)(2,1)}, u32[]{:S(2)}) copy-start(bf16[128,320]{0,1:T(8,128)(2,1)} %param.14) | copy-start | bytes 245764
  0.0 10.4 %collective-permute-start.1 = (bf16[320,128]{1,0:T(8,128)(2,1)}, bf16[320,128]{1,0:T(8,128)(2,1)}, u32[]{:S(2)}, u32[]{:S(2)}) collective-permute-start(bf16[320,128]{1,0:T(8,128)(2,1)} %bitcast.12), channel_id=1, source_target_pairs={{1,2},{3,4},{5,6},{7,8},{9,10},{11,12},{13,14},{15,16},{17,18},{19... | collective-permute-start | bytes 245768 | tf_op jit(solution)/shard_map/ppermute | solution.py:255
  1.4 5.8 %collective-permute-start = (bf16[320,128]{1,0:T(8,128)(2,1)}, bf16[320,128]{1,0:T(8,128)(2,1)}, u32[]{:S(2)}, u32[]{:S(2)}) collective-permute-start(bf16[320,128]{1,0:T(8,128)(2,1)} %bitcast.13), channel_id=1, source_target_pairs={{0,1},{1,0},{2,3},{3,2},{4,5},{5,4},{6,7},{7,6},{8,9},{9,8},{10,11... | collective-permute-start | bytes 245768 | tf_op jit(solution)/shard_map/ppermute | solution.py:256
  6.1 0.6 copy-start.10
  6.7 36.6 %copy-start.1 = (bf16[320,320]{1,0:T(8,128)(2,1)S(1)}, bf16[320,320]{1,0:T(8,128)(2,1)}, u32[]{:S(2)}) copy-start(bf16[320,320]{1,0:T(8,128)(2,1)} %proj_in.1) | copy-start | bytes 614404
  6.7 36.6 %copy-start.2 = (bf16[320,320]{1,0:T(8,128)(2,1)S(1)}, bf16[320,320]{1,0:T(8,128)(2,1)}, u32[]{:S(2)}) copy-start(bf16[320,320]{1,0:T(8,128)(2,1)} %wq.1) | copy-start | bytes 614404
  6.7 36.6 %copy-start.3 = (bf16[320,320]{1,0:T(8,128)(2,1)S(1)}, bf16[320,320]{1,0:T(8,128)(2,1)}, u32[]{:S(2)}) copy-start(bf16[320,320]{1,0:T(8,128)(2,1)} %wk.1) | copy-start | bytes 614404
  6.7 36.6 %copy-start.4 = (bf16[320,320]{1,0:T(8,128)(2,1)S(1)}, bf16[320,320]{1,0:T(8,128)(2,1)}, u32[]{:S(2)}) copy-start(bf16[320,320]{1,0:T(8,128)(2,1)} %wv.1) | copy-start | bytes 614404
  6.8 3.7 %copy-start.5 = (bf16[320,320]{1,0:T(8,128)(2,1)S(1)}, bf16[320,320]{1,0:T(8,128)(2,1)}, u32[]{:S(2)}) copy-start(bf16[320,320]{1,0:T(8,128)(2,1)} %zero_weight.1) | copy-start | bytes 614404
  7.2 0.9 copy-start.9
  8.2 0.7 copy-start.12
  8.8 1.6 %copy-start.11 = (bf16[320,128]{1,0:T(8,128)(2,1)S(1)}, bf16[320,128]{1,0:T(8,128)(2,1)}, u32[]{:S(2)}) copy-start(bf16[320,128]{1,0:T(8,128)(2,1)} %copy-done.10) | copy-start | bytes 245764
  8.9 1.6 %copy-start.13 = (f32[320]{0:T(512)S(1)}, f32[320]{0:T(512)}, u32[]{:S(2)}) copy-start(f32[320]{0:T(512)} %zero_bias.1) | copy-start | bytes 3844
  8.9 34.5 %copy-start.14 = (f32[320]{0:T(512)S(1)}, f32[320]{0:T(512)}, u32[]{:S(2)}) copy-start(f32[320]{0:T(512)} %group_gain.1) | copy-start | bytes 3844
  8.9 34.5 %copy-start.15 = (f32[320]{0:T(512)S(1)}, f32[320]{0:T(512)}, u32[]{:S(2)}) copy-start(f32[320]{0:T(512)} %norm_gain.1) | copy-start | bytes 3844
  63.1 14.9 %collective-permute-start.4 = (bf16[8,80,128]{2,1,0:T(8,128)(2,1)S(1)}, bf16[8,80,128]{2,1,0:T(8,128)(2,1)S(1)}, u32[]{:S(2)}, u32[]{:S(2)}) collective-permute-start(bf16[8,80,128]{2,1,0:T(8,128)(2,1)S(1)} %slice.9.refs_1_), channel_id=1, source_target_pairs={{0,16},{16,32},{32,48},{48,0},{1,17},{17,33},{33,49},{49,1},{2,18}... | collective-permute-start | bytes 491528 | tf_op jit(solution)/shard_map/ppermute | solution.py:287
  65.7 12.3 %collective-permute-start.3 = (bf16[8,80,128]{2,1,0:T(8,128)(2,1)S(1)}, bf16[8,80,128]{2,1,0:T(8,128)(2,1)S(1)}, u32[]{:S(2)}, u32[]{:S(2)}) collective-permute-start(bf16[8,80,128]{2,1,0:T(8,128)(2,1)S(1)} %slice.9.refs_1_), channel_id=1, source_target_pairs={{0,32},{16,48},{32,0},{48,16},{1,33},{17,49},{33,1},{49,17},{2,34}... | collective-permute-start | bytes 491528 | tf_op jit(solution)/shard_map/ppermute | solution.py:287
  69.5 8.5 %collective-permute-start.2 = (bf16[8,80,128]{2,1,0:T(8,128)(2,1)S(1)}, bf16[8,80,128]{2,1,0:T(8,128)(2,1)S(1)}, u32[]{:S(2)}, u32[]{:S(2)}) collective-permute-start(bf16[8,80,128]{2,1,0:T(8,128)(2,1)S(1)} %slice.9.refs_1_), channel_id=1, source_target_pairs={{0,48},{16,0},{32,16},{48,32},{1,49},{17,1},{33,17},{49,33},{2,50}... | collective-permute-start | bytes 491528 | tf_op jit(solution)/shard_map/ppermute | solution.py:287
  72.5 3.7 %collective-permute-start.5 = (bf16[8,40,128]{2,1,0:T(8,128)(2,1)S(1)}, bf16[8,40,128]{2,1,0:T(8,128)(2,1)S(1)}, u32[]{:S(2)}, u32[]{:S(2)}) collective-permute-start(bf16[8,40,128]{2,1,0:T(8,128)(2,1)S(1)} %slice.8.refs_0_), channel_id=1, source_target_pairs={{0,1},{1,0},{2,3},{3,2},{4,5},{5,4},{6,7},{7,6},{8,9},{9,8},{10,11... | collective-permute-start | bytes 245768 | tf_op jit(solution)/shard_map/ppermute | solution.py:288
  82.8 23.2 %copy-start.6 = (bf16[320,320]{1,0:T(8,128)(2,1)S(1)}, bf16[320,320]{1,0:T(8,128)(2,1)}, u32[]{:S(2)}) copy-start(bf16[320,320]{1,0:T(8,128)(2,1)} %attn_out.1) | copy-start | bytes 614404
  82.8 23.2 %copy-start.7 = (bf16[320,320]{1,0:T(8,128)(2,1)S(1)}, bf16[320,320]{1,0:T(8,128)(2,1)}, u32[]{:S(2)}) copy-start(bf16[320,320]{1,0:T(8,128)(2,1)} %proj_out.1) | copy-start | bytes 614404
  82.8 7.1 %collective-permute-start.6 = (f32[64,1024]{1,0:T(8,128)S(1)}, f32[64,1024]{1,0:T(8,128)S(1)}, u32[]{:S(2)}, u32[]{:S(2)}) collective-permute-start(f32[64,1024]{1,0:T(8,128)S(1)} %shard_map.143), channel_id=1, source_target_pairs={{0,1},{1,0},{2,3},{3,2},{4,5},{5,4},{6,7},{7,6},{8,9},{9,8},{10,11... | collective-permute-start | bytes 786440 | tf_op jit(solution)/shard_map/ppermute | solution.py:292

commit v8 on v7

--- a/solution.py
+++ b/solution.py
@@ -255,7 +255,7 @@
     odd = lax.ppermute(hint, SEQ, ends + [(b, a) for a, b in ends])
     pair = lax.ppermute(hint, "c", swap)
     masks = call(
-        masks_body, [shape((channels, 128), BF16)] * 2 + [shape((128, channels), BF16)] * 2, (), flops=2000000000
+        masks_body, [shape((channels, 128), BF16)] * 2 + [shape((128, channels), BF16)] * 2, (), flops=1000000000
     )
     partial, odd_weight, features = call(
         own_row_body,
@@ -287,8 +287,8 @@
     pieces = [lax.ppermute(pair, "x", ring(by)) for by in (chips - 1, 2, 1)]
     others = lax.ppermute(queries, "c", swap)
     state = attend([queries], [pair], None, head_dim)
-    other_state = attend([others], [pair], None, head_dim)
-    (theirs,) = attend([others], pieces, other_state, head_dim)
+    other_state = attend([others], [pair, pieces[2]], None, head_dim)
+    (theirs,) = attend([others], pieces[:2], other_state, head_dim)
     back = lax.ppermute(theirs, "c", swap)
     (mine,) = attend([queries], pieces, state, head_dim)
     result = call(

time: 108 us -> 105 us (0.972)
  local copies, waits for them, and re-layouts: 2.31 us -> 0.09 us
  Pallas kernels: 18.6 us -> 16.7 us
  blocking collectives: 65.6 us -> 66.7 us
    all_to_all x1, blocking collectives: 30.9 us -> 33.5 us  [local(): stats = lax.all_to_all(stats, SEQ, 0, 0, tiled=True)]
    unnamed x32 -> x28, local copies, waits for them, and re-layouts: 2.29 us -> 0.07 us
    pallas_call x10, Pallas kernels: 18.6 us -> 16.7 us  [call(): pl.pallas_call(body, out_shape=out_shape, in_specs=[SMEM] * smem + [VMEM]...]
    all_to_all x1, blocking collectives: 15.9 us -> 14.4 us  [local(): lax.all_to_all(result, 'z', 0, 0, tiled=True).reshape(channels, tokens)]
  transfers between devices with their start and end apart: 7 -> 7, of which waited for: 1 -> 1; matrix products, arithmetic and copies ran while one was open for 0% -> 0% of each run, Pallas kernels for 9% -> 10%
where the time goes in v8:
time: 105 us
  blocking collectives  66.7 us (64%)
  starting transfers between devices  19.8 us (19%)
  Pallas kernels  16.7 us (16%)
    all_to_all x1, blocking collectives, local(): stats = lax.all_to_all(stats, SEQ, 0, 0, tiled=True)  33.5 us
    all_to_all x1, blocking collectives, local(): received = lax.all_to_all(send, 'z', 0, 0, tiled=True)  18.8 us
    pallas_call x10, Pallas kernels, call(): pl.pallas_call(body, out_shape=out_shape, in_specs=[SMEM] * smem + [VMEM]...  16.7 us
    all_to_all x1, blocking collectives, local(): lax.all_to_all(result, 'z', 0, 0, tiled=True).reshape(channels, tokens)  14.4 us
    ppermute x3, starting transfers between devices, local(): pieces = [lax.ppermute(pair, 'x', ring(by)) for by in (chips - 1, 2, 1)]  9.36 us
    ppermute x1, starting transfers between devices, local(): pair = lax.ppermute(hint, 'c', swap)  5.18 us
    ppermute x1, starting transfers between devices, local(): back = lax.ppermute(theirs, 'c', swap)  2.53 us
  transfers between devices with their start and end apart: 7, of which 1 were waited for; matrix products, arithmetic and copies ran while one was open for 0% of the time, Pallas kernels for 10%

profile of v8, /device:TPU:24, one launch (start us, length us, event | category | flops | bytes accessed | tf_op | source)
XLA Modules:
  0.0 104.5 jit_solution(8747645428649427247)
XLA Ops:
  0.0 0.0 copy-start.8
  0.0 0.8 collective-permute-start.1
  0.8 5.2 %collective-permute-start = (bf16[320,128]{1,0:T(8,128)(2,1)}, bf16[320,128]{1,0:T(8,128)(2,1)S(1)}, u32[]{:S(2)}, u32[]{:S(2)}) collective-permute-start(bf16[320,128]{1,0:T(8,128)(2,1)} %bitcast.13), channel_id=1, source_target_pairs={{0,1},{1,0},{2,3},{3,2},{4,5},{5,4},{6,7},{7,6},{8,9},{9,8},{10,11... | collective-permute-start | bytes 245768 | tf_op jit(solution)/shard_map/ppermute | solution.py:256
  6.0 0.0 copy-start.5
  6.0 0.0 copy-start.11
  6.0 0.1 shard_map.136
  6.1 0.0 copy-start.1
  6.2 0.0 copy-start.2
  6.2 0.0 copy-start.3
  6.2 0.0 copy-start.4
  6.2 0.0 copy-start.12
  6.2 0.0 copy-start.13
  6.2 0.9 collective-permute-done.pair
  7.1 0.0 copy-done.9
  7.1 0.0 copy-done.10
  7.1 0.0 copy-done
  7.1 0.0 copy-done.8
  7.1 0.6 shard_map.137
  7.8 0.0 collective-permute-done.1.odd
  7.8 0.0 copy-done.5
  7.8 0.0 copy-done.11
  7.8 1.1 %shard_map.138 = (bf16[128,320]{1,0:T(8,128)(2,1)S(1)}, f32[64,128]{1,0:T(8,128)S(1)}) custom-call(f32[128,320]{1,0:T(8,128)S(1)} %get-tuple-element.17.partial, bf16[320,128]{1,0:T(8,128)(2,1)S(1)} %collective-permute-done.1.odd, bf16[3,320,320]{2,1,0:T(8,128)(2,1)S(1)} %get-tuple-element.18.odd_weight, bf16[320,320]{1,0:T(8,128)(2,1)S(1)} %copy-done.5, ...), custom_call_target="tpu_custom_call" | custom-call | flops 104857600 | bytes 819200 | tf_op jit(solution)/shard_map/pallas_call | solution.py:41
  8.8 33.5 %all_to_all.21 = f32[64,1,128]{2,1,0:T(1,128)S(1)} all-to-all(f32[64,1,128]{2,1,0:T(1,128)S(1)} %bitcast.15), channel_id=1, replica_groups=mesh['dp'=8,'x'=4,'z'=8,'c'=2] {'x','z','c'}, dimensions={0} | all-to-all | bytes 65536 | tf_op jit(solution)/shard_map/all_to_all | solution.py:275
  42.4 0.0 copy-done.1
  42.4 0.0 copy-done.2
  42.4 0.0 copy-done.3
  42.4 0.0 copy-done.4
  42.4 0.0 copy-done.12
  42.4 1.0 shard_map.139
  43.4 18.8 %all_to_all.22 = bf16[8,120,128]{2,1,0:T(8,128)(2,1)S(1)} all-to-all(bf16[8,120,128]{2,1,0:T(8,128)(2,1)S(1)} %get-tuple-element.25), channel_id=1, replica_groups=mesh['dp'=8,'x'=4,'z'=8,'c'=2] {'z'}, dimensions={0} | all-to-all | bytes 491520 | tf_op jit(solution)/shard_map/all_to_all | solution.py:283
  62.1 2.6 %collective-permute-start.4 = (bf16[8,80,128]{2,1,0:T(8,128)(2,1)S(1)}, bf16[8,80,128]{2,1,0:T(8,128)(2,1)S(1)}, u32[]{:S(2)}, u32[]{:S(2)}) collective-permute-start(bf16[8,80,128]{2,1,0:T(8,128)(2,1)S(1)} %slice.9.refs_1_), channel_id=1, source_target_pairs={{0,16},{16,32},{32,48},{48,0},{1,17},{17,33},{33,49},{49,1},{2,18}... | collective-permute-start | bytes 491528 | tf_op jit(solution)/shard_map/ppermute | solution.py:287
  64.7 3.8 %collective-permute-start.3 = (bf16[8,80,128]{2,1,0:T(8,128)(2,1)S(1)}, bf16[8,80,128]{2,1,0:T(8,128)(2,1)S(1)}, u32[]{:S(2)}, u32[]{:S(2)}) collective-permute-start(bf16[8,80,128]{2,1,0:T(8,128)(2,1)S(1)} %slice.9.refs_1_), channel_id=1, source_target_pairs={{0,32},{16,48},{32,0},{48,16},{1,33},{17,49},{33,1},{49,17},{2,34}... | collective-permute-start | bytes 491528 | tf_op jit(solution)/shard_map/ppermute | solution.py:287
  68.5 3.0 %collective-permute-start.2 = (bf16[8,80,128]{2,1,0:T(8,128)(2,1)S(1)}, bf16[8,80,128]{2,1,0:T(8,128)(2,1)S(1)}, u32[]{:S(2)}, u32[]{:S(2)}) collective-permute-start(bf16[8,80,128]{2,1,0:T(8,128)(2,1)S(1)} %slice.9.refs_1_), channel_id=1, source_target_pairs={{0,48},{16,0},{32,16},{48,32},{1,49},{17,1},{33,17},{49,33},{2,50}... | collective-permute-start | bytes 491528 | tf_op jit(solution)/shard_map/ppermute | solution.py:287
  71.5 1.9 %collective-permute-start.5 = (bf16[8,40,128]{2,1,0:T(8,128)(2,1)S(1)}, bf16[8,40,128]{2,1,0:T(8,128)(2,1)S(1)}, u32[]{:S(2)}, u32[]{:S(2)}) collective-permute-start(bf16[8,40,128]{2,1,0:T(8,128)(2,1)S(1)} %slice.8.refs_0_), channel_id=1, source_target_pairs={{0,1},{1,0},{2,3},{3,2},{4,5},{5,4},{6,7},{7,6},{8,9},{9,8},{10,11... | collective-permute-start | bytes 245768 | tf_op jit(solution)/shard_map/ppermute | solution.py:288
  73.5 1.8 %shard_map.140.refs_4_ = f32[64,1024]{1,0:T(8,128)S(1)} custom-call(bf16[8,40,128]{2,1,0:T(8,128)(2,1)S(1)} %slice.8.refs_0_, bf16[8,80,128]{2,1,0:T(8,128)(2,1)S(1)} %slice.9.refs_1_), custom_call_target="tpu_custom_call" | custom-call | flops 1073741824 | bytes 163840 | tf_op jit(solution)/shard_map/pallas_call | solution.py:41
  75.2 0.0 collective-permute-done.5.refs_0_
  75.2 0.0 collective-permute-done.4.refs_3_.refs_2_
  75.3 3.2 %shard_map.142.refs_3_ = f32[64,1024]{1,0:T(8,128)S(1)} custom-call(bf16[8,40,128]{2,1,0:T(8,128)(2,1)S(1)} %collective-permute-done.5.refs_0_, bf16[8,80,128]{2,1,0:T(8,128)(2,1)S(1)} %slice.9.refs_1_, bf16[8,80,128]{2,1,0:T(8,128)(2,1)S(1)} %collective-permute-done.4.refs_3_.refs_2_), custom_call_target="tpu_custom_call" | custom-call | flops 2147483648 | bytes 327680 | tf_op jit(solution)/shard_map/pallas_call | solution.py:41
  78.4 0.0 collective-permute-done.3.refs_2_
  78.4 0.0 collective-permute-done.2.refs_1_
  78.4 3.3 %shard_map.143 = f32[64,1024]{1,0:T(8,128)S(1)} custom-call(bf16[8,40,128]{2,1,0:T(8,128)(2,1)S(1)} %collective-permute-done.5.refs_0_, bf16[8,80,128]{2,1,0:T(8,128)(2,1)S(1)} %collective-permute-done.2.refs_1_, bf16[8,80,128]{2,1,0:T(8,128)(2,1)S(1)} %collective-permute-done.3.refs_2_, f32[64,1024]{1,0:T(8,128)S(1)} %shard_map.142.refs_3_), custom_call_target="tpu_custom_call" | custom-call | flops 2147483648 | bytes 327680 | tf_op jit(solution)/shard_map/pallas_call | solution.py:41
  81.7 0.0 copy-start.6
  81.8 0.0 copy-start.7
  81.8 2.5 %collective-permute-start.6 = (f32[64,1024]{1,0:T(8,128)S(1)}, f32[64,1024]{1,0:T(8,128)S(1)}, u32[]{:S(2)}, u32[]{:S(2)}) collective-permute-start(f32[64,1024]{1,0:T(8,128)S(1)} %shard_map.143), channel_id=1, source_target_pairs={{0,1},{1,0},{2,3},{3,2},{4,5},{5,4},{6,7},{7,6},{8,9},{9,8},{10,11... | collective-permute-start | bytes 786440 | tf_op jit(solution)/shard_map/ppermute | solution.py:292
  84.3 4.6 %shard_map.141.mine = f32[64,1024]{1,0:T(8,128)S(1)} custom-call(bf16[8,40,128]{2,1,0:T(8,128)(2,1)S(1)} %slice.8.refs_0_, bf16[8,80,128]{2,1,0:T(8,128)(2,1)S(1)} %collective-permute-done.2.refs_1_, bf16[8,80,128]{2,1,0:T(8,128)(2,1)S(1)} %collective-permute-done.3.refs_2_, bf16[8,80,128]{2,1,0:T(8,128)(2,1)S(1)} %collective-permute-done.4.refs_3_.refs_2_, ...), custom_call_target="tpu_custom_call" | custom-call | flops 3221225472 | bytes 491520 | tf_op jit(solution)/shard_map/pallas_call | solution.py:41
  88.9 0.0 collective-permute-done.6.theirs
  89.0 14.4 %all_to_all.23 = bf16[8,40,128]{2,1,0:T(8,128)(2,1)S(1)} all-to-all(bf16[8,40,128]{2,1,0:T(8,128)(2,1)S(1)} %shard_map.144), channel_id=1, replica_groups=mesh['dp'=8,'x'=4,'z'=8,'c'=2] {'z'}, dimensions={0} | all-to-all | bytes 163840 | tf_op jit(solution)/shard_map/all_to_all | solution.py:297
  103.4 1.1 %shard_map.145 = bf16[320,128]{1,0:T(8,128)(2,1)} custom-call(bf16[320,128]{1,0:T(8,128)(2,1)S(1)} %bitcast.9, bf16[128,320]{1,0:T(8,128)(2,1)S(1)} %get-tuple-element.26.inner, bf16[128,320]{1,0:T(8,128)(2,1)S(1)} %get-tuple-element.23.merged, bf16[320,320]{1,0:T(8,128)(2,1)S(1)} %copy-done.6, bf16[320,320]{1,0:T(8,128)(2,1)S(1)} %copy-done.7), custom_call_target="tpu_custom_call" | custom-call | flops 52428800 | bytes 409600 | tf_op jit(solution)/shard_map/pallas_call | solution.py:41
  (9 shorter events, 0.1 us)
Async XLA Ops:
  0.0 7.1 %copy-start.9 = (bf16[128,320]{0,1:T(8,128)(2,1)S(1)}, bf16[128,320]{0,1:T(8,128)(2,1)}, u32[]{:S(2)}) copy-start(bf16[128,320]{0,1:T(8,128)(2,1)} %param.15) | copy-start | bytes 245764
  0.0 7.1 %copy-start.10 = (f32[320]{0:T(512)S(1)}, f32[320]{0:T(512)}, u32[]{:S(2)}) copy-start(f32[320]{0:T(512)} %bias.1) | copy-start | bytes 3844
  0.0 7.1 %copy-start = (bf16[3,3,320,320]{3,2,1,0:T(8,128)(2,1)S(1)}, bf16[3,3,320,320]{3,2,1,0:T(8,128)(2,1)}, u32[]{:S(2)}) copy-start(bf16[3,3,320,320]{3,2,1,0:T(8,128)(2,1)} %weight.1) | copy-start | bytes 5529604
  0.0 7.1 %copy-start.8 = (bf16[128,320]{0,1:T(8,128)(2,1)S(1)}, bf16[128,320]{0,1:T(8,128)(2,1)}, u32[]{:S(2)}) copy-start(bf16[128,320]{0,1:T(8,128)(2,1)} %param.14) | copy-start | bytes 245764
  0.0 7.7 %collective-permute-start.1 = (bf16[320,128]{1,0:T(8,128)(2,1)}, bf16[320,128]{1,0:T(8,128)(2,1)S(1)}, u32[]{:S(2)}, u32[]{:S(2)}) collective-permute-start(bf16[320,128]{1,0:T(8,128)(2,1)} %bitcast.12), channel_id=1, source_target_pairs={{1,2},{3,4},{5,6},{7,8},{9,10},{11,12},{13,14},{15,16},{17,18},{19... | collective-permute-start | bytes 245768 | tf_op jit(solution)/shard_map/ppermute | solution.py:255
  0.8 6.3 %collective-permute-start = (bf16[320,128]{1,0:T(8,128)(2,1)}, bf16[320,128]{1,0:T(8,128)(2,1)S(1)}, u32[]{:S(2)}, u32[]{:S(2)}) collective-permute-start(bf16[320,128]{1,0:T(8,128)(2,1)} %bitcast.13), channel_id=1, source_target_pairs={{0,1},{1,0},{2,3},{3,2},{4,5},{5,4},{6,7},{7,6},{8,9},{9,8},{10,11... | collective-permute-start | bytes 245768 | tf_op jit(solution)/shard_map/ppermute | solution.py:256
  6.0 1.7 %copy-start.5 = (bf16[320,320]{1,0:T(8,128)(2,1)S(1)}, bf16[320,320]{1,0:T(8,128)(2,1)}, u32[]{:S(2)}) copy-start(bf16[320,320]{1,0:T(8,128)(2,1)} %zero_weight.1) | copy-start | bytes 614404
  6.0 1.7 %copy-start.11 = (f32[320]{0:T(512)S(1)}, f32[320]{0:T(512)}, u32[]{:S(2)}) copy-start(f32[320]{0:T(512)} %zero_bias.1) | copy-start | bytes 3844
  6.1 36.2 %copy-start.1 = (bf16[320,320]{1,0:T(8,128)(2,1)S(1)}, bf16[320,320]{1,0:T(8,128)(2,1)}, u32[]{:S(2)}) copy-start(bf16[320,320]{1,0:T(8,128)(2,1)} %proj_in.1) | copy-start | bytes 614404
  6.2 36.2 %copy-start.2 = (bf16[320,320]{1,0:T(8,128)(2,1)S(1)}, bf16[320,320]{1,0:T(8,128)(2,1)}, u32[]{:S(2)}) copy-start(bf16[320,320]{1,0:T(8,128)(2,1)} %wq.1) | copy-start | bytes 614404
  6.2 36.2 %copy-start.3 = (bf16[320,320]{1,0:T(8,128)(2,1)S(1)}, bf16[320,320]{1,0:T(8,128)(2,1)}, u32[]{:S(2)}) copy-start(bf16[320,320]{1,0:T(8,128)(2,1)} %wk.1) | copy-start | bytes 614404
  6.2 36.2 %copy-start.4 = (bf16[320,320]{1,0:T(8,128)(2,1)S(1)}, bf16[320,320]{1,0:T(8,128)(2,1)}, u32[]{:S(2)}) copy-start(bf16[320,320]{1,0:T(8,128)(2,1)} %wv.1) | copy-start | bytes 614404
  6.2 36.2 %copy-start.12 = (f32[320]{0:T(512)S(1)}, f32[320]{0:T(512)}, u32[]{:S(2)}) copy-start(f32[320]{0:T(512)} %group_gain.1) | copy-start | bytes 3844
  6.2 36.2 %copy-start.13 = (f32[320]{0:T(512)S(1)}, f32[320]{0:T(512)}, u32[]{:S(2)}) copy-start(f32[320]{0:T(512)} %norm_gain.1) | copy-start | bytes 3844
  62.1 13.1 %collective-permute-start.4 = (bf16[8,80,128]{2,1,0:T(8,128)(2,1)S(1)}, bf16[8,80,128]{2,1,0:T(8,128)(2,1)S(1)}, u32[]{:S(2)}, u32[]{:S(2)}) collective-permute-start(bf16[8,80,128]{2,1,0:T(8,128)(2,1)S(1)} %slice.9.refs_1_), channel_id=1, source_target_pairs={{0,16},{16,32},{32,48},{48,0},{1,17},{17,33},{33,49},{49,1},{2,18}... | collective-permute-start | bytes 491528 | tf_op jit(solution)/shard_map/ppermute | solution.py:287
  64.7 13.7 %collective-permute-start.3 = (bf16[8,80,128]{2,1,0:T(8,128)(2,1)S(1)}, bf16[8,80,128]{2,1,0:T(8,128)(2,1)S(1)}, u32[]{:S(2)}, u32[]{:S(2)}) collective-permute-start(bf16[8,80,128]{2,1,0:T(8,128)(2,1)S(1)} %slice.9.refs_1_), channel_id=1, source_target_pairs={{0,32},{16,48},{32,0},{48,16},{1,33},{17,49},{33,1},{49,17},{2,34}... | collective-permute-start | bytes 491528 | tf_op jit(solution)/shard_map/ppermute | solution.py:287
  68.5 9.9 %collective-permute-start.2 = (bf16[8,80,128]{2,1,0:T(8,128)(2,1)S(1)}, bf16[8,80,128]{2,1,0:T(8,128)(2,1)S(1)}, u32[]{:S(2)}, u32[]{:S(2)}) collective-permute-start(bf16[8,80,128]{2,1,0:T(8,128)(2,1)S(1)} %slice.9.refs_1_), channel_id=1, source_target_pairs={{0,48},{16,0},{32,16},{48,32},{1,49},{17,1},{33,17},{49,33},{2,50}... | collective-permute-start | bytes 491528 | tf_op jit(solution)/shard_map/ppermute | solution.py:287
  71.5 3.7 %collective-permute-start.5 = (bf16[8,40,128]{2,1,0:T(8,128)(2,1)S(1)}, bf16[8,40,128]{2,1,0:T(8,128)(2,1)S(1)}, u32[]{:S(2)}, u32[]{:S(2)}) collective-permute-start(bf16[8,40,128]{2,1,0:T(8,128)(2,1)S(1)} %slice.8.refs_0_), channel_id=1, source_target_pairs={{0,1},{1,0},{2,3},{3,2},{4,5},{5,4},{6,7},{7,6},{8,9},{9,8},{10,11... | collective-permute-start | bytes 245768 | tf_op jit(solution)/shard_map/ppermute | solution.py:288
  81.7 21.6 %copy-start.6 = (bf16[320,320]{1,0:T(8,128)(2,1)S(1)}, bf16[320,320]{1,0:T(8,128)(2,1)}, u32[]{:S(2)}) copy-start(bf16[320,320]{1,0:T(8,128)(2,1)} %attn_out.1) | copy-start | bytes 614404
  81.8 21.6 %copy-start.7 = (bf16[320,320]{1,0:T(8,128)(2,1)S(1)}, bf16[320,320]{1,0:T(8,128)(2,1)}, u32[]{:S(2)}) copy-start(bf16[320,320]{1,0:T(8,128)(2,1)} %proj_out.1) | copy-start | bytes 614404
  81.8 7.1 %collective-permute-start.6 = (f32[64,1024]{1,0:T(8,128)S(1)}, f32[64,1024]{1,0:T(8,128)S(1)}, u32[]{:S(2)}, u32[]{:S(2)}) collective-permute-start(f32[64,1024]{1,0:T(8,128)S(1)} %shard_map.143), channel_id=1, source_target_pairs={{0,1},{1,0},{2,3},{3,2},{4,5},{5,4},{6,7},{7,6},{8,9},{9,8},{10,11... | collective-permute-start | bytes 786440 | tf_op jit(solution)/shard_map/ppermute | solution.py:292

commit v9 on v8

--- a/solution.py
+++ b/solution.py
@@ -272,7 +272,11 @@
         flops=2 * tokens * channels * channels * 4,
         read=4 * channels * channels * 2,
     )
-    stats = lax.all_to_all(stats, SEQ, 0, 0, tiled=True)
+    chain = range(lax.axis_size("z"))
+    folded = [[*chain[::2], *chain[1::2][::-1]]]
+    lines, cores = lax.axis_size("x"), lax.axis_size("c")
+    whole = [[(x * len(chain) + z) * cores + c for x in range(lines) for z in folded[0] for c in range(cores)]]
+    stats = lax.all_to_all(stats, SEQ, 0, 0, axis_index_groups=whole, tiled=True)
     inner, send = call(
         project_body,
         [shape((tokens, channels), BF16), shape((HEADS, 3 * head_dim, tokens), BF16)],
@@ -280,7 +284,7 @@
         flops=2 * tokens * channels * channels * 4,
         read=4 * channels * channels * 2,
     )
-    received = lax.all_to_all(send, "z", 0, 0, tiled=True)
+    received = lax.all_to_all(send, "z", 0, 0, axis_index_groups=folded, tiled=True)
     queries, pair = received[:, :head_dim, :], received[:, head_dim:, :]
     chips = lax.axis_size("x")
     ring = lambda by: [(i, (i + by) % chips) for i in range(chips)]
@@ -294,7 +298,7 @@
     result = call(
         functools.partial(combine_body, head_dim), shape((HEADS, head_dim, tokens), BF16), (mine, back)
     )
-    attended = lax.all_to_all(result, "z", 0, 0, tiled=True).reshape(channels, tokens)
+    attended = lax.all_to_all(result, "z", 0, 0, axis_index_groups=folded, tiled=True).reshape(channels, tokens)
     return call(
         finish_body,
         shape((channels, tokens), BF16),

time: 105 us -> 105 us (level)
  no operation moved by 1% of the time
where the time goes in v9:
time: 105 us
  blocking collectives  67.1 us (64%)
  starting transfers between devices  20.2 us (19%)
  Pallas kernels  16.7 us (16%)
    all_to_all x1, blocking collectives, local(): lax.all_to_all(stats, SEQ, 0, 0, axis_index_groups=whole, tiled=True)  33.3 us
    all_to_all x1, blocking collectives, local(): lax.all_to_all(send, 'z', 0, 0, axis_index_groups=folded, tiled=True)  18.4 us
    pallas_call x10, Pallas kernels, call(): pl.pallas_call(body, out_shape=out_shape, in_specs=[SMEM] * smem + [VMEM]...  16.7 us
    all_to_all x1, blocking collectives, local(): lax.all_to_all(result, 'z', 0, 0, axis_index_groups=folded, tiled=True)  15.4 us
    ppermute x3, starting transfers between devices, local(): pieces = [lax.ppermute(pair, 'x', ring(by)) for by in (chips - 1, 2, 1)]  9.72 us
    ppermute x1, starting transfers between devices, local(): pair = lax.ppermute(hint, 'c', swap)  5.18 us
    ppermute x1, starting transfers between devices, local(): back = lax.ppermute(theirs, 'c', swap)  2.56 us
  transfers between devices with their start and end apart: 7, of which 1 were waited for; matrix products, arithmetic and copies ran while one was open for 0% of the time, Pallas kernels for 10%

profile of v9, /device:TPU:24, one launch (start us, length us, event | category | flops | bytes accessed | tf_op | source)
XLA Modules:
  0.0 105.3 jit_solution(4280932080051358219)
XLA Ops:
  0.0 0.0 copy-start.8
  0.0 0.8 collective-permute-start.1
  0.8 5.2 %collective-permute-start = (bf16[320,128]{1,0:T(8,128)(2,1)}, bf16[320,128]{1,0:T(8,128)(2,1)S(1)}, u32[]{:S(2)}, u32[]{:S(2)}) collective-permute-start(bf16[320,128]{1,0:T(8,128)(2,1)} %bitcast.13), channel_id=1, source_target_pairs={{0,1},{1,0},{2,3},{3,2},{4,5},{5,4},{6,7},{7,6},{8,9},{9,8},{10,11... | collective-permute-start | bytes 245768 | tf_op jit(solution)/shard_map/ppermute | solution.py:256
  6.0 0.0 copy-start.5
  6.0 0.0 copy-start.11
  6.0 0.1 shard_map.136
  6.1 0.0 copy-start.1
  6.2 0.0 copy-start.2
  6.2 0.0 copy-start.3
  6.2 0.0 copy-start.4
  6.2 0.0 copy-start.12
  6.2 0.0 copy-start.13
  6.2 0.9 collective-permute-done.pair
  7.1 0.0 copy-done.9
  7.1 0.0 copy-done.10
  7.1 0.0 copy-done
  7.1 0.0 copy-done.8
  7.1 0.6 shard_map.137
  7.8 0.0 collective-permute-done.1.odd
  7.8 0.0 copy-done.5
  7.8 0.0 copy-done.11
  7.8 1.1 %shard_map.138 = (bf16[128,320]{1,0:T(8,128)(2,1)S(1)}, f32[64,128]{1,0:T(8,128)S(1)}) custom-call(f32[128,320]{1,0:T(8,128)S(1)} %get-tuple-element.17.partial, bf16[320,128]{1,0:T(8,128)(2,1)S(1)} %collective-permute-done.1.odd, bf16[3,320,320]{2,1,0:T(8,128)(2,1)S(1)} %get-tuple-element.18.odd_weight, bf16[320,320]{1,0:T(8,128)(2,1)S(1)} %copy-done.5, ...), custom_call_target="tpu_custom_call" | custom-call | flops 104857600 | bytes 819200 | tf_op jit(solution)/shard_map/pallas_call | solution.py:41
  8.8 33.3 %all_to_all.21 = f32[64,1,128]{2,1,0:T(1,128)S(1)} all-to-all(f32[64,1,128]{2,1,0:T(1,128)S(1)} %bitcast.15), channel_id=1, replica_groups={{0,1,4,5,8,9,12,13,14,15,10,11,6,7,2,3,16,17,20,21,24,25,28,29,30,31,26..., dimensions={0} | all-to-all | bytes 65536 | tf_op jit(solution)/shard_map/all_to_all | solution.py:279
  42.1 0.0 copy-done.1
  42.1 0.0 copy-done.2
  42.1 0.0 copy-done.3
  42.1 0.0 copy-done.4
  42.1 0.0 copy-done.12
  42.2 1.0 shard_map.139
  43.1 18.4 %all_to_all.22 = bf16[8,120,128]{2,1,0:T(8,128)(2,1)S(1)} all-to-all(bf16[8,120,128]{2,1,0:T(8,128)(2,1)S(1)} %get-tuple-element.25), channel_id=1, replica_groups={{0,4,8,12,14,10,6,2},{1,5,9,13,15,11,7,3},{16,20,24,28,30,26,22,18},{17..., dimensions={0} | all-to-all | bytes 491520 | tf_op jit(solution)/shard_map/all_to_all | solution.py:287
  61.6 2.6 %collective-permute-start.4 = (bf16[8,80,128]{2,1,0:T(8,128)(2,1)S(1)}, bf16[8,80,128]{2,1,0:T(8,128)(2,1)S(1)}, u32[]{:S(2)}, u32[]{:S(2)}) collective-permute-start(bf16[8,80,128]{2,1,0:T(8,128)(2,1)S(1)} %slice.9.refs_1_), channel_id=1, source_target_pairs={{0,16},{16,32},{32,48},{48,0},{1,17},{17,33},{33,49},{49,1},{2,18}... | collective-permute-start | bytes 491528 | tf_op jit(solution)/shard_map/ppermute | solution.py:291
  64.2 3.8 %collective-permute-start.3 = (bf16[8,80,128]{2,1,0:T(8,128)(2,1)S(1)}, bf16[8,80,128]{2,1,0:T(8,128)(2,1)S(1)}, u32[]{:S(2)}, u32[]{:S(2)}) collective-permute-start(bf16[8,80,128]{2,1,0:T(8,128)(2,1)S(1)} %slice.9.refs_1_), channel_id=1, source_target_pairs={{0,32},{16,48},{32,0},{48,16},{1,33},{17,49},{33,1},{49,17},{2,34}... | collective-permute-start | bytes 491528 | tf_op jit(solution)/shard_map/ppermute | solution.py:291
  67.9 3.4 %collective-permute-start.2 = (bf16[8,80,128]{2,1,0:T(8,128)(2,1)S(1)}, bf16[8,80,128]{2,1,0:T(8,128)(2,1)S(1)}, u32[]{:S(2)}, u32[]{:S(2)}) collective-permute-start(bf16[8,80,128]{2,1,0:T(8,128)(2,1)S(1)} %slice.9.refs_1_), channel_id=1, source_target_pairs={{0,48},{16,0},{32,16},{48,32},{1,49},{17,1},{33,17},{49,33},{2,50}... | collective-permute-start | bytes 491528 | tf_op jit(solution)/shard_map/ppermute | solution.py:291
  71.3 1.9 %collective-permute-start.5 = (bf16[8,40,128]{2,1,0:T(8,128)(2,1)S(1)}, bf16[8,40,128]{2,1,0:T(8,128)(2,1)S(1)}, u32[]{:S(2)}, u32[]{:S(2)}) collective-permute-start(bf16[8,40,128]{2,1,0:T(8,128)(2,1)S(1)} %slice.8.refs_0_), channel_id=1, source_target_pairs={{0,1},{1,0},{2,3},{3,2},{4,5},{5,4},{6,7},{7,6},{8,9},{9,8},{10,11... | collective-permute-start | bytes 245768 | tf_op jit(solution)/shard_map/ppermute | solution.py:292
  73.3 1.8 %shard_map.140.refs_4_ = f32[64,1024]{1,0:T(8,128)S(1)} custom-call(bf16[8,40,128]{2,1,0:T(8,128)(2,1)S(1)} %slice.8.refs_0_, bf16[8,80,128]{2,1,0:T(8,128)(2,1)S(1)} %slice.9.refs_1_), custom_call_target="tpu_custom_call" | custom-call | flops 1073741824 | bytes 163840 | tf_op jit(solution)/shard_map/pallas_call | solution.py:41
  75.0 0.0 collective-permute-done.5.refs_0_
  75.0 0.0 collective-permute-done.4.refs_3_.refs_2_
  75.0 3.2 %shard_map.142.refs_3_ = f32[64,1024]{1,0:T(8,128)S(1)} custom-call(bf16[8,40,128]{2,1,0:T(8,128)(2,1)S(1)} %collective-permute-done.5.refs_0_, bf16[8,80,128]{2,1,0:T(8,128)(2,1)S(1)} %slice.9.refs_1_, bf16[8,80,128]{2,1,0:T(8,128)(2,1)S(1)} %collective-permute-done.4.refs_3_.refs_2_), custom_call_target="tpu_custom_call" | custom-call | flops 2147483648 | bytes 327680 | tf_op jit(solution)/shard_map/pallas_call | solution.py:41
  78.2 0.0 collective-permute-done.3.refs_2_
  78.2 0.0 collective-permute-done.2.refs_1_
  78.2 3.3 %shard_map.143 = f32[64,1024]{1,0:T(8,128)S(1)} custom-call(bf16[8,40,128]{2,1,0:T(8,128)(2,1)S(1)} %collective-permute-done.5.refs_0_, bf16[8,80,128]{2,1,0:T(8,128)(2,1)S(1)} %collective-permute-done.2.refs_1_, bf16[8,80,128]{2,1,0:T(8,128)(2,1)S(1)} %collective-permute-done.3.refs_2_, f32[64,1024]{1,0:T(8,128)S(1)} %shard_map.142.refs_3_), custom_call_target="tpu_custom_call" | custom-call | flops 2147483648 | bytes 327680 | tf_op jit(solution)/shard_map/pallas_call | solution.py:41
  81.5 0.0 copy-start.6
  81.5 0.0 copy-start.7
  81.5 2.6 %collective-permute-start.6 = (f32[64,1024]{1,0:T(8,128)S(1)}, f32[64,1024]{1,0:T(8,128)S(1)}, u32[]{:S(2)}, u32[]{:S(2)}) collective-permute-start(f32[64,1024]{1,0:T(8,128)S(1)} %shard_map.143), channel_id=1, source_target_pairs={{0,1},{1,0},{2,3},{3,2},{4,5},{5,4},{6,7},{7,6},{8,9},{9,8},{10,11... | collective-permute-start | bytes 786440 | tf_op jit(solution)/shard_map/ppermute | solution.py:296
  84.1 4.6 %shard_map.141.mine = f32[64,1024]{1,0:T(8,128)S(1)} custom-call(bf16[8,40,128]{2,1,0:T(8,128)(2,1)S(1)} %slice.8.refs_0_, bf16[8,80,128]{2,1,0:T(8,128)(2,1)S(1)} %collective-permute-done.2.refs_1_, bf16[8,80,128]{2,1,0:T(8,128)(2,1)S(1)} %collective-permute-done.3.refs_2_, bf16[8,80,128]{2,1,0:T(8,128)(2,1)S(1)} %collective-permute-done.4.refs_3_.refs_2_, ...), custom_call_target="tpu_custom_call" | custom-call | flops 3221225472 | bytes 491520 | tf_op jit(solution)/shard_map/pallas_call | solution.py:41
  88.7 0.0 collective-permute-done.6.theirs
  88.8 15.4 %all_to_all.23 = bf16[8,40,128]{2,1,0:T(8,128)(2,1)S(1)} all-to-all(bf16[8,40,128]{2,1,0:T(8,128)(2,1)S(1)} %shard_map.144), channel_id=1, replica_groups={{0,4,8,12,14,10,6,2},{1,5,9,13,15,11,7,3},{16,20,24,28,30,26,22,18},{17..., dimensions={0} | all-to-all | bytes 163840 | tf_op jit(solution)/shard_map/all_to_all | solution.py:301
  104.1 1.1 %shard_map.145 = bf16[320,128]{1,0:T(8,128)(2,1)} custom-call(bf16[320,128]{1,0:T(8,128)(2,1)S(1)} %bitcast.9, bf16[128,320]{1,0:T(8,128)(2,1)S(1)} %get-tuple-element.26.inner, bf16[128,320]{1,0:T(8,128)(2,1)S(1)} %get-tuple-element.23.merged, bf16[320,320]{1,0:T(8,128)(2,1)S(1)} %copy-done.6, bf16[320,320]{1,0:T(8,128)(2,1)S(1)} %copy-done.7), custom_call_target="tpu_custom_call" | custom-call | flops 52428800 | bytes 409600 | tf_op jit(solution)/shard_map/pallas_call | solution.py:41
  (9 shorter events, 0.1 us)
Async XLA Ops:
  0.0 7.1 %copy-start.9 = (bf16[128,320]{0,1:T(8,128)(2,1)S(1)}, bf16[128,320]{0,1:T(8,128)(2,1)}, u32[]{:S(2)}) copy-start(bf16[128,320]{0,1:T(8,128)(2,1)} %param.15) | copy-start | bytes 245764
  0.0 7.1 %copy-start.10 = (f32[320]{0:T(512)S(1)}, f32[320]{0:T(512)}, u32[]{:S(2)}) copy-start(f32[320]{0:T(512)} %bias.1) | copy-start | bytes 3844
  0.0 7.1 %copy-start = (bf16[3,3,320,320]{3,2,1,0:T(8,128)(2,1)S(1)}, bf16[3,3,320,320]{3,2,1,0:T(8,128)(2,1)}, u32[]{:S(2)}) copy-start(bf16[3,3,320,320]{3,2,1,0:T(8,128)(2,1)} %weight.1) | copy-start | bytes 5529604
  0.0 7.1 %copy-start.8 = (bf16[128,320]{0,1:T(8,128)(2,1)S(1)}, bf16[128,320]{0,1:T(8,128)(2,1)}, u32[]{:S(2)}) copy-start(bf16[128,320]{0,1:T(8,128)(2,1)} %param.14) | copy-start | bytes 245764
  0.0 7.7 %collective-permute-start.1 = (bf16[320,128]{1,0:T(8,128)(2,1)}, bf16[320,128]{1,0:T(8,128)(2,1)S(1)}, u32[]{:S(2)}, u32[]{:S(2)}) collective-permute-start(bf16[320,128]{1,0:T(8,128)(2,1)} %bitcast.12), channel_id=1, source_target_pairs={{1,2},{3,4},{5,6},{7,8},{9,10},{11,12},{13,14},{15,16},{17,18},{19... | collective-permute-start | bytes 245768 | tf_op jit(solution)/shard_map/ppermute | solution.py:255
  0.8 6.3 %collective-permute-start = (bf16[320,128]{1,0:T(8,128)(2,1)}, bf16[320,128]{1,0:T(8,128)(2,1)S(1)}, u32[]{:S(2)}, u32[]{:S(2)}) collective-permute-start(bf16[320,128]{1,0:T(8,128)(2,1)} %bitcast.13), channel_id=1, source_target_pairs={{0,1},{1,0},{2,3},{3,2},{4,5},{5,4},{6,7},{7,6},{8,9},{9,8},{10,11... | collective-permute-start | bytes 245768 | tf_op jit(solution)/shard_map/ppermute | solution.py:256
  6.0 1.7 %copy-start.5 = (bf16[320,320]{1,0:T(8,128)(2,1)S(1)}, bf16[320,320]{1,0:T(8,128)(2,1)}, u32[]{:S(2)}) copy-start(bf16[320,320]{1,0:T(8,128)(2,1)} %zero_weight.1) | copy-start | bytes 614404
  6.0 1.7 %copy-start.11 = (f32[320]{0:T(512)S(1)}, f32[320]{0:T(512)}, u32[]{:S(2)}) copy-start(f32[320]{0:T(512)} %zero_bias.1) | copy-start | bytes 3844
  6.1 36.0 %copy-start.1 = (bf16[320,320]{1,0:T(8,128)(2,1)S(1)}, bf16[320,320]{1,0:T(8,128)(2,1)}, u32[]{:S(2)}) copy-start(bf16[320,320]{1,0:T(8,128)(2,1)} %proj_in.1) | copy-start | bytes 614404
  6.2 36.0 %copy-start.2 = (bf16[320,320]{1,0:T(8,128)(2,1)S(1)}, bf16[320,320]{1,0:T(8,128)(2,1)}, u32[]{:S(2)}) copy-start(bf16[320,320]{1,0:T(8,128)(2,1)} %wq.1) | copy-start | bytes 614404
  6.2 36.0 %copy-start.3 = (bf16[320,320]{1,0:T(8,128)(2,1)S(1)}, bf16[320,320]{1,0:T(8,128)(2,1)}, u32[]{:S(2)}) copy-start(bf16[320,320]{1,0:T(8,128)(2,1)} %wk.1) | copy-start | bytes 614404
  6.2 36.0 %copy-start.4 = (bf16[320,320]{1,0:T(8,128)(2,1)S(1)}, bf16[320,320]{1,0:T(8,128)(2,1)}, u32[]{:S(2)}) copy-start(bf16[320,320]{1,0:T(8,128)(2,1)} %wv.1) | copy-start | bytes 614404
  6.2 35.9 %copy-start.12 = (f32[320]{0:T(512)S(1)}, f32[320]{0:T(512)}, u32[]{:S(2)}) copy-start(f32[320]{0:T(512)} %group_gain.1) | copy-start | bytes 3844
  6.2 35.9 %copy-start.13 = (f32[320]{0:T(512)S(1)}, f32[320]{0:T(512)}, u32[]{:S(2)}) copy-start(f32[320]{0:T(512)} %norm_gain.1) | copy-start | bytes 3844
  61.6 13.5 %collective-permute-start.4 = (bf16[8,80,128]{2,1,0:T(8,128)(2,1)S(1)}, bf16[8,80,128]{2,1,0:T(8,128)(2,1)S(1)}, u32[]{:S(2)}, u32[]{:S(2)}) collective-permute-start(bf16[8,80,128]{2,1,0:T(8,128)(2,1)S(1)} %slice.9.refs_1_), channel_id=1, source_target_pairs={{0,16},{16,32},{32,48},{48,0},{1,17},{17,33},{33,49},{49,1},{2,18}... | collective-permute-start | bytes 491528 | tf_op jit(solution)/shard_map/ppermute | solution.py:291
  64.2 14.1 %collective-permute-start.3 = (bf16[8,80,128]{2,1,0:T(8,128)(2,1)S(1)}, bf16[8,80,128]{2,1,0:T(8,128)(2,1)S(1)}, u32[]{:S(2)}, u32[]{:S(2)}) collective-permute-start(bf16[8,80,128]{2,1,0:T(8,128)(2,1)S(1)} %slice.9.refs_1_), channel_id=1, source_target_pairs={{0,32},{16,48},{32,0},{48,16},{1,33},{17,49},{33,1},{49,17},{2,34}... | collective-permute-start | bytes 491528 | tf_op jit(solution)/shard_map/ppermute | solution.py:291
  67.9 10.3 %collective-permute-start.2 = (bf16[8,80,128]{2,1,0:T(8,128)(2,1)S(1)}, bf16[8,80,128]{2,1,0:T(8,128)(2,1)S(1)}, u32[]{:S(2)}, u32[]{:S(2)}) collective-permute-start(bf16[8,80,128]{2,1,0:T(8,128)(2,1)S(1)} %slice.9.refs_1_), channel_id=1, source_target_pairs={{0,48},{16,0},{32,16},{48,32},{1,49},{17,1},{33,17},{49,33},{2,50}... | collective-permute-start | bytes 491528 | tf_op jit(solution)/shard_map/ppermute | solution.py:291
  71.3 3.7 %collective-permute-start.5 = (bf16[8,40,128]{2,1,0:T(8,128)(2,1)S(1)}, bf16[8,40,128]{2,1,0:T(8,128)(2,1)S(1)}, u32[]{:S(2)}, u32[]{:S(2)}) collective-permute-start(bf16[8,40,128]{2,1,0:T(8,128)(2,1)S(1)} %slice.8.refs_0_), channel_id=1, source_target_pairs={{0,1},{1,0},{2,3},{3,2},{4,5},{5,4},{6,7},{7,6},{8,9},{9,8},{10,11... | collective-permute-start | bytes 245768 | tf_op jit(solution)/shard_map/ppermute | solution.py:292
  81.5 22.6 %copy-start.6 = (bf16[320,320]{1,0:T(8,128)(2,1)S(1)}, bf16[320,320]{1,0:T(8,128)(2,1)}, u32[]{:S(2)}) copy-start(bf16[320,320]{1,0:T(8,128)(2,1)} %attn_out.1) | copy-start | bytes 614404
  81.5 22.6 %copy-start.7 = (bf16[320,320]{1,0:T(8,128)(2,1)S(1)}, bf16[320,320]{1,0:T(8,128)(2,1)}, u32[]{:S(2)}) copy-start(bf16[320,320]{1,0:T(8,128)(2,1)} %proj_out.1) | copy-start | bytes 614404
  81.5 7.2 %collective-permute-start.6 = (f32[64,1024]{1,0:T(8,128)S(1)}, f32[64,1024]{1,0:T(8,128)S(1)}, u32[]{:S(2)}, u32[]{:S(2)}) collective-permute-start(f32[64,1024]{1,0:T(8,128)S(1)} %shard_map.143), channel_id=1, source_target_pairs={{0,1},{1,0},{2,3},{3,2},{4,5},{5,4},{6,7},{7,6},{8,9},{9,8},{10,11... | collective-permute-start | bytes 786440 | tf_op jit(solution)/shard_map/ppermute | solution.py:296

commit v10 on v9

--- a/solution.py
+++ b/solution.py
@@ -288,7 +288,7 @@
     queries, pair = received[:, :head_dim, :], received[:, head_dim:, :]
     chips = lax.axis_size("x")
     ring = lambda by: [(i, (i + by) % chips) for i in range(chips)]
-    pieces = [lax.ppermute(pair, "x", ring(by)) for by in (chips - 1, 2, 1)]
+    pieces = [lax.ppermute(pair, "x", ring(by)) for by in (2, chips - 1, 1)]
     others = lax.ppermute(queries, "c", swap)
     state = attend([queries], [pair], None, head_dim)
     other_state = attend([others], [pair, pieces[2]], None, head_dim)

time: 105 us -> 105 us (level)
  no operation moved by 1% of the time
where the time goes in v10:
time: 105 us
  blocking collectives  67.1 us (64%)
  starting transfers between devices  19.6 us (19%)
  Pallas kernels  16.7 us (16%)
    all_to_all x1, blocking collectives, local(): lax.all_to_all(stats, SEQ, 0, 0, axis_index_groups=whole, tiled=True)  33.3 us
    all_to_all x1, blocking collectives, local(): lax.all_to_all(send, 'z', 0, 0, axis_index_groups=folded, tiled=True)  18.4 us
    pallas_call x10, Pallas kernels, call(): pl.pallas_call(body, out_shape=out_shape, in_specs=[SMEM] * smem + [VMEM]...  16.7 us
    all_to_all x1, blocking collectives, local(): lax.all_to_all(result, 'z', 0, 0, axis_index_groups=folded, tiled=True)  15.4 us
    ppermute x3, starting transfers between devices, local(): pieces = [lax.ppermute(pair, 'x', ring(by)) for by in (2, chips - 1, 1)]  9.12 us
    ppermute x1, starting transfers between devices, local(): pair = lax.ppermute(hint, 'c', swap)  5.18 us
    ppermute x1, starting transfers between devices, local(): back = lax.ppermute(theirs, 'c', swap)  2.53 us
  transfers between devices with their start and end apart: 7, of which 1 were waited for; matrix products, arithmetic and copies ran while one was open for 0% of the time, Pallas kernels for 10%

profile of v10, /device:TPU:24, one launch (start us, length us, event | category | flops | bytes accessed | tf_op | source)
XLA Modules:
  0.0 104.7 jit_solution(5611001537767054052)
XLA Ops:
  0.0 0.0 copy-start.8
  0.0 0.8 collective-permute-start.1
  0.8 5.2 %collective-permute-start = (bf16[320,128]{1,0:T(8,128)(2,1)}, bf16[320,128]{1,0:T(8,128)(2,1)S(1)}, u32[]{:S(2)}, u32[]{:S(2)}) collective-permute-start(bf16[320,128]{1,0:T(8,128)(2,1)} %bitcast.13), channel_id=1, source_target_pairs={{0,1},{1,0},{2,3},{3,2},{4,5},{5,4},{6,7},{7,6},{8,9},{9,8},{10,11... | collective-permute-start | bytes 245768 | tf_op jit(solution)/shard_map/ppermute | solution.py:256
  6.0 0.0 copy-start.5
  6.0 0.0 copy-start.11
  6.0 0.1 shard_map.136
  6.1 0.0 copy-start.1
  6.2 0.0 copy-start.2
  6.2 0.0 copy-start.3
  6.2 0.0 copy-start.4
  6.2 0.0 copy-start.12
  6.2 0.0 copy-start.13
  6.2 0.9 collective-permute-done.pair
  7.1 0.0 copy-done.9
  7.1 0.0 copy-done.10
  7.1 0.0 copy-done
  7.1 0.0 copy-done.8
  7.1 0.6 shard_map.137
  7.8 0.0 collective-permute-done.1.odd
  7.8 0.0 copy-done.5
  7.8 0.0 copy-done.11
  7.8 1.1 %shard_map.138 = (bf16[128,320]{1,0:T(8,128)(2,1)S(1)}, f32[64,128]{1,0:T(8,128)S(1)}) custom-call(f32[128,320]{1,0:T(8,128)S(1)} %get-tuple-element.17.partial, bf16[320,128]{1,0:T(8,128)(2,1)S(1)} %collective-permute-done.1.odd, bf16[3,320,320]{2,1,0:T(8,128)(2,1)S(1)} %get-tuple-element.18.odd_weight, bf16[320,320]{1,0:T(8,128)(2,1)S(1)} %copy-done.5, ...), custom_call_target="tpu_custom_call" | custom-call | flops 104857600 | bytes 819200 | tf_op jit(solution)/shard_map/pallas_call | solution.py:41
  8.8 33.3 %all_to_all.21 = f32[64,1,128]{2,1,0:T(1,128)S(1)} all-to-all(f32[64,1,128]{2,1,0:T(1,128)S(1)} %bitcast.15), channel_id=1, replica_groups={{0,1,4,5,8,9,12,13,14,15,10,11,6,7,2,3,16,17,20,21,24,25,28,29,30,31,26..., dimensions={0} | all-to-all | bytes 65536 | tf_op jit(solution)/shard_map/all_to_all | solution.py:279
  42.1 0.0 copy-done.1
  42.1 0.0 copy-done.2
  42.1 0.0 copy-done.3
  42.1 0.0 copy-done.4
  42.2 1.0 shard_map.139
  43.1 18.4 %all_to_all.22 = bf16[8,120,128]{2,1,0:T(8,128)(2,1)S(1)} all-to-all(bf16[8,120,128]{2,1,0:T(8,128)(2,1)S(1)} %get-tuple-element.25), channel_id=1, replica_groups={{0,4,8,12,14,10,6,2},{1,5,9,13,15,11,7,3},{16,20,24,28,30,26,22,18},{17..., dimensions={0} | all-to-all | bytes 491520 | tf_op jit(solution)/shard_map/all_to_all | solution.py:287
  61.6 2.6 %collective-permute-start.4 = (bf16[8,80,128]{2,1,0:T(8,128)(2,1)S(1)}, bf16[8,80,128]{2,1,0:T(8,128)(2,1)S(1)}, u32[]{:S(2)}, u32[]{:S(2)}) collective-permute-start(bf16[8,80,128]{2,1,0:T(8,128)(2,1)S(1)} %slice.9.refs_1_), channel_id=1, source_target_pairs={{0,16},{16,32},{32,48},{48,0},{1,17},{17,33},{33,49},{49,1},{2,18}... | collective-permute-start | bytes 491528 | tf_op jit(solution)/shard_map/ppermute | solution.py:291
  64.2 4.5 %collective-permute-start.3 = (bf16[8,80,128]{2,1,0:T(8,128)(2,1)S(1)}, bf16[8,80,128]{2,1,0:T(8,128)(2,1)S(1)}, u32[]{:S(2)}, u32[]{:S(2)}) collective-permute-start(bf16[8,80,128]{2,1,0:T(8,128)(2,1)S(1)} %slice.9.refs_1_), channel_id=1, source_target_pairs={{0,48},{16,0},{32,16},{48,32},{1,49},{17,1},{33,17},{49,33},{2,50}... | collective-permute-start | bytes 491528 | tf_op jit(solution)/shard_map/ppermute | solution.py:291
  68.6 2.1 %collective-permute-start.2 = (bf16[8,80,128]{2,1,0:T(8,128)(2,1)S(1)}, bf16[8,80,128]{2,1,0:T(8,128)(2,1)S(1)}, u32[]{:S(2)}, u32[]{:S(2)}) collective-permute-start(bf16[8,80,128]{2,1,0:T(8,128)(2,1)S(1)} %slice.9.refs_1_), channel_id=1, source_target_pairs={{0,32},{16,48},{32,0},{48,16},{1,33},{17,49},{33,1},{49,17},{2,34}... | collective-permute-start | bytes 491528 | tf_op jit(solution)/shard_map/ppermute | solution.py:291
  70.7 1.9 %collective-permute-start.5 = (bf16[8,40,128]{2,1,0:T(8,128)(2,1)S(1)}, bf16[8,40,128]{2,1,0:T(8,128)(2,1)S(1)}, u32[]{:S(2)}, u32[]{:S(2)}) collective-permute-start(bf16[8,40,128]{2,1,0:T(8,128)(2,1)S(1)} %slice.8.refs_0_), channel_id=1, source_target_pairs={{0,1},{1,0},{2,3},{3,2},{4,5},{5,4},{6,7},{7,6},{8,9},{9,8},{10,11... | collective-permute-start | bytes 245768 | tf_op jit(solution)/shard_map/ppermute | solution.py:292
  72.7 1.8 %shard_map.140.refs_4_ = f32[64,1024]{1,0:T(8,128)S(1)} custom-call(bf16[8,40,128]{2,1,0:T(8,128)(2,1)S(1)} %slice.8.refs_0_, bf16[8,80,128]{2,1,0:T(8,128)(2,1)S(1)} %slice.9.refs_1_), custom_call_target="tpu_custom_call" | custom-call | flops 1073741824 | bytes 163840 | tf_op jit(solution)/shard_map/pallas_call | solution.py:41
  74.4 0.0 collective-permute-done.5.refs_0_
  74.4 0.0 collective-permute-done.4.refs_3_.refs_2_
  74.4 3.2 %shard_map.142.refs_3_ = f32[64,1024]{1,0:T(8,128)S(1)} custom-call(bf16[8,40,128]{2,1,0:T(8,128)(2,1)S(1)} %collective-permute-done.5.refs_0_, bf16[8,80,128]{2,1,0:T(8,128)(2,1)S(1)} %slice.9.refs_1_, bf16[8,80,128]{2,1,0:T(8,128)(2,1)S(1)} %collective-permute-done.4.refs_3_.refs_2_), custom_call_target="tpu_custom_call" | custom-call | flops 2147483648 | bytes 327680 | tf_op jit(solution)/shard_map/pallas_call | solution.py:41
  77.6 0.0 collective-permute-done.3.refs_2_
  77.6 0.0 collective-permute-done.2.refs_1_
  77.6 3.3 %shard_map.143 = f32[64,1024]{1,0:T(8,128)S(1)} custom-call(bf16[8,40,128]{2,1,0:T(8,128)(2,1)S(1)} %collective-permute-done.5.refs_0_, bf16[8,80,128]{2,1,0:T(8,128)(2,1)S(1)} %collective-permute-done.2.refs_1_, bf16[8,80,128]{2,1,0:T(8,128)(2,1)S(1)} %collective-permute-done.3.refs_2_, f32[64,1024]{1,0:T(8,128)S(1)} %shard_map.142.refs_3_), custom_call_target="tpu_custom_call" | custom-call | flops 2147483648 | bytes 327680 | tf_op jit(solution)/shard_map/pallas_call | solution.py:41
  80.9 0.0 copy-start.6
  80.9 0.0 copy-start.7
  81.0 2.5 %collective-permute-start.6 = (f32[64,1024]{1,0:T(8,128)S(1)}, f32[64,1024]{1,0:T(8,128)S(1)}, u32[]{:S(2)}, u32[]{:S(2)}) collective-permute-start(f32[64,1024]{1,0:T(8,128)S(1)} %shard_map.143), channel_id=1, source_target_pairs={{0,1},{1,0},{2,3},{3,2},{4,5},{5,4},{6,7},{7,6},{8,9},{9,8},{10,11... | collective-permute-start | bytes 786440 | tf_op jit(solution)/shard_map/ppermute | solution.py:296
  83.5 4.6 %shard_map.141.mine = f32[64,1024]{1,0:T(8,128)S(1)} custom-call(bf16[8,40,128]{2,1,0:T(8,128)(2,1)S(1)} %slice.8.refs_0_, bf16[8,80,128]{2,1,0:T(8,128)(2,1)S(1)} %collective-permute-done.2.refs_1_, bf16[8,80,128]{2,1,0:T(8,128)(2,1)S(1)} %collective-permute-done.3.refs_2_, bf16[8,80,128]{2,1,0:T(8,128)(2,1)S(1)} %collective-permute-done.4.refs_3_.refs_2_, ...), custom_call_target="tpu_custom_call" | custom-call | flops 3221225472 | bytes 491520 | tf_op jit(solution)/shard_map/pallas_call | solution.py:41
  88.1 0.0 collective-permute-done.6.theirs
  88.1 15.4 %all_to_all.23 = bf16[8,40,128]{2,1,0:T(8,128)(2,1)S(1)} all-to-all(bf16[8,40,128]{2,1,0:T(8,128)(2,1)S(1)} %shard_map.144), channel_id=1, replica_groups={{0,4,8,12,14,10,6,2},{1,5,9,13,15,11,7,3},{16,20,24,28,30,26,22,18},{17..., dimensions={0} | all-to-all | bytes 163840 | tf_op jit(solution)/shard_map/all_to_all | solution.py:301
  103.5 0.0 copy-done.7
  103.5 1.1 %shard_map.145 = bf16[320,128]{1,0:T(8,128)(2,1)} custom-call(bf16[320,128]{1,0:T(8,128)(2,1)S(1)} %bitcast.9, bf16[128,320]{1,0:T(8,128)(2,1)S(1)} %get-tuple-element.26.inner, bf16[128,320]{1,0:T(8,128)(2,1)S(1)} %get-tuple-element.23.merged, bf16[320,320]{1,0:T(8,128)(2,1)S(1)} %copy-done.6, bf16[320,320]{1,0:T(8,128)(2,1)S(1)} %copy-done.7), custom_call_target="tpu_custom_call" | custom-call | flops 52428800 | bytes 409600 | tf_op jit(solution)/shard_map/pallas_call | solution.py:41
  (9 shorter events, 0.1 us)
Async XLA Ops:
  0.0 7.1 %copy-start.9 = (bf16[128,320]{0,1:T(8,128)(2,1)S(1)}, bf16[128,320]{0,1:T(8,128)(2,1)}, u32[]{:S(2)}) copy-start(bf16[128,320]{0,1:T(8,128)(2,1)} %param.15) | copy-start | bytes 245764
  0.0 7.1 %copy-start.10 = (f32[320]{0:T(512)S(1)}, f32[320]{0:T(512)}, u32[]{:S(2)}) copy-start(f32[320]{0:T(512)} %bias.1) | copy-start | bytes 3844
  0.0 7.1 %copy-start = (bf16[3,3,320,320]{3,2,1,0:T(8,128)(2,1)S(1)}, bf16[3,3,320,320]{3,2,1,0:T(8,128)(2,1)}, u32[]{:S(2)}) copy-start(bf16[3,3,320,320]{3,2,1,0:T(8,128)(2,1)} %weight.1) | copy-start | bytes 5529604
  0.0 7.1 %copy-start.8 = (bf16[128,320]{0,1:T(8,128)(2,1)S(1)}, bf16[128,320]{0,1:T(8,128)(2,1)}, u32[]{:S(2)}) copy-start(bf16[128,320]{0,1:T(8,128)(2,1)} %param.14) | copy-start | bytes 245764
  0.0 7.7 %collective-permute-start.1 = (bf16[320,128]{1,0:T(8,128)(2,1)}, bf16[320,128]{1,0:T(8,128)(2,1)S(1)}, u32[]{:S(2)}, u32[]{:S(2)}) collective-permute-start(bf16[320,128]{1,0:T(8,128)(2,1)} %bitcast.12), channel_id=1, source_target_pairs={{1,2},{3,4},{5,6},{7,8},{9,10},{11,12},{13,14},{15,16},{17,18},{19... | collective-permute-start | bytes 245768 | tf_op jit(solution)/shard_map/ppermute | solution.py:255
  0.8 6.3 %collective-permute-start = (bf16[320,128]{1,0:T(8,128)(2,1)}, bf16[320,128]{1,0:T(8,128)(2,1)S(1)}, u32[]{:S(2)}, u32[]{:S(2)}) collective-permute-start(bf16[320,128]{1,0:T(8,128)(2,1)} %bitcast.13), channel_id=1, source_target_pairs={{0,1},{1,0},{2,3},{3,2},{4,5},{5,4},{6,7},{7,6},{8,9},{9,8},{10,11... | collective-permute-start | bytes 245768 | tf_op jit(solution)/shard_map/ppermute | solution.py:256
  6.0 1.7 %copy-start.5 = (bf16[320,320]{1,0:T(8,128)(2,1)S(1)}, bf16[320,320]{1,0:T(8,128)(2,1)}, u32[]{:S(2)}) copy-start(bf16[320,320]{1,0:T(8,128)(2,1)} %zero_weight.1) | copy-start | bytes 614404
  6.0 1.7 %copy-start.11 = (f32[320]{0:T(512)S(1)}, f32[320]{0:T(512)}, u32[]{:S(2)}) copy-start(f32[320]{0:T(512)} %zero_bias.1) | copy-start | bytes 3844
  6.1 36.0 %copy-start.1 = (bf16[320,320]{1,0:T(8,128)(2,1)S(1)}, bf16[320,320]{1,0:T(8,128)(2,1)}, u32[]{:S(2)}) copy-start(bf16[320,320]{1,0:T(8,128)(2,1)} %proj_in.1) | copy-start | bytes 614404
  6.2 36.0 %copy-start.2 = (bf16[320,320]{1,0:T(8,128)(2,1)S(1)}, bf16[320,320]{1,0:T(8,128)(2,1)}, u32[]{:S(2)}) copy-start(bf16[320,320]{1,0:T(8,128)(2,1)} %wq.1) | copy-start | bytes 614404
  6.2 36.0 %copy-start.3 = (bf16[320,320]{1,0:T(8,128)(2,1)S(1)}, bf16[320,320]{1,0:T(8,128)(2,1)}, u32[]{:S(2)}) copy-start(bf16[320,320]{1,0:T(8,128)(2,1)} %wk.1) | copy-start | bytes 614404
  6.2 36.0 %copy-start.4 = (bf16[320,320]{1,0:T(8,128)(2,1)S(1)}, bf16[320,320]{1,0:T(8,128)(2,1)}, u32[]{:S(2)}) copy-start(bf16[320,320]{1,0:T(8,128)(2,1)} %wv.1) | copy-start | bytes 614404
  6.2 35.9 %copy-start.12 = (f32[320]{0:T(512)S(1)}, f32[320]{0:T(512)}, u32[]{:S(2)}) copy-start(f32[320]{0:T(512)} %group_gain.1) | copy-start | bytes 3844
  6.2 35.9 %copy-start.13 = (f32[320]{0:T(512)S(1)}, f32[320]{0:T(512)}, u32[]{:S(2)}) copy-start(f32[320]{0:T(512)} %norm_gain.1) | copy-start | bytes 3844
  61.6 12.9 %collective-permute-start.4 = (bf16[8,80,128]{2,1,0:T(8,128)(2,1)S(1)}, bf16[8,80,128]{2,1,0:T(8,128)(2,1)S(1)}, u32[]{:S(2)}, u32[]{:S(2)}) collective-permute-start(bf16[8,80,128]{2,1,0:T(8,128)(2,1)S(1)} %slice.9.refs_1_), channel_id=1, source_target_pairs={{0,16},{16,32},{32,48},{48,0},{1,17},{17,33},{33,49},{49,1},{2,18}... | collective-permute-start | bytes 491528 | tf_op jit(solution)/shard_map/ppermute | solution.py:291
  64.2 13.5 %collective-permute-start.3 = (bf16[8,80,128]{2,1,0:T(8,128)(2,1)S(1)}, bf16[8,80,128]{2,1,0:T(8,128)(2,1)S(1)}, u32[]{:S(2)}, u32[]{:S(2)}) collective-permute-start(bf16[8,80,128]{2,1,0:T(8,128)(2,1)S(1)} %slice.9.refs_1_), channel_id=1, source_target_pairs={{0,48},{16,0},{32,16},{48,32},{1,49},{17,1},{33,17},{49,33},{2,50}... | collective-permute-start | bytes 491528 | tf_op jit(solution)/shard_map/ppermute | solution.py:291
  68.6 9.0 %collective-permute-start.2 = (bf16[8,80,128]{2,1,0:T(8,128)(2,1)S(1)}, bf16[8,80,128]{2,1,0:T(8,128)(2,1)S(1)}, u32[]{:S(2)}, u32[]{:S(2)}) collective-permute-start(bf16[8,80,128]{2,1,0:T(8,128)(2,1)S(1)} %slice.9.refs_1_), channel_id=1, source_target_pairs={{0,32},{16,48},{32,0},{48,16},{1,33},{17,49},{33,1},{49,17},{2,34}... | collective-permute-start | bytes 491528 | tf_op jit(solution)/shard_map/ppermute | solution.py:291
  70.7 3.7 %collective-permute-start.5 = (bf16[8,40,128]{2,1,0:T(8,128)(2,1)S(1)}, bf16[8,40,128]{2,1,0:T(8,128)(2,1)S(1)}, u32[]{:S(2)}, u32[]{:S(2)}) collective-permute-start(bf16[8,40,128]{2,1,0:T(8,128)(2,1)S(1)} %slice.8.refs_0_), channel_id=1, source_target_pairs={{0,1},{1,0},{2,3},{3,2},{4,5},{5,4},{6,7},{7,6},{8,9},{9,8},{10,11... | collective-permute-start | bytes 245768 | tf_op jit(solution)/shard_map/ppermute | solution.py:292
  80.9 22.6 %copy-start.6 = (bf16[320,320]{1,0:T(8,128)(2,1)S(1)}, bf16[320,320]{1,0:T(8,128)(2,1)}, u32[]{:S(2)}) copy-start(bf16[320,320]{1,0:T(8,128)(2,1)} %attn_out.1) | copy-start | bytes 614404
  80.9 22.6 %copy-start.7 = (bf16[320,320]{1,0:T(8,128)(2,1)S(1)}, bf16[320,320]{1,0:T(8,128)(2,1)}, u32[]{:S(2)}) copy-start(bf16[320,320]{1,0:T(8,128)(2,1)} %proj_out.1) | copy-start | bytes 614404
  81.0 7.1 %collective-permute-start.6 = (f32[64,1024]{1,0:T(8,128)S(1)}, f32[64,1024]{1,0:T(8,128)S(1)}, u32[]{:S(2)}, u32[]{:S(2)}) collective-permute-start(f32[64,1024]{1,0:T(8,128)S(1)} %shard_map.143), channel_id=1, source_target_pairs={{0,1},{1,0},{2,3},{3,2},{4,5},{5,4},{6,7},{7,6},{8,9},{9,8},{10,11... | collective-permute-start | bytes 786440 | tf_op jit(solution)/shard_map/ppermute | solution.py:296

commit v11 on v10

--- a/solution.py
+++ b/solution.py
@@ -292,7 +292,8 @@
     others = lax.ppermute(queries, "c", swap)
     state = attend([queries], [pair], None, head_dim)
     other_state = attend([others], [pair, pieces[2]], None, head_dim)
-    (theirs,) = attend([others], pieces[:2], other_state, head_dim)
+    other_state = attend([others], pieces[1:2], other_state, head_dim)
+    (theirs,) = attend([others], pieces[:1], other_state, head_dim)
     back = lax.ppermute(theirs, "c", swap)
     (mine,) = attend([queries], pieces, state, head_dim)
     result = call(

time: 105 us -> 106 us (level)
    pallas_call x10 -> x11, Pallas kernels: 16.7 us -> 17.1 us  [call(): pl.pallas_call(body, out_shape=out_shape, in_specs=[SMEM] * smem + [VMEM]...]
  transfers between devices with their start and end apart: 7 -> 7, of which waited for: 1 -> 1; matrix products, arithmetic and copies ran while one was open for 0% -> 0% of each run, Pallas kernels for 10% -> 12%
where the time goes in v11:
time: 106 us; the launch traced here: 105 us
  blocking collectives  67.1 us (63%)
  starting transfers between devices  19.5 us (18%)
  Pallas kernels  17.1 us (16%)
    all_to_all x1, blocking collectives, local(): lax.all_to_all(stats, SEQ, 0, 0, axis_index_groups=whole, tiled=True)  33.3 us
    all_to_all x1, blocking collectives, local(): lax.all_to_all(send, 'z', 0, 0, axis_index_groups=folded, tiled=True)  18.4 us
    pallas_call x11, Pallas kernels, call(): pl.pallas_call(body, out_shape=out_shape, in_specs=[SMEM] * smem + [VMEM]...  17.1 us
    all_to_all x1, blocking collectives, local(): lax.all_to_all(result, 'z', 0, 0, axis_index_groups=folded, tiled=True)  15.4 us
    ppermute x3, starting transfers between devices, local(): pieces = [lax.ppermute(pair, 'x', ring(by)) for by in (2, chips - 1, 1)]  9.12 us
    ppermute x1, starting transfers between devices, local(): pair = lax.ppermute(hint, 'c', swap)  5.18 us
    ppermute x1, starting transfers between devices, local(): back = lax.ppermute(theirs, 'c', swap)  2.52 us
  transfers between devices with their start and end apart: 7, of which 1 were waited for; matrix products, arithmetic and copies ran while one was open for 0% of the time, Pallas kernels for 12%

profile of v11, /device:TPU:24, one launch (start us, length us, event | category | flops | bytes accessed | tf_op | source)
XLA Modules:
  0.0 105.0 jit_solution(4294511491993970727)
XLA Ops:
  0.0 0.0 copy-start.8
  0.0 0.8 collective-permute-start.1
  0.8 5.2 %collective-permute-start = (bf16[320,128]{1,0:T(8,128)(2,1)}, bf16[320,128]{1,0:T(8,128)(2,1)S(1)}, u32[]{:S(2)}, u32[]{:S(2)}) collective-permute-start(bf16[320,128]{1,0:T(8,128)(2,1)} %bitcast.13), channel_id=1, source_target_pairs={{0,1},{1,0},{2,3},{3,2},{4,5},{5,4},{6,7},{7,6},{8,9},{9,8},{10,11... | collective-permute-start | bytes 245768 | tf_op jit(solution)/shard_map/ppermute | solution.py:256
  6.0 0.0 copy-start.5
  6.0 0.0 copy-start.11
  6.0 0.1 shard_map.136
  6.1 0.0 copy-start.1
  6.2 0.0 copy-start.2
  6.2 0.0 copy-start.3
  6.2 0.0 copy-start.4
  6.2 0.0 copy-start.12
  6.2 0.0 copy-start.13
  6.2 0.9 collective-permute-done.pair
  7.1 0.0 copy-done.9
  7.1 0.0 copy-done.10
  7.1 0.0 copy-done
  7.1 0.0 copy-done.8
  7.1 0.6 shard_map.137
  7.8 0.0 collective-permute-done.1.odd
  7.8 0.0 copy-done.5
  7.8 0.0 copy-done.11
  7.8 1.1 %shard_map.138 = (bf16[128,320]{1,0:T(8,128)(2,1)S(1)}, f32[64,128]{1,0:T(8,128)S(1)}) custom-call(f32[128,320]{1,0:T(8,128)S(1)} %get-tuple-element.17.partial, bf16[320,128]{1,0:T(8,128)(2,1)S(1)} %collective-permute-done.1.odd, bf16[3,320,320]{2,1,0:T(8,128)(2,1)S(1)} %get-tuple-element.18.odd_weight, bf16[320,320]{1,0:T(8,128)(2,1)S(1)} %copy-done.5, ...), custom_call_target="tpu_custom_call" | custom-call | flops 104857600 | bytes 819200 | tf_op jit(solution)/shard_map/pallas_call | solution.py:41
  8.8 33.3 %all_to_all.21 = f32[64,1,128]{2,1,0:T(1,128)S(1)} all-to-all(f32[64,1,128]{2,1,0:T(1,128)S(1)} %bitcast.15), channel_id=1, replica_groups={{0,1,4,5,8,9,12,13,14,15,10,11,6,7,2,3,16,17,20,21,24,25,28,29,30,31,26..., dimensions={0} | all-to-all | bytes 65536 | tf_op jit(solution)/shard_map/all_to_all | solution.py:279
  42.1 0.0 copy-done.1
  42.1 0.0 copy-done.2
  42.1 0.0 copy-done.3
  42.2 1.0 shard_map.139
  43.1 18.4 %all_to_all.22 = bf16[8,120,128]{2,1,0:T(8,128)(2,1)S(1)} all-to-all(bf16[8,120,128]{2,1,0:T(8,128)(2,1)S(1)} %get-tuple-element.25), channel_id=1, replica_groups={{0,4,8,12,14,10,6,2},{1,5,9,13,15,11,7,3},{16,20,24,28,30,26,22,18},{17..., dimensions={0} | all-to-all | bytes 491520 | tf_op jit(solution)/shard_map/all_to_all | solution.py:287
  61.6 2.6 %collective-permute-start.4 = (bf16[8,80,128]{2,1,0:T(8,128)(2,1)S(1)}, bf16[8,80,128]{2,1,0:T(8,128)(2,1)S(1)}, u32[]{:S(2)}, u32[]{:S(2)}) collective-permute-start(bf16[8,80,128]{2,1,0:T(8,128)(2,1)S(1)} %slice.9.refs_1_), channel_id=1, source_target_pairs={{0,16},{16,32},{32,48},{48,0},{1,17},{17,33},{33,49},{49,1},{2,18}... | collective-permute-start | bytes 491528 | tf_op jit(solution)/shard_map/ppermute | solution.py:291
  64.2 4.5 %collective-permute-start.3 = (bf16[8,80,128]{2,1,0:T(8,128)(2,1)S(1)}, bf16[8,80,128]{2,1,0:T(8,128)(2,1)S(1)}, u32[]{:S(2)}, u32[]{:S(2)}) collective-permute-start(bf16[8,80,128]{2,1,0:T(8,128)(2,1)S(1)} %slice.9.refs_1_), channel_id=1, source_target_pairs={{0,48},{16,0},{32,16},{48,32},{1,49},{17,1},{33,17},{49,33},{2,50}... | collective-permute-start | bytes 491528 | tf_op jit(solution)/shard_map/ppermute | solution.py:291
  68.6 2.1 %collective-permute-start.2 = (bf16[8,80,128]{2,1,0:T(8,128)(2,1)S(1)}, bf16[8,80,128]{2,1,0:T(8,128)(2,1)S(1)}, u32[]{:S(2)}, u32[]{:S(2)}) collective-permute-start(bf16[8,80,128]{2,1,0:T(8,128)(2,1)S(1)} %slice.9.refs_1_), channel_id=1, source_target_pairs={{0,32},{16,48},{32,0},{48,16},{1,33},{17,49},{33,1},{49,17},{2,34}... | collective-permute-start | bytes 491528 | tf_op jit(solution)/shard_map/ppermute | solution.py:291
  70.7 1.9 %collective-permute-start.5 = (bf16[8,40,128]{2,1,0:T(8,128)(2,1)S(1)}, bf16[8,40,128]{2,1,0:T(8,128)(2,1)S(1)}, u32[]{:S(2)}, u32[]{:S(2)}) collective-permute-start(bf16[8,40,128]{2,1,0:T(8,128)(2,1)S(1)} %slice.8.refs_0_), channel_id=1, source_target_pairs={{0,1},{1,0},{2,3},{3,2},{4,5},{5,4},{6,7},{7,6},{8,9},{9,8},{10,11... | collective-permute-start | bytes 245768 | tf_op jit(solution)/shard_map/ppermute | solution.py:292
  72.7 1.8 %shard_map.140.refs_4_ = f32[64,1024]{1,0:T(8,128)S(1)} custom-call(bf16[8,40,128]{2,1,0:T(8,128)(2,1)S(1)} %slice.8.refs_0_, bf16[8,80,128]{2,1,0:T(8,128)(2,1)S(1)} %slice.9.refs_1_), custom_call_target="tpu_custom_call" | custom-call | flops 1073741824 | bytes 163840 | tf_op jit(solution)/shard_map/pallas_call | solution.py:41
  74.4 0.0 collective-permute-done.5.refs_0_
  74.4 0.0 collective-permute-done.4.refs_3_.refs_2_
  74.4 3.2 %shard_map.142.refs_2_ = f32[64,1024]{1,0:T(8,128)S(1)} custom-call(bf16[8,40,128]{2,1,0:T(8,128)(2,1)S(1)} %collective-permute-done.5.refs_0_, bf16[8,80,128]{2,1,0:T(8,128)(2,1)S(1)} %slice.9.refs_1_, bf16[8,80,128]{2,1,0:T(8,128)(2,1)S(1)} %collective-permute-done.4.refs_3_.refs_2_), custom_call_target="tpu_custom_call" | custom-call | flops 2147483648 | bytes 327680 | tf_op jit(solution)/shard_map/pallas_call | solution.py:41
  77.6 0.0 collective-permute-done.3.refs_2_.refs_1_
  77.6 1.9 %shard_map.143.refs_2_ = f32[64,1024]{1,0:T(8,128)S(1)} custom-call(bf16[8,40,128]{2,1,0:T(8,128)(2,1)S(1)} %collective-permute-done.5.refs_0_, bf16[8,80,128]{2,1,0:T(8,128)(2,1)S(1)} %collective-permute-done.3.refs_2_.refs_1_, f32[64,1024]{1,0:T(8,128)S(1)} %shard_map.142.refs_2_), custom_call_target="tpu_custom_call" | custom-call | flops 1073741824 | bytes 163840 | tf_op jit(solution)/shard_map/pallas_call | solution.py:41
  79.5 0.0 collective-permute-done.2.refs_1_
  79.6 1.7 %shard_map.144 = f32[64,1024]{1,0:T(8,128)S(1)} custom-call(bf16[8,40,128]{2,1,0:T(8,128)(2,1)S(1)} %collective-permute-done.5.refs_0_, bf16[8,80,128]{2,1,0:T(8,128)(2,1)S(1)} %collective-permute-done.2.refs_1_, f32[64,1024]{1,0:T(8,128)S(1)} %shard_map.143.refs_2_), custom_call_target="tpu_custom_call" | custom-call | flops 1073741824 | bytes 163840 | tf_op jit(solution)/shard_map/pallas_call | solution.py:41
  81.3 0.0 copy-start.6
  81.3 0.0 copy-start.7
  81.3 2.5 %collective-permute-start.6 = (f32[64,1024]{1,0:T(8,128)S(1)}, f32[64,1024]{1,0:T(8,128)S(1)}, u32[]{:S(2)}, u32[]{:S(2)}) collective-permute-start(f32[64,1024]{1,0:T(8,128)S(1)} %shard_map.144), channel_id=1, source_target_pairs={{0,1},{1,0},{2,3},{3,2},{4,5},{5,4},{6,7},{7,6},{8,9},{9,8},{10,11... | collective-permute-start | bytes 786440 | tf_op jit(solution)/shard_map/ppermute | solution.py:297
  83.9 4.6 %shard_map.141.mine = f32[64,1024]{1,0:T(8,128)S(1)} custom-call(bf16[8,40,128]{2,1,0:T(8,128)(2,1)S(1)} %slice.8.refs_0_, bf16[8,80,128]{2,1,0:T(8,128)(2,1)S(1)} %collective-permute-done.2.refs_1_, bf16[8,80,128]{2,1,0:T(8,128)(2,1)S(1)} %collective-permute-done.3.refs_2_.refs_1_, bf16[8,80,128]{2,1,0:T(8,128)(2,1)S(1)} %collective-permute-done.4.refs_3_.refs_2_, ...), custom_call_target="tpu_custom_call" | custom-call | flops 3221225472 | bytes 491520 | tf_op jit(solution)/shard_map/pallas_call | solution.py:41
  88.4 0.0 collective-permute-done.6.theirs
  88.5 15.4 %all_to_all.23 = bf16[8,40,128]{2,1,0:T(8,128)(2,1)S(1)} all-to-all(bf16[8,40,128]{2,1,0:T(8,128)(2,1)S(1)} %shard_map.145), channel_id=1, replica_groups={{0,4,8,12,14,10,6,2},{1,5,9,13,15,11,7,3},{16,20,24,28,30,26,22,18},{17..., dimensions={0} | all-to-all | bytes 163840 | tf_op jit(solution)/shard_map/all_to_all | solution.py:302
  103.9 0.0 copy-done.7
  103.9 1.1 %shard_map.146 = bf16[320,128]{1,0:T(8,128)(2,1)} custom-call(bf16[320,128]{1,0:T(8,128)(2,1)S(1)} %bitcast.9, bf16[128,320]{1,0:T(8,128)(2,1)S(1)} %get-tuple-element.26.inner, bf16[128,320]{1,0:T(8,128)(2,1)S(1)} %get-tuple-element.23.merged, bf16[320,320]{1,0:T(8,128)(2,1)S(1)} %copy-done.6, bf16[320,320]{1,0:T(8,128)(2,1)S(1)} %copy-done.7), custom_call_target="tpu_custom_call" | custom-call | flops 52428800 | bytes 409600 | tf_op jit(solution)/shard_map/pallas_call | solution.py:41
  (10 shorter events, 0.1 us)
Async XLA Ops:
  0.0 7.1 %copy-start.9 = (bf16[128,320]{0,1:T(8,128)(2,1)S(1)}, bf16[128,320]{0,1:T(8,128)(2,1)}, u32[]{:S(2)}) copy-start(bf16[128,320]{0,1:T(8,128)(2,1)} %param.15) | copy-start | bytes 245764
  0.0 7.1 %copy-start.10 = (f32[320]{0:T(512)S(1)}, f32[320]{0:T(512)}, u32[]{:S(2)}) copy-start(f32[320]{0:T(512)} %bias.1) | copy-start | bytes 3844
  0.0 7.1 %copy-start = (bf16[3,3,320,320]{3,2,1,0:T(8,128)(2,1)S(1)}, bf16[3,3,320,320]{3,2,1,0:T(8,128)(2,1)}, u32[]{:S(2)}) copy-start(bf16[3,3,320,320]{3,2,1,0:T(8,128)(2,1)} %weight.1) | copy-start | bytes 5529604
  0.0 7.1 %copy-start.8 = (bf16[128,320]{0,1:T(8,128)(2,1)S(1)}, bf16[128,320]{0,1:T(8,128)(2,1)}, u32[]{:S(2)}) copy-start(bf16[128,320]{0,1:T(8,128)(2,1)} %param.14) | copy-start | bytes 245764
  0.0 7.7 %collective-permute-start.1 = (bf16[320,128]{1,0:T(8,128)(2,1)}, bf16[320,128]{1,0:T(8,128)(2,1)S(1)}, u32[]{:S(2)}, u32[]{:S(2)}) collective-permute-start(bf16[320,128]{1,0:T(8,128)(2,1)} %bitcast.12), channel_id=1, source_target_pairs={{1,2},{3,4},{5,6},{7,8},{9,10},{11,12},{13,14},{15,16},{17,18},{19... | collective-permute-start | bytes 245768 | tf_op jit(solution)/shard_map/ppermute | solution.py:255
  0.8 6.3 %collective-permute-start = (bf16[320,128]{1,0:T(8,128)(2,1)}, bf16[320,128]{1,0:T(8,128)(2,1)S(1)}, u32[]{:S(2)}, u32[]{:S(2)}) collective-permute-start(bf16[320,128]{1,0:T(8,128)(2,1)} %bitcast.13), channel_id=1, source_target_pairs={{0,1},{1,0},{2,3},{3,2},{4,5},{5,4},{6,7},{7,6},{8,9},{9,8},{10,11... | collective-permute-start | bytes 245768 | tf_op jit(solution)/shard_map/ppermute | solution.py:256
  6.0 1.7 %copy-start.5 = (bf16[320,320]{1,0:T(8,128)(2,1)S(1)}, bf16[320,320]{1,0:T(8,128)(2,1)}, u32[]{:S(2)}) copy-start(bf16[320,320]{1,0:T(8,128)(2,1)} %zero_weight.1) | copy-start | bytes 614404
  6.0 1.7 %copy-start.11 = (f32[320]{0:T(512)S(1)}, f32[320]{0:T(512)}, u32[]{:S(2)}) copy-start(f32[320]{0:T(512)} %zero_bias.1) | copy-start | bytes 3844
  6.1 36.0 %copy-start.1 = (bf16[320,320]{1,0:T(8,128)(2,1)S(1)}, bf16[320,320]{1,0:T(8,128)(2,1)}, u32[]{:S(2)}) copy-start(bf16[320,320]{1,0:T(8,128)(2,1)} %proj_in.1) | copy-start | bytes 614404
  6.2 36.0 %copy-start.2 = (bf16[320,320]{1,0:T(8,128)(2,1)S(1)}, bf16[320,320]{1,0:T(8,128)(2,1)}, u32[]{:S(2)}) copy-start(bf16[320,320]{1,0:T(8,128)(2,1)} %wq.1) | copy-start | bytes 614404
  6.2 36.0 %copy-start.3 = (bf16[320,320]{1,0:T(8,128)(2,1)S(1)}, bf16[320,320]{1,0:T(8,128)(2,1)}, u32[]{:S(2)}) copy-start(bf16[320,320]{1,0:T(8,128)(2,1)} %wk.1) | copy-start | bytes 614404
  6.2 36.0 %copy-start.4 = (bf16[320,320]{1,0:T(8,128)(2,1)S(1)}, bf16[320,320]{1,0:T(8,128)(2,1)}, u32[]{:S(2)}) copy-start(bf16[320,320]{1,0:T(8,128)(2,1)} %wv.1) | copy-start | bytes 614404
  6.2 35.9 %copy-start.12 = (f32[320]{0:T(512)S(1)}, f32[320]{0:T(512)}, u32[]{:S(2)}) copy-start(f32[320]{0:T(512)} %group_gain.1) | copy-start | bytes 3844
  6.2 35.9 %copy-start.13 = (f32[320]{0:T(512)S(1)}, f32[320]{0:T(512)}, u32[]{:S(2)}) copy-start(f32[320]{0:T(512)} %norm_gain.1) | copy-start | bytes 3844
  61.6 12.9 %collective-permute-start.4 = (bf16[8,80,128]{2,1,0:T(8,128)(2,1)S(1)}, bf16[8,80,128]{2,1,0:T(8,128)(2,1)S(1)}, u32[]{:S(2)}, u32[]{:S(2)}) collective-permute-start(bf16[8,80,128]{2,1,0:T(8,128)(2,1)S(1)} %slice.9.refs_1_), channel_id=1, source_target_pairs={{0,16},{16,32},{32,48},{48,0},{1,17},{17,33},{33,49},{49,1},{2,18}... | collective-permute-start | bytes 491528 | tf_op jit(solution)/shard_map/ppermute | solution.py:291
  64.2 13.5 %collective-permute-start.3 = (bf16[8,80,128]{2,1,0:T(8,128)(2,1)S(1)}, bf16[8,80,128]{2,1,0:T(8,128)(2,1)S(1)}, u32[]{:S(2)}, u32[]{:S(2)}) collective-permute-start(bf16[8,80,128]{2,1,0:T(8,128)(2,1)S(1)} %slice.9.refs_1_), channel_id=1, source_target_pairs={{0,48},{16,0},{32,16},{48,32},{1,49},{17,1},{33,17},{49,33},{2,50}... | collective-permute-start | bytes 491528 | tf_op jit(solution)/shard_map/ppermute | solution.py:291
  68.6 10.9 %collective-permute-start.2 = (bf16[8,80,128]{2,1,0:T(8,128)(2,1)S(1)}, bf16[8,80,128]{2,1,0:T(8,128)(2,1)S(1)}, u32[]{:S(2)}, u32[]{:S(2)}) collective-permute-start(bf16[8,80,128]{2,1,0:T(8,128)(2,1)S(1)} %slice.9.refs_1_), channel_id=1, source_target_pairs={{0,32},{16,48},{32,0},{48,16},{1,33},{17,49},{33,1},{49,17},{2,34}... | collective-permute-start | bytes 491528 | tf_op jit(solution)/shard_map/ppermute | solution.py:291
  70.7 3.7 %collective-permute-start.5 = (bf16[8,40,128]{2,1,0:T(8,128)(2,1)S(1)}, bf16[8,40,128]{2,1,0:T(8,128)(2,1)S(1)}, u32[]{:S(2)}, u32[]{:S(2)}) collective-permute-start(bf16[8,40,128]{2,1,0:T(8,128)(2,1)S(1)} %slice.8.refs_0_), channel_id=1, source_target_pairs={{0,1},{1,0},{2,3},{3,2},{4,5},{5,4},{6,7},{7,6},{8,9},{9,8},{10,11... | collective-permute-start | bytes 245768 | tf_op jit(solution)/shard_map/ppermute | solution.py:292
  81.3 22.6 %copy-start.6 = (bf16[320,320]{1,0:T(8,128)(2,1)S(1)}, bf16[320,320]{1,0:T(8,128)(2,1)}, u32[]{:S(2)}) copy-start(bf16[320,320]{1,0:T(8,128)(2,1)} %attn_out.1) | copy-start | bytes 614404
  81.3 22.6 %copy-start.7 = (bf16[320,320]{1,0:T(8,128)(2,1)S(1)}, bf16[320,320]{1,0:T(8,128)(2,1)}, u32[]{:S(2)}) copy-start(bf16[320,320]{1,0:T(8,128)(2,1)} %proj_out.1) | copy-start | bytes 614404
  81.3 7.1 %collective-permute-start.6 = (f32[64,1024]{1,0:T(8,128)S(1)}, f32[64,1024]{1,0:T(8,128)S(1)}, u32[]{:S(2)}, u32[]{:S(2)}) collective-permute-start(f32[64,1024]{1,0:T(8,128)S(1)} %shard_map.144), channel_id=1, source_target_pairs={{0,1},{1,0},{2,3},{3,2},{4,5},{5,4},{6,7},{7,6},{8,9},{9,8},{10,11... | collective-permute-start | bytes 786440 | tf_op jit(solution)/shard_map/ppermute | solution.py:297
